TPU v7x, 128 devices: a whole 4x4x4 slice. The times are simulated.
128 devices in a mesh: pts: 128 (over z, y, x, core).
Axes of the slice: x: 4, y: 4, z: 4, core: 2. Of those that a mesh axis runs over, the one named last changes fastest.
Arguments:
- feats: bfloat16 [3670016, 128], P('pts'), may hold values from -6 to 6
- w_first: bfloat16 [128, 128], replicated, may hold values from -0.5 to 0.5
- w_second: bfloat16 [128, 128], replicated, may hold values from -0.5 to 0.5
- w_coarse: bfloat16 [128, 128], replicated, may hold values from -0.5 to 0.5
- send_weight: bfloat16 [14336, 16, 256], P('pts'), may hold values from -1 to 1
- return_weight: bfloat16 [14336, 16, 256], P('pts'), may hold values from -2 to 2
- neighbours: int32 [14336, 16], P('pts'), may hold values from 0 to 5119, as said below
- nbr_count: int32 [14336], P('pts'), may hold values from 1 to 16, as said below
- point_count: int32 [14336], P('pts'), may hold values from 64 to 256, as said below
- cotangent: bfloat16 [3670016, 128], P('pts'), may hold values from -6 to 6
Outputs:
- grad_feats: bfloat16 [3670016, 128], P('pts')
- grad_first: float32 [128, 128], replicated
- grad_second: float32 [128, 128], replicated
- grad_coarse: float32 [128, 128], replicated
Inputs may be any that keep to these rules, and one draw needn't show every extreme that they name: `neighbours`: every neighbour slot of a block of device d (blocks d * 112 to (d + 1) * 112 - 1) names an atom owned by device d - 1, d or d + 1, where device e owns atoms e * 40 to (e + 1) * 40 - 1; unused slots follow the same rule. `nbr_count`: the first block of every device uses all slots. `point_count`: the first block of every device uses all slots.
All inputs are finite; a program needn't handle non-finite values.
Results may differ from a plain program's by a relative error of at most 0.022.
Values may be sent and summed in bfloat16 or wider, within the bound.
No kernel may reach another device: no remote copies, remote signals or barrier semaphores. Data moves between devices by JAX's collectives and lax.ppermute only.
A program may use at most 192 MiB of HBM per device.

v0:
```python
import math

import jax
import jax.numpy as jnp
from jax import lax
from jax.sharding import PartitionSpec as P

A_DEV = 40


def padded(block, sides, width):
    for axis, dim in sides:
        count = lax.axis_size(axis)
        forward = [(i, i + 1) for i in range(count - 1)]
        backward = [(target, source) for source, target in forward]
        low = lax.ppermute(
            lax.slice_in_dim(block, block.shape[dim] - width, None, axis=dim), axis, forward
        )
        high = lax.ppermute(lax.slice_in_dim(block, 0, width, axis=dim), axis, backward)
        block = jnp.concatenate([low, block, high], axis=dim)
    return block


def silu_slope(value):
    sig = jax.nn.sigmoid(value)
    return sig * (1.0 + value * (1.0 - sig))


def coarse_layer(coarse, coarse_grad, w_coarse):
    pre_coarse = jnp.dot(coarse, w_coarse, preferred_element_type=jnp.float32)
    dpre_coarse = (coarse_grad * silu_slope(pre_coarse)).astype(jnp.bfloat16)
    dcoarse = jnp.dot(dpre_coarse, w_coarse.T, preferred_element_type=jnp.float32).astype(
        jnp.bfloat16
    )
    return (dpre_coarse, dcoarse)


def body(
    feats,
    w_first,
    w_second,
    w_coarse,
    send_weight,
    return_weight,
    neighbours,
    nbr_count,
    point_count,
    cotangent,
):
    num_blocks, num_slots, block_len = send_weight.shape
    width = feats.shape[1]
    owned = A_DEV
    device = lax.axis_index("pts")
    devices = lax.axis_size("pts")
    valid = (jnp.arange(num_slots, dtype=jnp.int32)[None, :] < nbr_count[:, None]).astype(
        jnp.float32
    )
    marks = (
        (jnp.arange(block_len, dtype=jnp.int32)[None, :] < point_count[:, None])
        .astype(jnp.float32)
        .reshape(-1, 1)
    )
    pre1 = jnp.dot(feats, w_first, preferred_element_type=jnp.float32)
    first = jax.nn.silu(pre1).astype(jnp.bfloat16)
    pre2 = jnp.dot(first, w_second, preferred_element_type=jnp.float32)
    point_feat = (
        (marks * jax.nn.silu(pre2)).astype(jnp.bfloat16).reshape(num_blocks, block_len, width)
    )
    message = (
        jnp.einsum("bkp,bpc->bkc", send_weight, point_feat, preferred_element_type=jnp.float32)
        * valid[..., None]
    ).astype(jnp.bfloat16)
    masked = (cotangent.astype(jnp.float32) * marks).astype(jnp.bfloat16)
    back_grad = (
        jnp.einsum(
            "bkp,bpc->bkc",
            return_weight,
            masked.reshape(num_blocks, block_len, width),
            preferred_element_type=jnp.float32,
        )
        * valid[..., None]
    ).astype(jnp.bfloat16)
    relative = neighbours.reshape(1, -1) - (device - 1) * owned
    selector = (
        (jnp.arange(3 * owned, dtype=jnp.int32)[:, None] == relative) & (valid.reshape(1, -1) > 0)
    ).astype(jnp.bfloat16)
    part_msg = jnp.dot(selector, message.reshape(-1, width), preferred_element_type=jnp.float32)
    part_grad = jnp.dot(selector, back_grad.reshape(-1, width), preferred_element_type=jnp.float32)
    partial_value = jnp.stack([part_msg, part_grad])
    ends = jnp.concatenate([partial_value[:, :owned], partial_value[:, 2 * owned :]], axis=1)
    rims = padded(ends, (("pts", 1),), owned)
    own_sums = partial_value[:, owned : 2 * owned] + rims[:, :owned] + rims[:, 3 * owned :]
    coarse = own_sums[0].astype(jnp.bfloat16)
    dpre_coarse, dcoarse = coarse_layer(coarse, own_sums[1], w_coarse)
    grad_coarse = jnp.dot(coarse.T, dpre_coarse, preferred_element_type=jnp.float32)
    window = padded(dcoarse, (("pts", 0),), owned)
    message_grad = lax.dot_general(
        selector, window, (((0,), (0,)), ((), ())), preferred_element_type=jnp.float32
    ).astype(jnp.bfloat16)
    spread = jnp.einsum(
        "bkp,bkc->bpc",
        send_weight,
        message_grad.reshape(num_blocks, num_slots, width),
        preferred_element_type=jnp.float32,
    ).reshape(-1, width)
    point_grad = masked.astype(jnp.float32) + spread
    dpre2 = (marks * point_grad * silu_slope(pre2)).astype(jnp.bfloat16)
    grad_two = jnp.dot(first.T, dpre2, preferred_element_type=jnp.float32)
    dfirst = jnp.dot(dpre2, w_second.T, preferred_element_type=jnp.float32)
    dpre1 = (dfirst * silu_slope(pre1)).astype(jnp.bfloat16)
    grad_one = jnp.dot(feats.T, dpre1, preferred_element_type=jnp.float32)
    grad_feats = jnp.dot(dpre1, w_first.T, preferred_element_type=jnp.float32).astype(jnp.bfloat16)
    total_one, total_two, total_coarse = lax.psum((grad_one, grad_two, grad_coarse), "pts")
    total_points = devices * num_blocks * block_len
    total_atoms = devices * owned
    factor = 1.0 / math.sqrt(total_points)
    return (
        grad_feats,
        total_one * factor,
        total_two * factor,
        total_coarse * (1.0 / math.sqrt(total_atoms)),
    )


def solution(mesh):
    placed = (
        P("pts", None),
        P(),
        P(),
        P(),
        P("pts", None, None),
        P("pts", None, None),
        P("pts", None),
        P("pts"),
        P("pts"),
        P("pts", None),
    )
    return jax.shard_map(
        body, mesh=mesh, in_specs=placed, out_specs=(P("pts", None), P(), P(), P()), check_vma=False
    )
```

profile of v0, /device:TPU:1, one launch (start us, length us, event | category | flops | bytes accessed | tf_op | source)
XLA Modules:
  0.0 280.9 jit_solution(11165709871867237578)
XLA Ops:
  7.2 0.8 broadcast_subtract_fusion
  8.0 0.1 copy.18
  8.2 0.7 fusion.16
  9.0 0.7 convert_bitcast_fusion
  9.9 9.2 %multiply_convert_fusion.1 = (bf16[28672,128]{1,0:T(8,128)(2,1)S(1)}, f32[28672,128]{1,0:T(8,128)}) fusion(bf16[28672,128]{1,0:T(8,128)(2,1)} %param.10, bf16[128,128]{1,0:T(8,128)(2,1)} %param.11), kind=kOutput, calls=%fused_computation.9 | convolution fusion | flops 957874176 | bytes 29392896 | tf_op jit(solution)/shard_map/dot_general | solution.py:63
  19.1 15.8 %multiply_convert_fusion = (bf16[28672,128]{1,0:T(8,128)(2,1)S(1)}, bf16[28672,128]{1,0:T(8,128)(2,1)S(1)}, f32[28672,128]{1,0:T(8,128)}) fusion(f32[28672]{0:T(1024)S(1)} %bitcast.66, bf16[28672,128]{1,0:T(8,128)(2,1)} %param.19, bf16[28672,128]{1,0:T(8,128)(2,1)S(1)} %get-tuple-element.21, bf16[128,128]{1,0:T(8,128)(2,1)S(1)} %copy-done.7), kind=kOutput, calls=%fused_computation.7 | convolution fusion | flops 972554240 | bytes 44187648 | tf_op jit(solution)/shard_map/dot_general | solution.py:65
  34.9 1.1 fusion.4
  36.0 1.1 fusion.5
  37.0 0.3 convolution_bitcast_fusion.3
  37.3 0.3 convolution_bitcast_fusion.2
  37.6 3.3 %collective-permute-start.1 = (f32[2,40,128]{2,1,0:T(8,128)S(1)}, f32[2,40,128]{2,1,0:T(8,128)S(1)}, u32[]{:S(2)}, u32[]{:S(2)}) collective-permute-start(f32[2,40,128]{2,1,0:T(8,128)S(1)} %get-tuple-element.16), channel_id=1, source_target_pairs={{1,0},{2,1},{3,2},{4,3},{5,4},{6,5},{7,6},{8,7},{9,8},{10,9},{11,1... | collective-permute-start | bytes 122888 | tf_op jit(solution)/shard_map/ppermute | solution.py:19
  41.0 3.1 %collective-permute-start = (f32[2,40,128]{2,1,0:T(8,128)S(1)}, f32[2,40,128]{2,1,0:T(8,128)S(1)}, u32[]{:S(2)}, u32[]{:S(2)}) collective-permute-start(f32[2,40,128]{2,1,0:T(8,128)S(1)} %get-tuple-element.15), channel_id=1, source_target_pairs={{0,1},{1,2},{2,3},{3,4},{4,5},{5,6},{6,7},{7,8},{8,9},{9,10},{10,1... | collective-permute-start | bytes 122888 | tf_op jit(solution)/shard_map/ppermute | solution.py:16
  44.1 1.1 collective-permute-done
  45.2 0.2 fusion.27
  45.4 0.1 convolution_convert_fusion.2
  45.5 1.9 collective-permute-start.3
  47.4 4.2 %collective-permute-start.2 = (bf16[40,128]{1,0:T(8,128)(2,1)S(1)}, bf16[40,128]{1,0:T(8,128)(2,1)S(1)}, u32[]{:S(2)}, u32[]{:S(2)}) collective-permute-start(bf16[40,128]{1,0:T(8,128)(2,1)S(1)} %convolution_convert_fusion.2), channel_id=1, source_target_pairs={{0,1},{1,2},{2,3},{3,4},{4,5},{5,6},{6,7},{7,8},{8,9},{9,10},{10,1... | collective-permute-start | bytes 30728 | tf_op jit(solution)/shard_map/ppermute | solution.py:16
  51.7 0.8 fusion.29
  52.5 0.4 convolution_convert_fusion.1
  52.9 7.2 %convolution_bitcast_fusion = f32[112,256,128]{1,2,0:T(8,128)} fusion(bf16[112,16,128]{2,1,0:T(8,128)(2,1)S(1)} %bitcast.68, bf16[112,16,256]{2,1,0:T(8,128)(2,1)S(1)} %copy-done), kind=kOutput, calls=%fused_computation.12 | convolution fusion | flops 117440512 | bytes 16056320 | tf_op jit(solution)/shard_map/bkp,bkc->bpc/dot_general | solution.py:100
  60.2 15.1 %copy.19 = f32[112,256,128]{2,1,0:T(8,128)} copy(f32[112,256,128]{1,2,0:T(8,128)} %convolution_bitcast_fusion) | data formatting | bytes 29360128 | tf_op jit(solution)/shard_map/bkp,bkc->bpc/dot_general | solution.py:100
  75.2 17.1 %fusion.3 = bf16[28672,128]{1,0:T(8,128)(2,1)S(1)} fusion(f32[112,256,128]{2,1,0:T(8,128)} %copy.19, f32[28672,128]{1,0:T(8,128)} %get-tuple-element.23, f32[28672]{0:T(1024)S(1)} %bitcast.67, bf16[28672,128]{1,0:T(8,128)(2,1)} %param.19), kind=kLoop, calls=%fused_computation.6 | loop fusion | flops 55050240 | bytes 44154880 | tf_op jit(solution)/shard_map/convert_element_type | solution.py:107
  92.3 6.1 %fusion.36 = f32[128,128]{0,1:T(8,128)} fusion(bf16[28672,128]{1,0:T(8,128)(2,1)} %copy-done.3, bf16[28672,128]{1,0:T(8,128)(2,1)S(1)} %fusion.3), kind=kOutput, calls=%fused_computation.61 | convolution fusion | flops 939524096 | bytes 14745600 | tf_op jit(solution)/shard_map/dot_general | solution.py:108
  98.4 8.9 %fusion = bf16[28672,128]{1,0:T(8,128)(2,1)S(1)} fusion(bf16[28672,128]{1,0:T(8,128)(2,1)S(1)} %fusion.3, bf16[128,128]{1,0:T(8,128)(2,1)S(1)} %copy-done.7, f32[28672,128]{1,0:T(8,128)} %get-tuple-element.22), kind=kOutput, calls=%fused_computation.2 | convolution fusion | flops 972554240 | bytes 29392896 | tf_op jit(solution)/shard_map/dot_general | solution.py:109
  107.3 2.9 %copy-done.2 = bf16[28672,128]{1,0:T(8,128)(2,1)} copy-done((bf16[28672,128]{1,0:T(8,128)(2,1)}, bf16[28672,128]{1,0:T(8,128)(2,1)S(1)}, u32[]{:S(2)}) %copy-start.2) | copy-done | bytes 7340056
  110.3 6.0 %convolution_bitcast_fusion.1 = f32[128,128]{0,1:T(8,128)} fusion(bf16[28672,128]{1,0:T(8,128)(2,1)S(1)} %fusion, bf16[28672,128]{1,0:T(8,128)(2,1)} %param.10), kind=kOutput, calls=%fused_computation.18 | convolution fusion | flops 939524096 | bytes 14745600 | tf_op jit(solution)/shard_map/dot_general | solution.py:111
  116.2 8.2 %convolution_convert_fusion = bf16[28672,128]{1,0:T(8,128)(2,1)} fusion(bf16[28672,128]{1,0:T(8,128)(2,1)} %copy-done.2, bf16[128,128]{1,0:T(8,128)(2,1)S(1)} %copy-done.5), kind=kOutput, calls=%fused_computation | convolution fusion | flops 943194112 | bytes 14712832 | tf_op jit(solution)/shard_map/dot_general | solution.py:112
  124.5 145.8 %all-reduce.3.cloned.1.call-done = (f32[128,128]{0,1:T(8,128)}, f32[128,128]{0,1:T(8,128)}, f32[128,128]{1,0:T(8,128)}) async-done(((f32[128,128]{0,1:T(8,128)}, f32[128,128]{0,1:T(8,128)}, f32[128,128]{1,0:T(8,128)}), (f32[128,128]{0,1:T(8,128)}, f32[128,128]{0,1:T(8,128)}, f32[128,128]{1,0:T(8,128)})) %all-reduce.3.cloned.1.call-update) | async-done | bytes 196624 | tf_op jit(solution)/shard_map/psum | solution.py:113
  270.3 0.9 broadcast_multiply_fusion.1
  271.2 0.7 copy.21
  271.9 0.7 copy.22
  272.6 1.5 broadcast_multiply_fusion
  (25 shorter events, 0.4 us)
Async XLA Ops:
  7.2 27.7 %copy-start = (bf16[112,16,256]{2,1,0:T(8,128)(2,1)S(1)}, bf16[112,16,256]{2,1,0:T(8,128)(2,1)}, u32[]{:S(2)}) copy-start(bf16[112,16,256]{2,1,0:T(8,128)(2,1)} %param.14) | copy-start | bytes 2752516
  7.2 263.1 %all-reduce.3.cloned.1.call-start = ((), (), s32[]{:S(2)}) async-start(), calls=%async_computation | async-start | bytes 393216 | tf_op jit(solution)/shard_map/psum | solution.py:113
  9.8 9.2 %copy-start.7 = (bf16[128,128]{1,0:T(8,128)(2,1)S(1)}, bf16[128,128]{1,0:T(8,128)(2,1)}, u32[]{:S(2)}) copy-start(bf16[128,128]{1,0:T(8,128)(2,1)} %param.12) | copy-start | bytes 98308
  19.1 15.8 %copy-start.3 = (bf16[28672,128]{1,0:T(8,128)(2,1)}, bf16[28672,128]{1,0:T(8,128)(2,1)S(1)}, u32[]{:S(2)}) copy-start(bf16[28672,128]{1,0:T(8,128)(2,1)S(1)} %get-tuple-element.21) | copy-start | bytes 22020100
  19.1 16.9 %copy-start.4 = (bf16[112,16,256]{2,1,0:T(8,128)(2,1)S(1)}, bf16[112,16,256]{2,1,0:T(8,128)(2,1)}, u32[]{:S(2)}) copy-start(bf16[112,16,256]{2,1,0:T(8,128)(2,1)} %param.15) | copy-start | bytes 2752516
  34.9 10.3 %copy-start.6 = (bf16[128,128]{1,0:T(8,128)(2,1)S(1)}, bf16[128,128]{1,0:T(8,128)(2,1)}, u32[]{:S(2)}) copy-start(bf16[128,128]{1,0:T(8,128)(2,1)} %param.13) | copy-start | bytes 98308
  37.6 6.4 %collective-permute-start.1 = (f32[2,40,128]{2,1,0:T(8,128)S(1)}, f32[2,40,128]{2,1,0:T(8,128)S(1)}, u32[]{:S(2)}, u32[]{:S(2)}) collective-permute-start(f32[2,40,128]{2,1,0:T(8,128)S(1)} %get-tuple-element.16), channel_id=1, source_target_pairs={{1,0},{2,1},{3,2},{4,3},{5,4},{6,5},{7,6},{8,7},{9,8},{10,9},{11,1... | collective-permute-start | bytes 122888 | tf_op jit(solution)/shard_map/ppermute | solution.py:19
  41.0 4.2 %collective-permute-start = (f32[2,40,128]{2,1,0:T(8,128)S(1)}, f32[2,40,128]{2,1,0:T(8,128)S(1)}, u32[]{:S(2)}, u32[]{:S(2)}) collective-permute-start(f32[2,40,128]{2,1,0:T(8,128)S(1)} %get-tuple-element.15), channel_id=1, source_target_pairs={{0,1},{1,2},{2,3},{3,4},{4,5},{5,6},{6,7},{7,8},{8,9},{9,10},{10,1... | collective-permute-start | bytes 122888 | tf_op jit(solution)/shard_map/ppermute | solution.py:16
  45.5 7.0 %collective-permute-start.3 = (bf16[40,128]{1,0:T(8,128)(2,1)S(1)}, bf16[40,128]{1,0:T(8,128)(2,1)S(1)}, u32[]{:S(2)}, u32[]{:S(2)}) collective-permute-start(bf16[40,128]{1,0:T(8,128)(2,1)S(1)} %convolution_convert_fusion.2), channel_id=1, source_target_pairs={{1,0},{2,1},{3,2},{4,3},{5,4},{6,5},{7,6},{8,7},{9,8},{10,9},{11,1... | collective-permute-start | bytes 30728 | tf_op jit(solution)/shard_map/ppermute | solution.py:19
  47.4 5.1 %collective-permute-start.2 = (bf16[40,128]{1,0:T(8,128)(2,1)S(1)}, bf16[40,128]{1,0:T(8,128)(2,1)S(1)}, u32[]{:S(2)}, u32[]{:S(2)}) collective-permute-start(bf16[40,128]{1,0:T(8,128)(2,1)S(1)} %convolution_convert_fusion.2), channel_id=1, source_target_pairs={{0,1},{1,2},{2,3},{3,4},{4,5},{5,6},{6,7},{7,8},{8,9},{9,10},{10,1... | collective-permute-start | bytes 30728 | tf_op jit(solution)/shard_map/ppermute | solution.py:16
  98.4 175.7 %copy-start.1 = (bf16[112,16,256]{2,1,0:T(8,128)(2,1)S(1)}, bf16[112,16,256]{2,1,0:T(8,128)(2,1)}, u32[]{:S(2)}) copy-start(bf16[112,16,256]{2,1,0:T(8,128)(2,1)} %param.14) | copy-start | bytes 2752516
  107.3 2.9 %copy-start.2 = (bf16[28672,128]{1,0:T(8,128)(2,1)}, bf16[28672,128]{1,0:T(8,128)(2,1)S(1)}, u32[]{:S(2)}) copy-start(bf16[28672,128]{1,0:T(8,128)(2,1)S(1)} %fusion) | copy-start | bytes 22020100
  110.3 6.0 %copy-start.5 = (bf16[128,128]{1,0:T(8,128)(2,1)S(1)}, bf16[128,128]{1,0:T(8,128)(2,1)}, u32[]{:S(2)}) copy-start(bf16[128,128]{1,0:T(8,128)(2,1)} %param.11) | copy-start | bytes 98308
Sparse Core Ops, SparseCore 0:
  116.4 153.8 all-reduce.2
where the time goes:
time: 282 us; the launch traced here: 281 us
  waiting for transfers between devices  147 us (52%)
  matrix products  65.6 us (23%)
  other arithmetic  21.7 us (8%)
  local copies, waits for them, and re-layouts  19.8 us (7%)
  between operations  14.2 us (5%)
  starting transfers between devices  12.6 us (4%)
    psum x1, waiting for transfers between devices, body(): lax.psum((grad_one, grad_two, grad_coarse), 'pts')  146 us
    convert_element_type x1, other arithmetic, body(): dpre2 = (marks * point_grad * silu_slope(pre2)).astype(jnp.bfloat16)  17.1 us
    dot_general x1, matrix products, body(): pre2 = jnp.dot(first, w_second, preferred_element_type=jnp.float32)  15.8 us
    dot_general x1, local copies, waits for them, and re-layouts, body(): jnp.einsum('bkp,bkc->bpc', send_weight, message_grad.reshape(num_blocks,...  15.1 us
    dot_general x1, matrix products, body(): pre1 = jnp.dot(feats, w_first, preferred_element_type=jnp.float32)  9.22 us
    dot_general x1, matrix products, body(): dfirst = jnp.dot(dpre2, w_second.T, preferred_element_type=jnp.float32)  8.92 us
    dot_general x1, matrix products, body(): jnp.dot(dpre1, w_first.T, preferred_element_type=jnp.float32)  8.2 us
    ppermute x2, starting transfers between devices, padded(): lax.ppermute(lax.slice_in_dim(block, block.shape[dim] - width, None, axis...  7.33 us
  transfers between devices with their start and end apart: 5, of which 2 were waited for; matrix products, arithmetic and copies ran while one was open for 3% of the time, Pallas kernels for 0%

commit v1 on v0

v1 whole, which is shorter than its diff:
```python
import math

import jax
import jax.numpy as jnp
from jax import lax
from jax.experimental import pallas as pl
from jax.experimental.pallas import tpu as pltpu
from jax.sharding import PartitionSpec as P

A_DEV = 40
A_PAD = 48
TILE = 8
HALF = TILE // 2

BF16 = jnp.bfloat16
F32 = jnp.float32


def dot(left, right):
    return jnp.dot(left, right, preferred_element_type=F32)


def dot_rows(left, right):
    return lax.dot_general(left, right, (((0,), (0,)), ((), ())), preferred_element_type=F32)


def diag_pair(weight):
    zero = jnp.zeros_like(weight)
    return jnp.concatenate(
        [jnp.concatenate([weight, zero], axis=1), jnp.concatenate([zero, weight], axis=1)], axis=0
    )


def silu_pair(half):
    up = 1.0 + jnp.tanh(half)
    value = half * up
    return value, up + value * (2.0 - up)


def select_slots(nb_ref):
    rows = lax.broadcasted_iota(jnp.int32, (3 * A_PAD, nb_ref.shape[-1]), 0)
    return jnp.where(rows == nb_ref[0], 1.0, 0.0).astype(BF16)


def outgoing_kernel(
    count_ref,
    nb_ref,
    feats_ref,
    cot_ref,
    send_ref,
    ret_ref,
    w_first_ref,
    w_second_ref,
    first_ref,
    slope1_ref,
    slope2_ref,
    to_right_ref,
    to_left_ref,
    edge_right_ref,
    edge_left_ref,
    w1_ref,
    w2_ref,
    spot_ref,
    part_ref,
):
    step = pl.program_id(0)
    block_len = send_ref.shape[1]
    slots = send_ref.shape[0] // TILE
    width = feats_ref.shape[1]

    @pl.when(step == 0)
    def _():
        w1_ref[...] = diag_pair(w_first_ref[...] * 0.5)
        w2_ref[...] = diag_pair(w_second_ref[...] * 0.5)
        spot_ref[...] = lax.broadcasted_iota(jnp.int32, spot_ref.shape, 0).astype(F32).astype(BF16)
        part_ref[...] = jnp.zeros_like(part_ref)

    lanes = lax.broadcasted_iota(jnp.int32, (slots, block_len), 1)
    lo_msg, hi_msg, lo_back, hi_back = [], [], [], []
    for pair in range(HALF):
        rows = pl.ds(pair * block_len, block_len)
        far = pl.ds((pair + HALF) * block_len, block_len)
        out = pl.ds(pl.multiple_of((step * HALF + pair) * block_len, block_len), block_len)
        counts = [count_ref[step * TILE + pair], count_ref[step * TILE + pair + HALF]]
        x = jnp.concatenate([feats_ref[rows, :], feats_ref[far, :]], axis=1)
        half1 = dot(x, w1_ref[...]).astype(BF16)
        first, slope1 = silu_pair(half1)
        first_ref[out, :] = first
        slope1_ref[out, :] = slope1
        half2 = dot(first, w2_ref[...]).astype(BF16)
        point, slope2 = silu_pair(half2)
        mask = jnp.concatenate(
            [
                jnp.clip(jnp.full((block_len, width), c.astype(F32)).astype(BF16) - spot_ref[...], 0, 1)
                for c in counts
            ],
            axis=1,
        )
        slope2_ref[out, :] = slope2 * mask

        def weights(ref):
            return jnp.concatenate(
                [
                    jnp.where(lanes < c, ref[pl.ds(b * slots, slots), :].astype(F32), 0.0).astype(BF16)
                    for b, c in zip((pair, pair + HALF), counts)
                ],
                axis=0,
            )

        cot = jnp.concatenate([cot_ref[rows, :], cot_ref[far, :]], axis=1)
        msg = dot(weights(send_ref), point)
        back = dot(weights(ret_ref), cot)
        lo_msg.append(msg[:slots, :width])
        hi_msg.append(msg[slots:, width:])
        lo_back.append(back[:slots, :width])
        hi_back.append(back[slots:, width:])
    both = jnp.concatenate(
        [jnp.concatenate(lo_msg + hi_msg, axis=0), jnp.concatenate(lo_back + hi_back, axis=0)], axis=1
    ).astype(BF16)
    part_ref[...] += dot(select_slots(nb_ref), both)

    @pl.when(step == pl.num_programs(0) - 1)
    def _():
        part = part_ref[...].astype(BF16)
        to_right_ref[...] = part[A_PAD:]
        to_left_ref[...] = part[: 2 * A_PAD]
        edge_right_ref[...] = part[2 * A_PAD :]
        edge_left_ref[...] = part[:A_PAD]


def outgoing(counts, relative, feats, cot, send, ret, w_first, w_second):
    points, width = feats.shape
    block_len = send.shape[1]
    slots = send.shape[0] // (points // block_len)
    steps = points // (TILE * block_len)
    rows = TILE * block_len
    packed = (points // 2, 2 * width)

    def whole(shape):
        return pl.BlockSpec(shape, lambda i, c: (0,) * len(shape))

    def tiled(*shape):
        return pl.BlockSpec(shape, lambda i, c: (i,) + (0,) * (len(shape) - 1))

    window = jax.ShapeDtypeStruct((2 * A_PAD, 2 * width), BF16)
    edge = jax.ShapeDtypeStruct((A_PAD, 2 * width), BF16)
    resident = pl.BlockSpec(memory_space=pltpu.VMEM)
    return pl.pallas_call(
        outgoing_kernel,
        grid_spec=pltpu.PrefetchScalarGridSpec(
            num_scalar_prefetch=1,
            grid=(steps,),
            in_specs=[
                tiled(1, 1, TILE * slots),
                tiled(rows, width),
                tiled(rows, width),
                tiled(TILE * slots, block_len),
                tiled(TILE * slots, block_len),
                whole((width, width)),
                whole((width, width)),
            ],
            out_specs=[resident] * 3
            + [whole((2 * A_PAD, 2 * width))] * 2
            + [whole((A_PAD, 2 * width))] * 2,
            scratch_shapes=[
                pltpu.VMEM((2 * width, 2 * width), BF16),
                pltpu.VMEM((2 * width, 2 * width), BF16),
                pltpu.VMEM((block_len, width), BF16),
                pltpu.VMEM((3 * A_PAD, 2 * width), F32),
            ],
        ),
        out_shape=[pltpu.VMEM(packed, BF16)] * 3 + [window] * 2 + [edge] * 2,
        compiler_params=pltpu.CompilerParams(vmem_limit_bytes=24 * 2**20),
        name="outgoing",
    )(counts, relative, feats, cot, send, ret, w_first, w_second)


def incoming_kernel(
    nb_ref,
    feats_ref,
    cot_ref,
    send_ref,
    w_first_ref,
    w_second_ref,
    w_coarse_ref,
    own_right_ref,
    own_left_ref,
    near_low_ref,
    near_high_ref,
    far_low_ref,
    far_high_ref,
    first_ref,
    slope1_ref,
    slope2_ref,
    grad_feats_ref,
    grads_ref,
    w1_ref,
    w2_ref,
    dcoarse_ref,
    acc1_ref,
    acc2_ref,
):
    step = pl.program_id(0)
    block_len = send_ref.shape[1]
    slots = send_ref.shape[0] // TILE
    width = feats_ref.shape[1]

    @pl.when(step == 0)
    def _():
        w1_ref[...] = diag_pair(w_first_ref[...].T * 0.5)
        w2_ref[...] = diag_pair(w_second_ref[...].T * 0.5)
        acc1_ref[...] = jnp.zeros_like(acc1_ref)
        acc2_ref[...] = jnp.zeros_like(acc2_ref)

        def load(ref, place):
            return ref[pl.ds(place * A_PAD, A_PAD), :].astype(F32)

        total = jnp.concatenate(
            [
                load(own_left_ref, 0) + load(near_low_ref, 0) + load(far_low_ref, 0),
                load(own_left_ref, 1) + load(near_low_ref, 1) + load(near_high_ref, 0),
                load(own_right_ref, 1) + load(near_high_ref, 1) + load(far_high_ref, 0),
            ],
            axis=0,
        )
        coarse = total[:, :width].astype(BF16)
        pre = dot(coarse, w_coarse_ref[...])
        sig = jax.nn.sigmoid(pre)
        slope = sig * (1.0 + pre * (1.0 - sig))
        dpre = (total[:, width:] * slope).astype(BF16)
        dcoarse_ref[...] = dot(dpre, w_coarse_ref[...].T).astype(BF16)
        grads_ref[2 * width :, :] = dot_rows(
            coarse[A_PAD : 2 * A_PAD], dpre[A_PAD : 2 * A_PAD]
        ).astype(BF16)

    send_t = send_ref[...].T
    spread_in = dot_rows(select_slots(nb_ref), dcoarse_ref[...]).astype(BF16)
    owner = lax.broadcasted_iota(jnp.int32, spread_in.shape, 0) // slots
    acc1 = jnp.zeros(acc1_ref.shape, F32)
    acc2 = jnp.zeros(acc2_ref.shape, F32)
    for pair in range(HALF):
        rows = pl.ds(pair * block_len, block_len)
        far = pl.ds((pair + HALF) * block_len, block_len)
        place = pl.ds(pl.multiple_of((step * HALF + pair) * block_len, block_len), block_len)
        share = jnp.concatenate(
            [
                jnp.where(owner == b, spread_in.astype(F32), 0.0).astype(BF16)
                for b in (pair, pair + HALF)
            ],
            axis=1,
        )
        spread = dot(send_t, share).astype(BF16)
        cot = jnp.concatenate([cot_ref[rows, :], cot_ref[far, :]], axis=1)
        dpre2 = (cot + spread) * slope2_ref[place, :]
        acc2 += dot_rows(first_ref[place, :], dpre2)
        dfirst = dot(dpre2, w2_ref[...]).astype(BF16)
        dpre1 = dfirst * slope1_ref[place, :]
        x = jnp.concatenate([feats_ref[rows, :], feats_ref[far, :]], axis=1)
        acc1 += dot_rows(x, dpre1)
        grad = dot(dpre1, w1_ref[...]).astype(BF16)
        grad_feats_ref[rows, :] = grad[:, :width]
        grad_feats_ref[far, :] = grad[:, width:]
    acc1_ref[...] += acc1
    acc2_ref[...] += acc2

    @pl.when(step == pl.num_programs(0) - 1)
    def _():
        for place, ref in enumerate((acc1_ref, acc2_ref)):
            grads_ref[pl.ds(place * width, width), :] = (
                ref[:width, :width] + ref[width:, width:]
            ).astype(BF16)


def incoming(relative, feats, cot, send, w_first, w_second, w_coarse, windows, kept):
    points, width = feats.shape
    block_len = send.shape[1]
    slots = send.shape[0] // (points // block_len)
    steps = points // (TILE * block_len)
    rows = TILE * block_len

    def whole(shape):
        return pl.BlockSpec(shape, lambda i: (0,) * len(shape))

    def tiled(*shape):
        return pl.BlockSpec(shape, lambda i: (i,) + (0,) * (len(shape) - 1))

    resident = pl.BlockSpec(memory_space=pltpu.VMEM)
    kept = [pltpu.with_memory_space_constraint(k, pltpu.VMEM) for k in kept]
    return pl.pallas_call(
        incoming_kernel,
        grid=(steps,),
        in_specs=[
            tiled(1, 1, TILE * slots),
            tiled(rows, width),
            tiled(rows, width),
            tiled(TILE * slots, block_len),
        ]
        + [whole((width, width))] * 3
        + [whole(w.shape) for w in windows]
        + [resident] * 3,
        out_specs=[tiled(rows, width), whole((3 * width, width))],
        out_shape=[
            jax.ShapeDtypeStruct((points, width), BF16),
            jax.ShapeDtypeStruct((3 * width, width), BF16),
        ],
        scratch_shapes=[
            pltpu.VMEM((2 * width, 2 * width), BF16),
            pltpu.VMEM((2 * width, 2 * width), BF16),
            pltpu.VMEM((3 * A_PAD, width), BF16),
            pltpu.VMEM((2 * width, 2 * width), F32),
            pltpu.VMEM((2 * width, 2 * width), F32),
        ],
        compiler_params=pltpu.CompilerParams(vmem_limit_bytes=24 * 2**20),
        name="incoming",
    )(relative, feats, cot, send, w_first, w_second, w_coarse, *windows, *kept)


def shifted(value, by):
    count = lax.axis_size("pts")
    pairs = [(i, i + by) for i in range(count) if 0 <= i + by < count]
    return lax.ppermute(value, "pts", pairs)


def total(value):
    count = lax.axis_size("pts")
    flips = [1]
    bit = 1
    while 2 << bit <= count:
        flips += [1 << bit, 3 << bit]
        bit += 2
    for flip in flips:
        other = lax.ppermute(value, "pts", [(i, i ^ flip) for i in range(count)])
        value = (value.astype(F32) + other.astype(F32)).astype(BF16)
    return value


def body(
    feats,
    w_first,
    w_second,
    w_coarse,
    send_weight,
    return_weight,
    neighbours,
    nbr_count,
    point_count,
    cotangent,
):
    num_blocks, num_slots, block_len = send_weight.shape
    width = feats.shape[1]
    device = lax.axis_index("pts")
    devices = lax.axis_size("pts")
    used = jnp.arange(num_slots, dtype=jnp.int32)[None, :] < nbr_count[:, None]
    relative = neighbours - (device - 1) * A_DEV
    relative = jnp.where(used, relative + (A_PAD - A_DEV) * (relative // A_DEV), -1)
    relative = relative.reshape(num_blocks // TILE, 1, TILE * num_slots)
    send = send_weight.reshape(num_blocks * num_slots, block_len)
    ret = return_weight.reshape(num_blocks * num_slots, block_len)
    *kept, to_right, to_left, edge_right, edge_left = outgoing(
        point_count, relative, feats, cotangent, send, ret, w_first, w_second
    )
    windows = (
        to_right,
        to_left,
        shifted(to_right, 1),
        shifted(to_left, -1),
        shifted(edge_right, 2),
        shifted(edge_left, -2),
    )
    grad_feats, grads = incoming(
        relative, feats, cotangent, send, w_first, w_second, w_coarse, windows, kept
    )
    grads = total(grads).astype(F32)
    total_points = devices * num_blocks * block_len
    total_atoms = devices * A_DEV
    factor = 0.5 / math.sqrt(total_points)
    return (
        grad_feats,
        grads[:width] * factor,
        grads[width : 2 * width] * factor,
        grads[2 * width :] * (1.0 / math.sqrt(total_atoms)),
    )


def solution(mesh):
    placed = (
        P("pts", None),
        P(),
        P(),
        P(),
        P("pts", None, None),
        P("pts", None, None),
        P("pts", None),
        P("pts"),
        P("pts"),
        P("pts", None),
    )
    return jax.shard_map(
        body, mesh=mesh, in_specs=placed, out_specs=(P("pts", None), P(), P(), P()), check_vma=False
    )
```

time: 282 us -> 123 us (0.44)
  the two profiles are of different devices: /device:TPU:1 before, /device:TPU:30 now
where the time goes in v1:
time: 123 us
  Pallas kernels  53.2 us (43%)
  waiting for transfers between devices  36.8 us (30%)
  starting transfers between devices  19.6 us (16%)
  local copies, waits for them, and re-layouts  10.9 us (9%)
  other arithmetic  1.59 us (1%)
    ppermute x7, waiting for transfers between devices, total(): other = lax.ppermute(value, 'pts', [(i, i ^ flip) for i in range(count)])  28.8 us
    pallas_call x1, Pallas kernels, incoming(): pl.pallas_call(incoming_kernel, grid=(steps,), in_specs=[tiled(1, 1, TILE...  27.3 us
    pallas_call x1, Pallas kernels, outgoing(): pl.pallas_call(outgoing_kernel, grid_spec=pltpu.PrefetchScalarGridSpec(nu...  25.9 us
    ppermute x4, starting transfers between devices, shifted(): return lax.ppermute(value, 'pts', pairs)  15.1 us
    unnamed x24, local copies, waits for them, and re-layouts  10.7 us
    ppermute x4, waiting for transfers between devices, shifted(): return lax.ppermute(value, 'pts', pairs)  8.01 us
    ppermute x7, starting transfers between devices, total(): other = lax.ppermute(value, 'pts', [(i, i ^ flip) for i in range(count)])  4.55 us
  transfers between devices with their start and end apart: 11, of which 8 were waited for; matrix products, arithmetic and copies ran while one was open for 0% of the time, Pallas kernels for 0%

profile of v1, /device:TPU:30, one launch (start us, length us, event | category | flops | bytes accessed | tf_op | source)
XLA Modules:
  0.0 122.9 jit_solution(17710458498021004317)
XLA Ops:
  0.6 0.7 fusion.3
  1.4 0.1 copy.15
  1.4 0.1 reshape.21.nb_ref
  1.6 1.2 copy-done.3
  2.7 1.2 copy-done.5
  3.9 0.8 copy-done.6
  4.7 0.8 copy-done.8
  5.4 0.7 copy-done.11
  6.1 0.0 copy-start.10
  6.1 25.9 %outgoing.1 = (bf16[14336,256]{1,0:T(8,128)(2,1)S(1)}, bf16[14336,256]{1,0:T(8,128)(2,1)S(1)}, bf16[14336,256]{1,0:T(8,128)(2,1)S(1)}, bf16[96,256]{1,0:T(8,128)...) custom-call(s32[112]{0:T(128)S(1)} %copy-done.11, ...), custom_call_target="tpu_custom_call" | custom-call | tf_op jit(solution)/shard_map/outgoing/pallas_call | solution.py:148
  32.0 3.0 %copy-done.1 = bf16[14336,256]{1,0:T(8,128)(2,1)} copy-done((bf16[14336,256]{1,0:T(8,128)(2,1)}, bf16[14336,256]{1,0:T(8,128)(2,1)S(1)}, u32[]{:S(2)}) %copy-start.1) | copy-done | bytes 7340056
  35.0 1.9 %collective-permute-start = (bf16[96,256]{1,0:T(8,128)(2,1)S(1)}, bf16[96,256]{1,0:T(8,128)(2,1)S(1)}, u32[]{:S(2)}, u32[]{:S(2)}) collective-permute-start(bf16[96,256]{1,0:T(8,128)(2,1)S(1)} %get-tuple-element.13.own_right_ref), channel_id=1, source_target_pairs={{0,1},{1,2},{2,3},{3,4},{4,5},{5,6},{6,7},{7,8},{8,9},{9,10},{10,1... | collective-permute-start | bytes 147464 | tf_op jit(solution)/shard_map/ppermute | solution.py:321
  37.0 3.6 %collective-permute-start.1 = (bf16[96,256]{1,0:T(8,128)(2,1)S(1)}, bf16[96,256]{1,0:T(8,128)(2,1)S(1)}, u32[]{:S(2)}, u32[]{:S(2)}) collective-permute-start(bf16[96,256]{1,0:T(8,128)(2,1)S(1)} %get-tuple-element.14.own_left_ref), channel_id=1, source_target_pairs={{1,0},{2,1},{3,2},{4,3},{5,4},{6,5},{7,6},{8,7},{9,8},{10,9},{11,1... | collective-permute-start | bytes 147464 | tf_op jit(solution)/shard_map/ppermute | solution.py:321
  40.6 7.6 %collective-permute-start.2 = (bf16[48,256]{1,0:T(8,128)(2,1)S(1)}, bf16[48,256]{1,0:T(8,128)(2,1)S(1)}, u32[]{:S(2)}, u32[]{:S(2)}) collective-permute-start(bf16[48,256]{1,0:T(8,128)(2,1)S(1)} %get-tuple-element.15), channel_id=1, source_target_pairs={{0,2},{1,3},{2,4},{3,5},{4,6},{5,7},{6,8},{7,9},{8,10},{9,11},{10,... | collective-permute-start | bytes 73736 | tf_op jit(solution)/shard_map/ppermute | solution.py:321
  48.2 1.9 %collective-permute-start.3 = (bf16[48,256]{1,0:T(8,128)(2,1)S(1)}, bf16[48,256]{1,0:T(8,128)(2,1)S(1)}, u32[]{:S(2)}, u32[]{:S(2)}) collective-permute-start(bf16[48,256]{1,0:T(8,128)(2,1)S(1)} %get-tuple-element.16), channel_id=1, source_target_pairs={{2,0},{3,1},{4,2},{5,3},{6,4},{7,5},{8,6},{9,7},{10,8},{11,9},{12,... | collective-permute-start | bytes 73736 | tf_op jit(solution)/shard_map/ppermute | solution.py:321
  50.2 8.0 %collective-permute-done.3.far_high_ref = bf16[48,256]{1,0:T(8,128)(2,1)S(1)} collective-permute-done((bf16[48,256]{1,0:T(8,128)(2,1)S(1)}, bf16[48,256]{1,0:T(8,128)(2,1)S(1)}, u32[]{:S(2)}, u32[]{:S(2)}) %collective-permute-start.3) | collective-permute-done | bytes 24608 | tf_op jit(solution)/shard_map/ppermute | solution.py:321
  58.2 3.1 %copy-done.2 = bf16[14336,256]{1,0:T(8,128)(2,1)S(1)} copy-done((bf16[14336,256]{1,0:T(8,128)(2,1)S(1)}, bf16[14336,256]{1,0:T(8,128)(2,1)}, u32[]{:S(2)}) %copy-start.2) | copy-done | bytes 7340056
  61.3 27.3 %incoming.1 = (bf16[28672,128]{1,0:T(8,128)(2,1)}, bf16[384,128]{1,0:T(8,128)(2,1)S(1)}) custom-call(s32[14,1,128]{2,1,0:T(1,128)S(1)} %reshape.21.nb_ref, bf16[28672,128]{1,0:T(8,128)(2,1)S(1)} %copy-done, bf16[28672,128]{1,0:T(8,128)(2,1)} %cot_ref.3, bf16[1792,256]{1,0:T(8,128)(2,1)S(1)} %bitcast.3, bf16[128,128]{1,0:T(8,128)(2,1)S(1)} %copy-done.7, ...), custom_call_target="tpu_custom_call" | custom-call | tf_op jit(solution)/shard_map/incoming/pallas_call | solution.py:289
  88.7 1.3 %collective-permute-done.4 = bf16[384,128]{1,0:T(8,128)(2,1)S(1)} collective-permute-done((bf16[384,128]{1,0:T(8,128)(2,1)S(1)}, bf16[384,128]{1,0:T(8,128)(2,1)S(1)}, u32[]{:S(2)}, u32[]{:S(2)}) %collective-permute-start.4) | collective-permute-done | bytes 98336 | tf_op jit(solution)/shard_map/ppermute | solution.py:332
  90.0 0.1 collective-permute-start.5
  90.1 4.8 %collective-permute-done.5 = bf16[384,128]{1,0:T(8,128)(2,1)S(1)} collective-permute-done((bf16[384,128]{1,0:T(8,128)(2,1)S(1)}, bf16[384,128]{1,0:T(8,128)(2,1)S(1)}, u32[]{:S(2)}, u32[]{:S(2)}) %collective-permute-start.5) | collective-permute-done | bytes 98336 | tf_op jit(solution)/shard_map/ppermute | solution.py:332
  95.0 0.1 collective-permute-start.6
  95.1 5.8 %collective-permute-done.6 = bf16[384,128]{1,0:T(8,128)(2,1)S(1)} collective-permute-done((bf16[384,128]{1,0:T(8,128)(2,1)S(1)}, bf16[384,128]{1,0:T(8,128)(2,1)S(1)}, u32[]{:S(2)}, u32[]{:S(2)}) %collective-permute-start.6) | collective-permute-done | bytes 98336 | tf_op jit(solution)/shard_map/ppermute | solution.py:332
  100.9 0.1 collective-permute-start.7
  101.0 4.6 %collective-permute-done.7 = bf16[384,128]{1,0:T(8,128)(2,1)S(1)} collective-permute-done((bf16[384,128]{1,0:T(8,128)(2,1)S(1)}, bf16[384,128]{1,0:T(8,128)(2,1)S(1)}, u32[]{:S(2)}, u32[]{:S(2)}) %collective-permute-start.7) | collective-permute-done | bytes 98336 | tf_op jit(solution)/shard_map/ppermute | solution.py:332
  105.6 0.1 collective-permute-start.8
  105.7 5.8 %collective-permute-done.8 = bf16[384,128]{1,0:T(8,128)(2,1)S(1)} collective-permute-done((bf16[384,128]{1,0:T(8,128)(2,1)S(1)}, bf16[384,128]{1,0:T(8,128)(2,1)S(1)}, u32[]{:S(2)}, u32[]{:S(2)}) %collective-permute-start.8) | collective-permute-done | bytes 98336 | tf_op jit(solution)/shard_map/ppermute | solution.py:332
  111.6 2.0 %collective-permute-start.9 = (bf16[384,128]{1,0:T(8,128)(2,1)S(1)}, bf16[384,128]{1,0:T(8,128)(2,1)S(1)}, u32[]{:S(2)}, u32[]{:S(2)}) collective-permute-start(bf16[384,128]{1,0:T(8,128)(2,1)S(1)} %add_convert_fusion.2), channel_id=1, source_target_pairs={{0,32},{1,33},{2,34},{3,35},{4,36},{5,37},{6,38},{7,39},{8,40},{9,... | collective-permute-start | bytes 294920 | tf_op jit(solution)/shard_map/ppermute | solution.py:332
  113.6 2.7 %collective-permute-done.9 = bf16[384,128]{1,0:T(8,128)(2,1)S(1)} collective-permute-done((bf16[384,128]{1,0:T(8,128)(2,1)S(1)}, bf16[384,128]{1,0:T(8,128)(2,1)S(1)}, u32[]{:S(2)}, u32[]{:S(2)}) %collective-permute-start.9) | collective-permute-done | bytes 98336 | tf_op jit(solution)/shard_map/ppermute | solution.py:332
  116.3 2.2 %collective-permute-start.10 = (bf16[384,128]{1,0:T(8,128)(2,1)S(1)}, bf16[384,128]{1,0:T(8,128)(2,1)S(1)}, u32[]{:S(2)}, u32[]{:S(2)}) collective-permute-start(bf16[384,128]{1,0:T(8,128)(2,1)S(1)} %add_convert_fusion.1), channel_id=1, source_target_pairs={{0,96},{1,97},{2,98},{3,99},{4,100},{5,101},{6,102},{7,103},{8,104... | collective-permute-start | bytes 294920 | tf_op jit(solution)/shard_map/ppermute | solution.py:332
  118.5 3.7 %collective-permute-done.10 = bf16[384,128]{1,0:T(8,128)(2,1)S(1)} collective-permute-done((bf16[384,128]{1,0:T(8,128)(2,1)S(1)}, bf16[384,128]{1,0:T(8,128)(2,1)S(1)}, u32[]{:S(2)}, u32[]{:S(2)}) %collective-permute-start.10) | collective-permute-done | bytes 98336 | tf_op jit(solution)/shard_map/ppermute | solution.py:332
  122.2 0.7 slice_multiply_fusion
  (27 shorter events, 0.2 us)
Async XLA Ops:
  1.5 1.2 copy-start.3
  2.7 1.2 copy-start.5
  3.9 0.8 copy-start.6
  4.7 0.8 copy-start.8
  5.4 0.7 copy-start.11
  6.1 52.1 %copy-start = (bf16[28672,128]{1,0:T(8,128)(2,1)S(1)}, bf16[28672,128]{1,0:T(8,128)(2,1)}, u32[]{:S(2)}) copy-start(bf16[28672,128]{1,0:T(8,128)(2,1)} %feats_ref.3) | copy-start | bytes 22020100
  6.1 52.1 %copy-start.4 = (bf16[112,16,256]{2,1,0:T(8,128)(2,1)S(1)}, bf16[112,16,256]{2,1,0:T(8,128)(2,1)}, u32[]{:S(2)}) copy-start(bf16[112,16,256]{2,1,0:T(8,128)(2,1)} %param.14) | copy-start | bytes 2752516
  6.1 52.1 %copy-start.7 = (bf16[128,128]{1,0:T(8,128)(2,1)S(1)}, bf16[128,128]{1,0:T(8,128)(2,1)}, u32[]{:S(2)}) copy-start(bf16[128,128]{1,0:T(8,128)(2,1)} %w_first_ref.3) | copy-start | bytes 98308
  6.1 52.1 %copy-start.9 = (bf16[128,128]{1,0:T(8,128)(2,1)S(1)}, bf16[128,128]{1,0:T(8,128)(2,1)}, u32[]{:S(2)}) copy-start(bf16[128,128]{1,0:T(8,128)(2,1)} %w_second_ref.3) | copy-start | bytes 98308
  6.1 52.1 %copy-start.10 = (bf16[128,128]{1,0:T(8,128)(2,1)S(1)}, bf16[128,128]{1,0:T(8,128)(2,1)}, u32[]{:S(2)}) copy-start(bf16[128,128]{1,0:T(8,128)(2,1)} %w_coarse_ref.1) | copy-start | bytes 98308
  32.0 3.1 %copy-start.1 = (bf16[14336,256]{1,0:T(8,128)(2,1)}, bf16[14336,256]{1,0:T(8,128)(2,1)S(1)}, u32[]{:S(2)}) copy-start(bf16[14336,256]{1,0:T(8,128)(2,1)S(1)} %get-tuple-element.17.first_ref) | copy-start | bytes 22020100
  35.0 23.1 %collective-permute-start = (bf16[96,256]{1,0:T(8,128)(2,1)S(1)}, bf16[96,256]{1,0:T(8,128)(2,1)S(1)}, u32[]{:S(2)}, u32[]{:S(2)}) collective-permute-start(bf16[96,256]{1,0:T(8,128)(2,1)S(1)} %get-tuple-element.13.own_right_ref), channel_id=1, source_target_pairs={{0,1},{1,2},{2,3},{3,4},{4,5},{5,6},{6,7},{7,8},{8,9},{9,10},{10,1... | collective-permute-start | bytes 147464 | tf_op jit(solution)/shard_map/ppermute | solution.py:321
  37.0 21.2 %collective-permute-start.1 = (bf16[96,256]{1,0:T(8,128)(2,1)S(1)}, bf16[96,256]{1,0:T(8,128)(2,1)S(1)}, u32[]{:S(2)}, u32[]{:S(2)}) collective-permute-start(bf16[96,256]{1,0:T(8,128)(2,1)S(1)} %get-tuple-element.14.own_left_ref), channel_id=1, source_target_pairs={{1,0},{2,1},{3,2},{4,3},{5,4},{6,5},{7,6},{8,7},{9,8},{10,9},{11,1... | collective-permute-start | bytes 147464 | tf_op jit(solution)/shard_map/ppermute | solution.py:321
  40.6 9.6 %collective-permute-start.2 = (bf16[48,256]{1,0:T(8,128)(2,1)S(1)}, bf16[48,256]{1,0:T(8,128)(2,1)S(1)}, u32[]{:S(2)}, u32[]{:S(2)}) collective-permute-start(bf16[48,256]{1,0:T(8,128)(2,1)S(1)} %get-tuple-element.15), channel_id=1, source_target_pairs={{0,2},{1,3},{2,4},{3,5},{4,6},{5,7},{6,8},{7,9},{8,10},{9,11},{10,... | collective-permute-start | bytes 73736 | tf_op jit(solution)/shard_map/ppermute | solution.py:321
  48.2 9.9 %collective-permute-start.3 = (bf16[48,256]{1,0:T(8,128)(2,1)S(1)}, bf16[48,256]{1,0:T(8,128)(2,1)S(1)}, u32[]{:S(2)}, u32[]{:S(2)}) collective-permute-start(bf16[48,256]{1,0:T(8,128)(2,1)S(1)} %get-tuple-element.16), channel_id=1, source_target_pairs={{2,0},{3,1},{4,2},{5,3},{6,4},{7,5},{8,6},{9,7},{10,8},{11,9},{12,... | collective-permute-start | bytes 73736 | tf_op jit(solution)/shard_map/ppermute | solution.py:321
  58.2 3.1 %copy-start.2 = (bf16[14336,256]{1,0:T(8,128)(2,1)S(1)}, bf16[14336,256]{1,0:T(8,128)(2,1)}, u32[]{:S(2)}) copy-start(bf16[14336,256]{1,0:T(8,128)(2,1)} %copy-done.1) | copy-start | bytes 22020100
  88.7 1.3 %collective-permute-start.4 = (bf16[384,128]{1,0:T(8,128)(2,1)S(1)}, bf16[384,128]{1,0:T(8,128)(2,1)S(1)}, u32[]{:S(2)}, u32[]{:S(2)}) collective-permute-start(bf16[384,128]{1,0:T(8,128)(2,1)S(1)} %get-tuple-element.21), channel_id=1, source_target_pairs={{0,1},{1,0},{2,3},{3,2},{4,5},{5,4},{6,7},{7,6},{8,9},{9,8},{10,11... | collective-permute-start | bytes 294920 | tf_op jit(solution)/shard_map/ppermute | solution.py:332
  90.0 4.9 %collective-permute-start.5 = (bf16[384,128]{1,0:T(8,128)(2,1)S(1)}, bf16[384,128]{1,0:T(8,128)(2,1)S(1)}, u32[]{:S(2)}, u32[]{:S(2)}) collective-permute-start(bf16[384,128]{1,0:T(8,128)(2,1)S(1)} %add_convert_fusion.6), channel_id=1, source_target_pairs={{0,2},{1,3},{2,0},{3,1},{4,6},{5,7},{6,4},{7,5},{8,10},{9,11},{10,... | collective-permute-start | bytes 294920 | tf_op jit(solution)/shard_map/ppermute | solution.py:332
  95.0 5.9 %collective-permute-start.6 = (bf16[384,128]{1,0:T(8,128)(2,1)S(1)}, bf16[384,128]{1,0:T(8,128)(2,1)S(1)}, u32[]{:S(2)}, u32[]{:S(2)}) collective-permute-start(bf16[384,128]{1,0:T(8,128)(2,1)S(1)} %add_convert_fusion.5), channel_id=1, source_target_pairs={{0,6},{1,7},{2,4},{3,5},{4,2},{5,3},{6,0},{7,1},{8,14},{9,15},{10,... | collective-permute-start | bytes 294920 | tf_op jit(solution)/shard_map/ppermute | solution.py:332
  100.9 4.7 %collective-permute-start.7 = (bf16[384,128]{1,0:T(8,128)(2,1)S(1)}, bf16[384,128]{1,0:T(8,128)(2,1)S(1)}, u32[]{:S(2)}, u32[]{:S(2)}) collective-permute-start(bf16[384,128]{1,0:T(8,128)(2,1)S(1)} %add_convert_fusion.4), channel_id=1, source_target_pairs={{0,8},{1,9},{2,10},{3,11},{4,12},{5,13},{6,14},{7,15},{8,0},{9,1},... | collective-permute-start | bytes 294920 | tf_op jit(solution)/shard_map/ppermute | solution.py:332
  105.6 5.9 %collective-permute-start.8 = (bf16[384,128]{1,0:T(8,128)(2,1)S(1)}, bf16[384,128]{1,0:T(8,128)(2,1)S(1)}, u32[]{:S(2)}, u32[]{:S(2)}) collective-permute-start(bf16[384,128]{1,0:T(8,128)(2,1)S(1)} %add_convert_fusion.3), channel_id=1, source_target_pairs={{0,24},{1,25},{2,26},{3,27},{4,28},{5,29},{6,30},{7,31},{8,16},{9,... | collective-permute-start | bytes 294920 | tf_op jit(solution)/shard_map/ppermute | solution.py:332
  111.6 4.7 %collective-permute-start.9 = (bf16[384,128]{1,0:T(8,128)(2,1)S(1)}, bf16[384,128]{1,0:T(8,128)(2,1)S(1)}, u32[]{:S(2)}, u32[]{:S(2)}) collective-permute-start(bf16[384,128]{1,0:T(8,128)(2,1)S(1)} %add_convert_fusion.2), channel_id=1, source_target_pairs={{0,32},{1,33},{2,34},{3,35},{4,36},{5,37},{6,38},{7,39},{8,40},{9,... | collective-permute-start | bytes 294920 | tf_op jit(solution)/shard_map/ppermute | solution.py:332
  116.3 5.9 %collective-permute-start.10 = (bf16[384,128]{1,0:T(8,128)(2,1)S(1)}, bf16[384,128]{1,0:T(8,128)(2,1)S(1)}, u32[]{:S(2)}, u32[]{:S(2)}) collective-permute-start(bf16[384,128]{1,0:T(8,128)(2,1)S(1)} %add_convert_fusion.1), channel_id=1, source_target_pairs={{0,96},{1,97},{2,98},{3,99},{4,100},{5,101},{6,102},{7,103},{8,104... | collective-permute-start | bytes 294920 | tf_op jit(solution)/shard_map/ppermute | solution.py:332

commit v2 on v0

v2 whole, which is shorter than its diff:
```python
import math

import jax
import jax.numpy as jnp
from jax import lax
from jax.experimental import pallas as pl
from jax.experimental.pallas import tpu as pltpu
from jax.sharding import PartitionSpec as P

A_DEV = 40
A_PAD = 48
OUT_PAIRS, OUT_GROUP = 28, 7
IN_PAIRS = 7

BF16 = jnp.bfloat16
F32 = jnp.float32


def dot(left, right):
    return jnp.dot(left, right, preferred_element_type=F32)


def dot_rows(left, right):
    return lax.dot_general(left, right, (((0,), (0,)), ((), ())), preferred_element_type=F32)


def diag_pair(weight):
    zero = jnp.zeros_like(weight)
    return jnp.concatenate(
        [jnp.concatenate([weight, zero], axis=1), jnp.concatenate([zero, weight], axis=1)], axis=0
    )


def silu_pair(half):
    up = 1.0 + jnp.tanh(half)
    value = half * up
    return value, up + value * (2.0 - up)


def span(start, size):
    return pl.ds(pl.multiple_of(start, size), size)


def outgoing_kernel(
    first_atom,
    point_count_hbm,
    nbr_count_hbm,
    neighbours_hbm,
    feats_hbm,
    cot_hbm,
    send_hbm,
    ret_hbm,
    w_first_hbm,
    w_second_hbm,
    feats_ref,
    cot_ref,
    send_ref,
    select_ref,
    first_ref,
    slope1_ref,
    slope2_ref,
    part_out_ref,
    ret_ref,
    w_first_ref,
    w_second_ref,
    neighbours_ref,
    point_count_ref,
    nbr_count_ref,
    w1_ref,
    w2_ref,
    spot_ref,
    lane_ref,
    part_ref,
    atoms_ref,
    small_sems,
    sems,
):
    block_len = send_ref.shape[1]
    width = feats_ref.shape[1]
    slots, blocks = neighbours_ref.shape
    half_blocks = blocks // 2
    steps = half_blocks // OUT_PAIRS

    smalls = [
        pltpu.make_async_copy(src, dst, small_sems.at[place])
        for place, (src, dst) in enumerate(
            (
                (w_first_hbm, w_first_ref),
                (w_second_hbm, w_second_ref),
                (point_count_hbm, point_count_ref),
                (nbr_count_hbm, nbr_count_ref),
                (neighbours_hbm, neighbours_ref),
            )
        )
    ]

    def copies(step):
        made = []
        for side in range(2):
            block = step * OUT_PAIRS + side * half_blocks
            points = span(block * block_len, OUT_PAIRS * block_len)
            edges = span(block * slots, OUT_PAIRS * slots)
            for place, (src, dst, rows) in enumerate(
                (
                    (feats_hbm, feats_ref, points),
                    (send_hbm, send_ref, edges),
                    (ret_hbm, ret_ref, edges),
                    (cot_hbm, cot_ref, points),
                )
            ):
                made.append(
                    pltpu.make_async_copy(
                        src.at[rows, :], dst.at[rows, :], sems.at[place * 2 + side, step]
                    )
                )
        return made

    for copy in smalls:
        copy.start()
    for step in range(steps):
        for copy in copies(step):
            copy.start()
    spot_ref[...] = lax.broadcasted_iota(jnp.int32, spot_ref.shape, 0).astype(F32).astype(BF16)
    lane_ref[...] = lax.broadcasted_iota(jnp.int32, lane_ref.shape, 1).astype(F32).astype(BF16)
    part_ref[...] = jnp.zeros_like(part_ref)
    for copy in smalls:
        copy.wait()
    w1_ref[...] = diag_pair(w_first_ref[...] * 0.5)
    w2_ref[...] = diag_pair(w_second_ref[...] * 0.5)
    atoms = neighbours_ref[...] - first_atom
    for step in range(steps):
        for side in range(2):
            block = step * OUT_PAIRS + side * half_blocks
            atoms_ref[step, side] = atoms[:, block : block + OUT_PAIRS]
    column = lax.broadcasted_iota(jnp.int32, (slots, select_ref.shape[1]), 1)
    slot = lax.broadcasted_iota(jnp.int32, (slots, 1), 0)

    def work(step, carry):
        for copy in copies(step):
            copy.wait()
        messages = [[], []]
        backs = [[], []]
        for group in range(0, OUT_PAIRS, OUT_GROUP):
            pairs = [step * OUT_PAIRS + group + i for i in range(OUT_GROUP)]
            near = [span(p * block_len, block_len) for p in pairs]
            far = [span((p + half_blocks) * block_len, block_len) for p in pairs]
            half1 = [
                dot(jnp.concatenate([feats_ref[n, :], feats_ref[f, :]], axis=1), w1_ref[...]).astype(
                    BF16
                )
                for n, f in zip(near, far)
            ]
            firsts = []
            for n, half in zip(near, half1):
                first, slope1 = silu_pair(half)
                first_ref[n, :] = first
                slope1_ref[n, :] = slope1
                firsts.append(first)
            half2 = [dot(first, w2_ref[...]).astype(BF16) for first in firsts]
            points = []
            counts = []
            for p, n, half in zip(pairs, near, half2):
                point, slope2 = silu_pair(half)
                count = [
                    jnp.full((slots, width), point_count_ref[b].astype(F32)).astype(BF16)
                    for b in (p, p + half_blocks)
                ]
                mask = [
                    jnp.clip(jnp.tile(c, (block_len // slots, 1)) - spot_ref[...], 0, 1) for c in count
                ]
                slope2_ref[n, :] = slope2 * jnp.concatenate(mask, axis=1)
                points.append(point)
                counts.append(count)
            for p, n, f, point, count in zip(pairs, near, far, points, counts):
                masks = [jnp.clip(jnp.concatenate([c, c], axis=1) - lane_ref[...], 0, 1) for c in count]
                edges = [span(b * slots, slots) for b in (p, p + half_blocks)]
                send = jnp.concatenate([send_ref[e, :] * m for e, m in zip(edges, masks)], axis=0)
                ret = jnp.concatenate([ret_ref[e, :] * m for e, m in zip(edges, masks)], axis=0)
                cot = jnp.concatenate([cot_ref[n, :], cot_ref[f, :]], axis=1)
                message = dot(send, point)
                back = dot(ret, cot)
                messages[0].append(message[:slots, :width])
                messages[1].append(message[slots:, width:])
                backs[0].append(back[:slots, :width])
                backs[1].append(back[slots:, width:])
        for side in range(2):
            both = jnp.concatenate(
                [jnp.concatenate(messages[side], axis=0), jnp.concatenate(backs[side], axis=0)], axis=1
            ).astype(BF16)
            block = step * OUT_PAIRS + side * half_blocks
            select = []
            for i in range(OUT_PAIRS):
                mine = jnp.where(slot < nbr_count_ref[block + i], atoms_ref[step, side, :, i : i + 1], -1)
                select.append(jnp.where(column == mine, 1.0, 0.0).astype(BF16))
            select = jnp.concatenate(select, axis=0)
            select_ref[span(block * slots, OUT_PAIRS * slots), :] = select
            part_ref[...] += dot_rows(select, both)
        return carry

    lax.fori_loop(0, steps, work, 0)
    part_out_ref[...] = jnp.zeros_like(part_out_ref)
    for place in range(3):
        part_out_ref[pl.ds(place * A_PAD, A_DEV), :] = part_ref[
            pl.ds(place * A_DEV, A_DEV), :
        ].astype(BF16)


def outgoing(
    first_atom, feats, cot, send, ret, neighbours, nbr_count, point_count, w_first, w_second
):
    points, width = feats.shape
    slots, blocks = neighbours.shape
    block_len = points // blocks
    steps = blocks // 2 // OUT_PAIRS
    packed = (points // 2, 2 * width)
    window = (3 * A_PAD, 2 * width)
    vmem = pl.BlockSpec(memory_space=pltpu.VMEM)
    hbm = pl.BlockSpec(memory_space=pltpu.HBM)
    inputs = (point_count, nbr_count, neighbours, feats, cot, send, ret, w_first, w_second)
    weight = pltpu.VMEM((width, width), BF16)
    weights = pltpu.VMEM((2 * width, 2 * width), BF16)

    def kernel(*refs):
        outgoing_kernel(first_atom(), *refs)

    return pl.pallas_call(
        kernel,
        in_specs=[hbm] * len(inputs),
        out_specs=[vmem] * 8,
        out_shape=[
            pltpu.VMEM(feats.shape, BF16),
            pltpu.VMEM(feats.shape, BF16),
            pltpu.VMEM(send.shape, BF16),
            pltpu.VMEM((blocks * slots, width), BF16),
            pltpu.VMEM(packed, BF16),
            pltpu.VMEM(packed, BF16),
            pltpu.VMEM(packed, BF16),
            pltpu.VMEM(window, BF16),
        ],
        scratch_shapes=[
            pltpu.VMEM(ret.shape, BF16),
            weight,
            weight,
            pltpu.VMEM(neighbours.shape, jnp.int32),
            pltpu.SMEM(point_count.shape, jnp.int32),
            pltpu.SMEM(nbr_count.shape, jnp.int32),
            weights,
            weights,
            pltpu.VMEM((block_len, width), BF16),
            pltpu.VMEM((slots, block_len), BF16),
            pltpu.VMEM((width, 2 * width), F32),
            pltpu.VMEM((steps, 2, slots, OUT_PAIRS), jnp.int32),
            pltpu.SemaphoreType.DMA((5,)),
            pltpu.SemaphoreType.DMA((8, steps)),
        ],
        compiler_params=pltpu.CompilerParams(vmem_limit_bytes=12 * 2**20),
        name="outgoing",
    )(*(pltpu.with_memory_space_constraint(value, pltpu.HBM) for value in inputs))


def incoming_kernel(
    side,
    w_first_ref,
    w_second_ref,
    w_coarse_ref,
    kept_ref,
    last_ref,
    feats_ref,
    cot_ref,
    send_ref,
    select_ref,
    first_ref,
    slope1_ref,
    slope2_ref,
    grad_feats_hbm,
    grads_ref,
    stage_ref,
    w1_ref,
    w2_ref,
    total_ref,
    dcoarse_ref,
    dpre1_ref,
    dpre2_ref,
    acc1_ref,
    acc2_ref,
    sems,
):
    width = feats_ref.shape[1]
    block_len = send_ref.shape[1]
    blocks = feats_ref.shape[0] // block_len
    slots = send_ref.shape[0] // blocks
    half_blocks = blocks // 2
    steps = half_blocks // IN_PAIRS
    rows = IN_PAIRS * block_len

    w1_ref[...] = diag_pair(w_first_ref[...].T * 0.5)
    w2_ref[...] = diag_pair(w_second_ref[...].T * 0.5)
    acc1_ref[...] = jnp.zeros_like(acc1_ref)
    acc2_ref[...] = jnp.zeros_like(acc2_ref)
    total_ref[span(side * A_PAD, A_PAD), :] = kept_ref[:A_PAD, :].astype(F32)
    total_ref[span((side + 1) * A_PAD, A_PAD), :] = kept_ref[A_PAD:, :].astype(F32)
    total_ref[span((1 - side) * 2 * A_PAD, A_PAD), :] = last_ref[...].astype(F32)
    coarse = total_ref[:, :width].astype(BF16)
    pre = dot(coarse, w_coarse_ref[...])
    sig = jax.nn.sigmoid(pre)
    slope = sig * (1.0 + pre * (1.0 - sig))
    dpre = (total_ref[:, width:] * slope).astype(BF16)
    dcoarse = dot(dpre, w_coarse_ref[...].T)
    dcoarse = [dcoarse[place * A_PAD : place * A_PAD + A_DEV] for place in range(3)]
    dcoarse.append(jnp.zeros((dcoarse_ref.shape[0] - 3 * A_DEV, width), F32))
    dcoarse_ref[...] = jnp.concatenate(dcoarse, axis=0).astype(BF16)
    grads_ref[2 * width :, :] = dot_rows(coarse[A_PAD : 2 * A_PAD], dpre[A_PAD : 2 * A_PAD]).astype(
        BF16
    )

    def send_out(step):
        slot = lax.rem(step, 2)
        return [
            pltpu.make_async_copy(
                stage_ref.at[slot, half],
                grad_feats_hbm.at[span(step * rows + half * half_blocks * block_len, rows), :],
                sems.at[slot, half],
            )
            for half in range(2)
        ]

    def places(step):
        pairs = [step * IN_PAIRS + i for i in range(IN_PAIRS)]
        near = [span(p * block_len, block_len) for p in pairs]
        far = [span((p + half_blocks) * block_len, block_len) for p in pairs]
        held = [pl.ds(i * block_len, block_len) for i in range(IN_PAIRS)]
        return near, far, held

    def second_grad(step):
        near, far, held = places(step)
        edges = [
            span((step * IN_PAIRS + half * half_blocks) * slots, IN_PAIRS * slots) for half in range(2)
        ]
        send_t = jnp.concatenate([send_ref[e, :] for e in edges], axis=0).T
        spread_in = jnp.concatenate([dot(select_ref[e, :], dcoarse_ref[...]) for e in edges], axis=0)
        owner = lax.broadcasted_iota(jnp.int32, spread_in.shape, 0) // slots
        for p, (n, f, h) in enumerate(zip(near, far, held)):
            share = jnp.concatenate(
                [jnp.where(owner == b, spread_in, 0.0).astype(BF16) for b in (p, p + IN_PAIRS)], axis=1
            )
            spread = dot(send_t, share).astype(BF16)
            cot = jnp.concatenate([cot_ref[n, :], cot_ref[f, :]], axis=1)
            dpre2_ref[h, :] = (cot + spread) * slope2_ref[n, :]

    def first_grad(step):
        near, _, held = places(step)
        for n, h in zip(near, held):
            dfirst = dot(dpre2_ref[h, :], w2_ref[...]).astype(BF16)
            dpre1_ref[h, :] = dfirst * slope1_ref[n, :]
        packed = span(step * IN_PAIRS * block_len, IN_PAIRS * block_len)
        acc2_ref[...] += dot_rows(first_ref[packed, :], dpre2_ref[...])

    def feats_grad(step):
        near, far, held = places(step)
        slot = lax.rem(step, 2)
        for p, h in enumerate(held):
            grad = dot(dpre1_ref[h, :], w1_ref[...]).astype(BF16)
            stage_ref[slot, 0, h, :] = grad[:, :width]
            stage_ref[slot, 1, h, :] = grad[:, width:]
        feats = [jnp.concatenate([feats_ref[n, :], feats_ref[f, :]], axis=1) for n, f in zip(near, far)]
        acc1_ref[...] += dot_rows(jnp.concatenate(feats, axis=0), dpre1_ref[...])

    def depart(step):
        for copy in send_out(step):
            copy.start()

    def work(step, carry):
        @pl.when(step >= 4)
        def _():
            for copy in send_out(step - 4):
                copy.wait()

        feats_grad(step - 2)
        first_grad(step - 1)
        second_grad(step)
        depart(step - 2)
        return carry

    second_grad(0)
    first_grad(0)
    second_grad(1)
    lax.fori_loop(2, steps, work, 0)
    for step in (steps - 2, steps - 1):
        for copy in send_out(step - 2):
            copy.wait()
        feats_grad(step)
        if step < steps - 1:
            first_grad(step + 1)
        depart(step)
    for place, ref in enumerate((acc1_ref, acc2_ref)):
        grads_ref[pl.ds(place * width, width), :] = (ref[:width, :width] + ref[width:, width:]).astype(
            BF16
        )
    for step in range(steps - 2, steps):
        for copy in send_out(step):
            copy.wait()


def incoming(side, w_first, w_second, w_coarse, kept, last, resident):
    points, width = resident[0].shape
    block_len = resident[2].shape[1]
    vmem = pl.BlockSpec(memory_space=pltpu.VMEM)
    resident = [pltpu.with_memory_space_constraint(value, pltpu.VMEM) for value in resident]
    inputs = (w_first, w_second, w_coarse, kept, last, *resident)
    weights = pltpu.VMEM((2 * width, 2 * width), BF16)
    sums = pltpu.VMEM((2 * width, 2 * width), F32)
    held = pltpu.VMEM((IN_PAIRS * block_len, 2 * width), BF16)

    def kernel(*refs):
        incoming_kernel(side(), *refs)

    return pl.pallas_call(
        kernel,
        in_specs=[vmem] * len(inputs),
        out_specs=[pl.BlockSpec(memory_space=pltpu.HBM), vmem],
        out_shape=[pltpu.HBM((points, width), BF16), jax.ShapeDtypeStruct((3 * width, width), BF16)],
        scratch_shapes=[
            pltpu.VMEM((2, 2, IN_PAIRS * block_len, width), BF16),
            weights,
            weights,
            pltpu.VMEM((3 * A_PAD, 2 * width), F32),
            pltpu.VMEM((width, width), BF16),
            held,
            held,
            sums,
            sums,
            pltpu.SemaphoreType.DMA((2, 2)),
        ],
        compiler_params=pltpu.CompilerParams(vmem_limit_bytes=12 * 2**20),
        name="incoming",
    )(*inputs)


def flipped(value, flip):
    count = lax.axis_size("pts")
    return lax.ppermute(value, "pts", [(i, i ^ flip) for i in range(count)])


def added(*values):
    total = values[0].astype(F32)
    for value in values[1:]:
        total = total + value.astype(F32)
    return total.astype(BF16)


def near_sums(part):
    count = lax.axis_size("pts")
    part = part.reshape(3, A_PAD, -1)
    odd = lax.rem(lax.axis_index("pts"), 2) == 1
    kept = jnp.where(odd, part[1:], part[:2])
    other = flipped(jnp.where(odd, part[0], part[2]), 1)
    inner = (lax.broadcasted_iota(jnp.int32, (2, 1, 1), 0) == 0) == odd
    kept = added(kept, jnp.where(inner, other[None], 0.0))
    steps = [(i, i + 1) for i in range(1, count - 1, 2)]
    kept = added(kept, lax.ppermute(kept, "pts", steps + [(j, i) for i, j in steps]))
    last = flipped(jnp.where(odd, kept[0], kept[1]), 1)
    return kept.reshape(2 * A_PAD, -1), last


def device_sum(value):
    count = lax.axis_size("pts")
    odd = lax.rem(lax.axis_index("pts"), 2) == 1
    low, high = jnp.split(value, 2, axis=0)
    part = added(jnp.where(odd, high, low), flipped(jnp.where(odd, low, high), 1))
    place = 1
    while 2 << place <= count:
        part = added(part, *(flipped(part, k << place) for k in (1, 3, 2)))
        place += 2
    other = flipped(part, 1)
    return jnp.concatenate([jnp.where(odd, other, part), jnp.where(odd, part, other)], axis=0)


def body(
    feats,
    w_first,
    w_second,
    w_coarse,
    send_weight,
    return_weight,
    neighbours,
    nbr_count,
    point_count,
    cotangent,
):
    num_blocks, num_slots, block_len = send_weight.shape
    width = feats.shape[1]
    devices = lax.axis_size("pts")
    send = send_weight.reshape(num_blocks * num_slots, block_len)
    ret = return_weight.reshape(num_blocks * num_slots, block_len)
    *resident, part = outgoing(
        lambda: (lax.axis_index("pts") - 1) * A_DEV,
        feats,
        cotangent,
        send,
        ret,
        neighbours.T,
        nbr_count,
        point_count,
        w_first,
        w_second,
    )
    kept, last = near_sums(part)
    grad_feats, grads = incoming(
        lambda: lax.rem(lax.axis_index("pts"), 2), w_first, w_second, w_coarse, kept, last, resident
    )
    grads = device_sum(grads).astype(F32)
    total_points = devices * num_blocks * block_len
    total_atoms = devices * A_DEV
    factor = 0.5 / math.sqrt(total_points)
    return (
        grad_feats,
        grads[:width] * factor,
        grads[width : 2 * width] * factor,
        grads[2 * width :] * (1.0 / math.sqrt(total_atoms)),
    )


def solution(mesh):
    placed = (
        P("pts", None),
        P(),
        P(),
        P(),
        P("pts", None, None),
        P("pts", None, None),
        P("pts", None),
        P("pts"),
        P("pts"),
        P("pts", None),
    )
    return jax.shard_map(
        body, mesh=mesh, in_specs=placed, out_specs=(P("pts", None), P(), P(), P()), check_vma=False
    )
```

time: 282 us -> 69.5 us (0.25)
  waiting for transfers between devices: 147 us -> 15.5 us
  matrix products: 65.6 us -> 0 us
  Pallas kernels: 0 us -> 28.3 us
  other arithmetic: 21.7 us -> 1.03 us
  local copies, waits for them, and re-layouts: 19.8 us -> 0.01 us
  between operations: 14.2 us -> 0.77 us
  starting transfers between devices: 12.6 us -> 23.7 us
    psum x1 -> x0, waiting for transfers between devices: 146 us -> none  [body(): lax.psum((grad_one, grad_two, grad_coarse), 'pts')]
    dot_general x15 -> x0, matrix products: 65.6 us -> none  [the longest x1 15.8 us: body(): pre2 = jnp.dot(first, w_second, preferred_element_type=jnp.float32)]
    pallas_call x0 -> x2, Pallas kernels: none -> 28.3 us  [the longest x1 14.5 us: outgoing(): pl.pallas_call(kernel, in_specs=[hbm] * len(inputs), out_specs=[vmem] * 8...]
    convert_element_type x2 -> x7, other arithmetic: 17.8 us -> 0.3 us  [the longest x6 0.28 us: added(): return total.astype(BF16)]
    dot_general x1 -> x0, local copies, waits for them, and re-layouts: 15.1 us -> none  [body(): jnp.einsum('bkp,bkc->bpc', send_weight, message_grad.reshape(num_blocks,...]
    ppermute x4 -> x14, waiting for transfers between devices: 1.08 us -> 15.5 us  [the longest x13 13.6 us: flipped(): return lax.ppermute(value, 'pts', [(i, i ^ flip) for i in range(count)])]
    ppermute x4 -> x14, starting transfers between devices: 12.6 us -> 23.7 us  [the longest x13 20.3 us: flipped(): return lax.ppermute(value, 'pts', [(i, i ^ flip) for i in range(count)])]
    unnamed x19 -> x6, local copies, waits for them, and re-layouts: 4.5 us -> 0.01 us
  transfers between devices with their start and end apart: 5 -> 14, of which waited for: 2 -> 11; matrix products, arithmetic and copies ran while one was open for 3% -> 0% of each run, Pallas kernels for 0% -> 0%
where the time goes in v2:
time: 69.5 us; the launch traced here: 69.4 us
  Pallas kernels  28.3 us (41%)
  starting transfers between devices  23.7 us (34%)
  waiting for transfers between devices  15.5 us (22%)
  other arithmetic  1.03 us (1%)
  between operations  0.77 us (1%)
    ppermute x13, starting transfers between devices, flipped(): return lax.ppermute(value, 'pts', [(i, i ^ flip) for i in range(count)])  20.3 us
    pallas_call x1, Pallas kernels, outgoing(): pl.pallas_call(kernel, in_specs=[hbm] * len(inputs), out_specs=[vmem] * 8...  14.5 us
    pallas_call x1, Pallas kernels, incoming(): pl.pallas_call(kernel, in_specs=[vmem] * len(inputs), out_specs=[pl.Block...  13.8 us
    ppermute x13, waiting for transfers between devices, flipped(): return lax.ppermute(value, 'pts', [(i, i ^ flip) for i in range(count)])  13.6 us
    ppermute x1, starting transfers between devices, near_sums(): lax.ppermute(kept, 'pts', steps + [(j, i) for i, j in steps])  3.43 us
    ppermute x1, waiting for transfers between devices, near_sums(): lax.ppermute(kept, 'pts', steps + [(j, i) for i, j in steps])  1.97 us
  transfers between devices with their start and end apart: 14, of which 11 were waited for; matrix products, arithmetic and copies ran while one was open for 0% of the time, Pallas kernels for 0%

profile of v2, /device:TPU:1, one launch (start us, length us, event | category | flops | bytes accessed | tf_op | source)
XLA Modules:
  0.0 69.4 jit_solution(16826274825958427860)
XLA Ops:
  0.7 14.5 %outgoing.1 = (bf16[28672,128]{1,0:T(8,128)(2,1)S(1)}, bf16[28672,128]{1,0:T(8,128)(2,1)S(1)}, bf16[1792,256]{1,0:T(8,128)(2,1)S(1)}, bf16[1792,128]{1,0:T(8,128...) custom-call(s32[112]{0:T(128)} %refs_0_.2, ...), custom_call_target="tpu_custom_call" | custom-call | tf_op jit(solution)/shard_map/outgoing/pallas_call | solution.py:226
  15.2 1.5 %collective-permute-start = (bf16[48,256]{1,0:T(8,128)(2,1)S(1)}, bf16[48,256]{1,0:T(8,128)(2,1)S(1)}, u32[]{:S(2)}, u32[]{:S(2)}) collective-permute-start(bf16[48,256]{1,0:T(8,128)(2,1)S(1)} %slice_select_fusion.2), channel_id=1, source_target_pairs={{0,1},{1,0},{2,3},{3,2},{4,5},{5,4},{6,7},{7,6},{8,9},{9,8},{10,11... | collective-permute-start | bytes 73736 | tf_op jit(solution)/shard_map/ppermute | solution.py:441
  16.8 0.8 %collective-permute-done = bf16[48,256]{1,0:T(8,128)(2,1)S(1)} collective-permute-done((bf16[48,256]{1,0:T(8,128)(2,1)S(1)}, bf16[48,256]{1,0:T(8,128)(2,1)S(1)}, u32[]{:S(2)}, u32[]{:S(2)}) %collective-permute-start) | collective-permute-done | bytes 24608 | tf_op jit(solution)/shard_map/ppermute | solution.py:441
  17.6 0.1 fusion
  17.7 3.4 %collective-permute-start.1 = (bf16[2,48,256]{2,1,0:T(8,128)(2,1)S(1)}, bf16[2,48,256]{2,1,0:T(8,128)(2,1)S(1)}, u32[]{:S(2)}, u32[]{:S(2)}) collective-permute-start(bf16[2,48,256]{2,1,0:T(8,128)(2,1)S(1)} %fusion), channel_id=1, source_target_pairs={{1,2},{3,4},{5,6},{7,8},{9,10},{11,12},{13,14},{15,16},{17,18},{19... | collective-permute-start | bytes 147464 | tf_op jit(solution)/shard_map/ppermute | solution.py:460
  21.1 2.0 %collective-permute-done.1 = bf16[2,48,256]{2,1,0:T(8,128)(2,1)S(1)} collective-permute-done((bf16[2,48,256]{2,1,0:T(8,128)(2,1)S(1)}, bf16[2,48,256]{2,1,0:T(8,128)(2,1)S(1)}, u32[]{:S(2)}, u32[]{:S(2)}) %collective-permute-start.1) | collective-permute-done | bytes 49184 | tf_op jit(solution)/shard_map/ppermute | solution.py:460
  23.1 0.1 add_convert_fusion.4
  23.2 0.1 collective-permute-start.2
  23.3 1.2 %collective-permute-done.2.refs_4_ = bf16[48,256]{1,0:T(8,128)(2,1)S(1)} collective-permute-done((bf16[48,256]{1,0:T(8,128)(2,1)S(1)}, bf16[48,256]{1,0:T(8,128)(2,1)S(1)}, u32[]{:S(2)}, u32[]{:S(2)}) %collective-permute-start.2) | collective-permute-done | bytes 24608 | tf_op jit(solution)/shard_map/ppermute | solution.py:441
  24.5 13.8 %incoming.1 = (bf16[28672,128]{1,0:T(8,128)(2,1)}, bf16[384,128]{1,0:T(8,128)(2,1)S(1)}) custom-call(bf16[128,128]{1,0:T(8,128)(2,1)S(1)} %copy-done, bf16[128,128]{1,0:T(8,128)(2,1)S(1)} %copy-done.1, bf16[128,128]{1,0:T(8,128)(2,1)S(1)} %copy-done.2, bf16[96,256]{1,0:T(8,128)(2,1)S(1)} %bitcast.8, bf16[48,256]{1,0:T(8,128)(2,1)S(1)} %collective-permute-done.2.refs_4_, ...), custom_call_target="tpu_custom_call" | custom-call | tf_op jit(solution)/shard_map/incoming/pallas_call | solution.py:417
  38.3 0.2 collective-permute-start.3
  38.5 1.1 %collective-permute-done.3 = bf16[192,128]{1,0:T(8,128)(2,1)S(1)} collective-permute-done((bf16[192,128]{1,0:T(8,128)(2,1)S(1)}, bf16[192,128]{1,0:T(8,128)(2,1)S(1)}, u32[]{:S(2)}, u32[]{:S(2)}) %collective-permute-start.3) | collective-permute-done | bytes 49184 | tf_op jit(solution)/shard_map/ppermute | solution.py:441
  39.6 2.9 %collective-permute-start.6 = (bf16[192,128]{1,0:T(8,128)(2,1)S(1)}, bf16[192,128]{1,0:T(8,128)(2,1)S(1)}, u32[]{:S(2)}, u32[]{:S(2)}) collective-permute-start(bf16[192,128]{1,0:T(8,128)(2,1)S(1)} %add_convert_fusion.3), channel_id=1, source_target_pairs={{0,4},{1,5},{2,6},{3,7},{4,0},{5,1},{6,2},{7,3},{8,12},{9,13},{10,... | collective-permute-start | bytes 147464 | tf_op jit(solution)/shard_map/ppermute | solution.py:441
  42.5 1.9 %collective-permute-start.5 = (bf16[192,128]{1,0:T(8,128)(2,1)S(1)}, bf16[192,128]{1,0:T(8,128)(2,1)S(1)}, u32[]{:S(2)}, u32[]{:S(2)}) collective-permute-start(bf16[192,128]{1,0:T(8,128)(2,1)S(1)} %add_convert_fusion.3), channel_id=1, source_target_pairs={{0,6},{1,7},{2,4},{3,5},{4,2},{5,3},{6,0},{7,1},{8,14},{9,15},{10,... | collective-permute-start | bytes 147464 | tf_op jit(solution)/shard_map/ppermute | solution.py:441
  44.5 0.5 collective-permute-start.4
  45.0 0.0 collective-permute-done.6
  45.0 1.7 %collective-permute-done.5 = bf16[192,128]{1,0:T(8,128)(2,1)S(1)} collective-permute-done((bf16[192,128]{1,0:T(8,128)(2,1)S(1)}, bf16[192,128]{1,0:T(8,128)(2,1)S(1)}, u32[]{:S(2)}, u32[]{:S(2)}) %collective-permute-start.5) | collective-permute-done | bytes 49184 | tf_op jit(solution)/shard_map/ppermute | solution.py:441
  46.7 1.2 %collective-permute-done.4 = bf16[192,128]{1,0:T(8,128)(2,1)S(1)} collective-permute-done((bf16[192,128]{1,0:T(8,128)(2,1)S(1)}, bf16[192,128]{1,0:T(8,128)(2,1)S(1)}, u32[]{:S(2)}, u32[]{:S(2)}) %collective-permute-start.4) | collective-permute-done | bytes 49184 | tf_op jit(solution)/shard_map/ppermute | solution.py:441
  47.9 3.0 %collective-permute-start.9 = (bf16[192,128]{1,0:T(8,128)(2,1)S(1)}, bf16[192,128]{1,0:T(8,128)(2,1)S(1)}, u32[]{:S(2)}, u32[]{:S(2)}) collective-permute-start(bf16[192,128]{1,0:T(8,128)(2,1)S(1)} %add_convert_fusion.2), channel_id=1, source_target_pairs={{0,16},{1,17},{2,18},{3,19},{4,20},{5,21},{6,22},{7,23},{8,24},{9,... | collective-permute-start | bytes 147464 | tf_op jit(solution)/shard_map/ppermute | solution.py:441
  50.9 1.7 %collective-permute-start.8 = (bf16[192,128]{1,0:T(8,128)(2,1)S(1)}, bf16[192,128]{1,0:T(8,128)(2,1)S(1)}, u32[]{:S(2)}, u32[]{:S(2)}) collective-permute-start(bf16[192,128]{1,0:T(8,128)(2,1)S(1)} %add_convert_fusion.2), channel_id=1, source_target_pairs={{0,24},{1,25},{2,26},{3,27},{4,28},{5,29},{6,30},{7,31},{8,16},{9,... | collective-permute-start | bytes 147464 | tf_op jit(solution)/shard_map/ppermute | solution.py:441
  52.6 0.5 collective-permute-start.7
  53.1 0.0 collective-permute-done.9
  53.1 1.9 %collective-permute-done.8 = bf16[192,128]{1,0:T(8,128)(2,1)S(1)} collective-permute-done((bf16[192,128]{1,0:T(8,128)(2,1)S(1)}, bf16[192,128]{1,0:T(8,128)(2,1)S(1)}, u32[]{:S(2)}, u32[]{:S(2)}) %collective-permute-start.8) | collective-permute-done | bytes 49184 | tf_op jit(solution)/shard_map/ppermute | solution.py:441
  55.1 0.5 collective-permute-done.7
  55.6 3.9 %collective-permute-start.12 = (bf16[192,128]{1,0:T(8,128)(2,1)S(1)}, bf16[192,128]{1,0:T(8,128)(2,1)S(1)}, u32[]{:S(2)}, u32[]{:S(2)}) collective-permute-start(bf16[192,128]{1,0:T(8,128)(2,1)S(1)} %add_convert_fusion.1), channel_id=1, source_target_pairs={{0,64},{1,65},{2,66},{3,67},{4,68},{5,69},{6,70},{7,71},{8,72},{9,... | collective-permute-start | bytes 147464 | tf_op jit(solution)/shard_map/ppermute | solution.py:441
  59.6 0.4 collective-permute-start.11
  60.0 0.0 collective-permute-start.10
  60.0 1.1 %collective-permute-done.12 = bf16[192,128]{1,0:T(8,128)(2,1)S(1)} collective-permute-done((bf16[192,128]{1,0:T(8,128)(2,1)S(1)}, bf16[192,128]{1,0:T(8,128)(2,1)S(1)}, u32[]{:S(2)}, u32[]{:S(2)}) %collective-permute-start.12) | collective-permute-done | bytes 49184 | tf_op jit(solution)/shard_map/ppermute | solution.py:441
  61.0 3.2 %collective-permute-done.11 = bf16[192,128]{1,0:T(8,128)(2,1)S(1)} collective-permute-done((bf16[192,128]{1,0:T(8,128)(2,1)S(1)}, bf16[192,128]{1,0:T(8,128)(2,1)S(1)}, u32[]{:S(2)}, u32[]{:S(2)}) %collective-permute-start.11) | collective-permute-done | bytes 49184 | tf_op jit(solution)/shard_map/ppermute | solution.py:441
  64.3 3.6 %collective-permute-start.13 = (bf16[192,128]{1,0:T(8,128)(2,1)S(1)}, bf16[192,128]{1,0:T(8,128)(2,1)S(1)}, u32[]{:S(2)}, u32[]{:S(2)}) collective-permute-start(bf16[192,128]{1,0:T(8,128)(2,1)S(1)} %add_convert_fusion), channel_id=1, source_target_pairs={{0,1},{1,0},{2,3},{3,2},{4,5},{5,4},{6,7},{7,6},{8,9},{9,8},{10,11... | collective-permute-start | bytes 147464 | tf_op jit(solution)/shard_map/ppermute | solution.py:441
  67.8 0.9 %collective-permute-done.13 = bf16[192,128]{1,0:T(8,128)(2,1)S(1)} collective-permute-done((bf16[192,128]{1,0:T(8,128)(2,1)S(1)}, bf16[192,128]{1,0:T(8,128)(2,1)S(1)}, u32[]{:S(2)}, u32[]{:S(2)}) %collective-permute-start.13) | collective-permute-done | bytes 49184 | tf_op jit(solution)/shard_map/ppermute | solution.py:441
  68.8 0.7 slice_multiply_fusion
  (18 shorter events, 0.2 us)
Async XLA Ops:
  0.6 23.8 %copy-start = (bf16[128,128]{1,0:T(8,128)(2,1)S(1)}, bf16[128,128]{1,0:T(8,128)(2,1)}, u32[]{:S(2)}) copy-start(bf16[128,128]{1,0:T(8,128)(2,1)} %refs_0_.3) | copy-start | bytes 98308
  0.6 23.8 %copy-start.1 = (bf16[128,128]{1,0:T(8,128)(2,1)S(1)}, bf16[128,128]{1,0:T(8,128)(2,1)}, u32[]{:S(2)}) copy-start(bf16[128,128]{1,0:T(8,128)(2,1)} %refs_1_.3) | copy-start | bytes 98308
  0.7 23.8 %copy-start.2 = (bf16[128,128]{1,0:T(8,128)(2,1)S(1)}, bf16[128,128]{1,0:T(8,128)(2,1)}, u32[]{:S(2)}) copy-start(bf16[128,128]{1,0:T(8,128)(2,1)} %refs_2_.1) | copy-start | bytes 98308
  15.2 2.4 %collective-permute-start = (bf16[48,256]{1,0:T(8,128)(2,1)S(1)}, bf16[48,256]{1,0:T(8,128)(2,1)S(1)}, u32[]{:S(2)}, u32[]{:S(2)}) collective-permute-start(bf16[48,256]{1,0:T(8,128)(2,1)S(1)} %slice_select_fusion.2), channel_id=1, source_target_pairs={{0,1},{1,0},{2,3},{3,2},{4,5},{5,4},{6,7},{7,6},{8,9},{9,8},{10,11... | collective-permute-start | bytes 73736 | tf_op jit(solution)/shard_map/ppermute | solution.py:441
  17.7 5.4 %collective-permute-start.1 = (bf16[2,48,256]{2,1,0:T(8,128)(2,1)S(1)}, bf16[2,48,256]{2,1,0:T(8,128)(2,1)S(1)}, u32[]{:S(2)}, u32[]{:S(2)}) collective-permute-start(bf16[2,48,256]{2,1,0:T(8,128)(2,1)S(1)} %fusion), channel_id=1, source_target_pairs={{1,2},{3,4},{5,6},{7,8},{9,10},{11,12},{13,14},{15,16},{17,18},{19... | collective-permute-start | bytes 147464 | tf_op jit(solution)/shard_map/ppermute | solution.py:460
  23.2 1.3 %collective-permute-start.2 = (bf16[48,256]{1,0:T(8,128)(2,1)S(1)}, bf16[48,256]{1,0:T(8,128)(2,1)S(1)}, u32[]{:S(2)}, u32[]{:S(2)}) collective-permute-start(bf16[48,256]{1,0:T(8,128)(2,1)S(1)} %fusion.1), channel_id=1, source_target_pairs={{0,1},{1,0},{2,3},{3,2},{4,5},{5,4},{6,7},{7,6},{8,9},{9,8},{10,11... | collective-permute-start | bytes 73736 | tf_op jit(solution)/shard_map/ppermute | solution.py:441
  38.3 1.3 %collective-permute-start.3 = (bf16[192,128]{1,0:T(8,128)(2,1)S(1)}, bf16[192,128]{1,0:T(8,128)(2,1)S(1)}, u32[]{:S(2)}, u32[]{:S(2)}) collective-permute-start(bf16[192,128]{1,0:T(8,128)(2,1)S(1)} %broadcast_select_fusion.2), channel_id=1, source_target_pairs={{0,1},{1,0},{2,3},{3,2},{4,5},{5,4},{6,7},{7,6},{8,9},{9,8},{10,11... | collective-permute-start | bytes 147464 | tf_op jit(solution)/shard_map/ppermute | solution.py:441
  39.6 5.3 %collective-permute-start.6 = (bf16[192,128]{1,0:T(8,128)(2,1)S(1)}, bf16[192,128]{1,0:T(8,128)(2,1)S(1)}, u32[]{:S(2)}, u32[]{:S(2)}) collective-permute-start(bf16[192,128]{1,0:T(8,128)(2,1)S(1)} %add_convert_fusion.3), channel_id=1, source_target_pairs={{0,4},{1,5},{2,6},{3,7},{4,0},{5,1},{6,2},{7,3},{8,12},{9,13},{10,... | collective-permute-start | bytes 147464 | tf_op jit(solution)/shard_map/ppermute | solution.py:441
  42.5 4.2 %collective-permute-start.5 = (bf16[192,128]{1,0:T(8,128)(2,1)S(1)}, bf16[192,128]{1,0:T(8,128)(2,1)S(1)}, u32[]{:S(2)}, u32[]{:S(2)}) collective-permute-start(bf16[192,128]{1,0:T(8,128)(2,1)S(1)} %add_convert_fusion.3), channel_id=1, source_target_pairs={{0,6},{1,7},{2,4},{3,5},{4,2},{5,3},{6,0},{7,1},{8,14},{9,15},{10,... | collective-permute-start | bytes 147464 | tf_op jit(solution)/shard_map/ppermute | solution.py:441
  44.5 3.4 %collective-permute-start.4 = (bf16[192,128]{1,0:T(8,128)(2,1)S(1)}, bf16[192,128]{1,0:T(8,128)(2,1)S(1)}, u32[]{:S(2)}, u32[]{:S(2)}) collective-permute-start(bf16[192,128]{1,0:T(8,128)(2,1)S(1)} %add_convert_fusion.3), channel_id=1, source_target_pairs={{0,2},{1,3},{2,0},{3,1},{4,6},{5,7},{6,4},{7,5},{8,10},{9,11},{10,... | collective-permute-start | bytes 147464 | tf_op jit(solution)/shard_map/ppermute | solution.py:441
  47.9 5.2 %collective-permute-start.9 = (bf16[192,128]{1,0:T(8,128)(2,1)S(1)}, bf16[192,128]{1,0:T(8,128)(2,1)S(1)}, u32[]{:S(2)}, u32[]{:S(2)}) collective-permute-start(bf16[192,128]{1,0:T(8,128)(2,1)S(1)} %add_convert_fusion.2), channel_id=1, source_target_pairs={{0,16},{1,17},{2,18},{3,19},{4,20},{5,21},{6,22},{7,23},{8,24},{9,... | collective-permute-start | bytes 147464 | tf_op jit(solution)/shard_map/ppermute | solution.py:441
  50.9 4.2 %collective-permute-start.8 = (bf16[192,128]{1,0:T(8,128)(2,1)S(1)}, bf16[192,128]{1,0:T(8,128)(2,1)S(1)}, u32[]{:S(2)}, u32[]{:S(2)}) collective-permute-start(bf16[192,128]{1,0:T(8,128)(2,1)S(1)} %add_convert_fusion.2), channel_id=1, source_target_pairs={{0,24},{1,25},{2,26},{3,27},{4,28},{5,29},{6,30},{7,31},{8,16},{9,... | collective-permute-start | bytes 147464 | tf_op jit(solution)/shard_map/ppermute | solution.py:441
  52.6 2.9 %collective-permute-start.7 = (bf16[192,128]{1,0:T(8,128)(2,1)S(1)}, bf16[192,128]{1,0:T(8,128)(2,1)S(1)}, u32[]{:S(2)}, u32[]{:S(2)}) collective-permute-start(bf16[192,128]{1,0:T(8,128)(2,1)S(1)} %add_convert_fusion.2), channel_id=1, source_target_pairs={{0,8},{1,9},{2,10},{3,11},{4,12},{5,13},{6,14},{7,15},{8,0},{9,1},... | collective-permute-start | bytes 147464 | tf_op jit(solution)/shard_map/ppermute | solution.py:441
  55.6 5.4 %collective-permute-start.12 = (bf16[192,128]{1,0:T(8,128)(2,1)S(1)}, bf16[192,128]{1,0:T(8,128)(2,1)S(1)}, u32[]{:S(2)}, u32[]{:S(2)}) collective-permute-start(bf16[192,128]{1,0:T(8,128)(2,1)S(1)} %add_convert_fusion.1), channel_id=1, source_target_pairs={{0,64},{1,65},{2,66},{3,67},{4,68},{5,69},{6,70},{7,71},{8,72},{9,... | collective-permute-start | bytes 147464 | tf_op jit(solution)/shard_map/ppermute | solution.py:441
  59.6 4.7 %collective-permute-start.11 = (bf16[192,128]{1,0:T(8,128)(2,1)S(1)}, bf16[192,128]{1,0:T(8,128)(2,1)S(1)}, u32[]{:S(2)}, u32[]{:S(2)}) collective-permute-start(bf16[192,128]{1,0:T(8,128)(2,1)S(1)} %add_convert_fusion.1), channel_id=1, source_target_pairs={{0,96},{1,97},{2,98},{3,99},{4,100},{5,101},{6,102},{7,103},{8,104... | collective-permute-start | bytes 147464 | tf_op jit(solution)/shard_map/ppermute | solution.py:441
  60.0 4.3 %collective-permute-start.10 = (bf16[192,128]{1,0:T(8,128)(2,1)S(1)}, bf16[192,128]{1,0:T(8,128)(2,1)S(1)}, u32[]{:S(2)}, u32[]{:S(2)}) collective-permute-start(bf16[192,128]{1,0:T(8,128)(2,1)S(1)} %add_convert_fusion.1), channel_id=1, source_target_pairs={{0,32},{1,33},{2,34},{3,35},{4,36},{5,37},{6,38},{7,39},{8,40},{9,... | collective-permute-start | bytes 147464 | tf_op jit(solution)/shard_map/ppermute | solution.py:441
  64.3 4.4 %collective-permute-start.13 = (bf16[192,128]{1,0:T(8,128)(2,1)S(1)}, bf16[192,128]{1,0:T(8,128)(2,1)S(1)}, u32[]{:S(2)}, u32[]{:S(2)}) collective-permute-start(bf16[192,128]{1,0:T(8,128)(2,1)S(1)} %add_convert_fusion), channel_id=1, source_target_pairs={{0,1},{1,0},{2,3},{3,2},{4,5},{5,4},{6,7},{7,6},{8,9},{9,8},{10,11... | collective-permute-start | bytes 147464 | tf_op jit(solution)/shard_map/ppermute | solution.py:441

commit v3 on v2

--- a/solution.py
+++ b/solution.py
@@ -9,8 +9,9 @@
 
 A_DEV = 40
 A_PAD = 48
-OUT_PAIRS, OUT_GROUP = 28, 7
-IN_PAIRS = 7
+AHEAD = 2
+OUT_PAIRS, OUT_MERGE = 8, 2
+IN_PAIRS, IN_MERGE = 8, 2
 
 BF16 = jnp.bfloat16
 F32 = jnp.float32
@@ -72,6 +73,9 @@
     lane_ref,
     part_ref,
     atoms_ref,
+    half1_ref,
+    half2_ref,
+    both_ref,
     small_sems,
     sems,
 ):
@@ -94,7 +98,7 @@
         )
     ]
 
-    def copies(step):
+    def copies(step, arrays):
         made = []
         for side in range(2):
             block = step * OUT_PAIRS + side * half_blocks
@@ -108,18 +112,35 @@
                     (cot_hbm, cot_ref, points),
                 )
             ):
-                made.append(
-                    pltpu.make_async_copy(
-                        src.at[rows, :], dst.at[rows, :], sems.at[place * 2 + side, step]
+                if place in arrays:
+                    made.append(
+                        pltpu.make_async_copy(
+                            src.at[rows, :], dst.at[rows, :], sems.at[place * 2 + side, step]
+                        )
                     )
-                )
         return made
 
+    def ask(step, arrays):
+        def start():
+            for copy in copies(step, arrays):
+                copy.start()
+
+        if isinstance(step, int):
+            if step < steps:
+                start()
+        else:
+            pl.when(step < steps)(start)
+
+    def arrive(step, arrays):
+        for copy in copies(step, arrays):
+            copy.wait()
+
+    points_in, others_in = (0,), (1, 2, 3)
     for copy in smalls:
         copy.start()
-    for step in range(steps):
-        for copy in copies(step):
-            copy.start()
+    for step in range(AHEAD):
+        ask(step, points_in)
+    ask(0, others_in)
     spot_ref[...] = lax.broadcasted_iota(jnp.int32, spot_ref.shape, 0).astype(F32).astype(BF16)
     lane_ref[...] = lax.broadcasted_iota(jnp.int32, lane_ref.shape, 1).astype(F32).astype(BF16)
     part_ref[...] = jnp.zeros_like(part_ref)
@@ -135,58 +156,53 @@
     column = lax.broadcasted_iota(jnp.int32, (slots, select_ref.shape[1]), 1)
     slot = lax.broadcasted_iota(jnp.int32, (slots, 1), 0)
 
-    def work(step, carry):
-        for copy in copies(step):
-            copy.wait()
-        messages = [[], []]
-        backs = [[], []]
-        for group in range(0, OUT_PAIRS, OUT_GROUP):
-            pairs = [step * OUT_PAIRS + group + i for i in range(OUT_GROUP)]
-            near = [span(p * block_len, block_len) for p in pairs]
-            far = [span((p + half_blocks) * block_len, block_len) for p in pairs]
-            half1 = [
-                dot(jnp.concatenate([feats_ref[n, :], feats_ref[f, :]], axis=1), w1_ref[...]).astype(
-                    BF16
-                )
-                for n, f in zip(near, far)
+    size = OUT_MERGE * block_len
+
+    def rows(step, i, merge=OUT_MERGE):
+        near, far = [
+            pl.ds(pl.multiple_of((step * OUT_PAIRS + i + b) * block_len, block_len), merge * block_len)
+            for b in (0, half_blocks)
+        ]
+        return near, far, pl.ds(i * block_len, merge * block_len)
+
+    def start_layer(step, i):
+        near, far, held = rows(step, i)
+        x = jnp.concatenate([feats_ref[near, :], feats_ref[far, :]], axis=1)
+        half1_ref[held, :] = dot(x, w1_ref[...]).astype(BF16)
+
+    def second_layer(step, i):
+        near, _, held = rows(step, i)
+        first, slope1 = silu_pair(half1_ref[held, :])
+        first_ref[near, :] = first
+        slope1_ref[near, :] = slope1
+        half2_ref[held, :] = dot(first, w2_ref[...]).astype(BF16)
+
+    def messages(step, i):
+        for j in range(i, i + OUT_MERGE):
+            p = step * OUT_PAIRS + j
+            near, far, held = rows(step, j, 1)
+            point, slope2 = silu_pair(half2_ref[held, :])
+            count = [
+                jnp.full((slots, width), point_count_ref[b].astype(F32)).astype(BF16)
+                for b in (p, p + half_blocks)
             ]
-            firsts = []
-            for n, half in zip(near, half1):
-                first, slope1 = silu_pair(half)
-                first_ref[n, :] = first
-                slope1_ref[n, :] = slope1
-                firsts.append(first)
-            half2 = [dot(first, w2_ref[...]).astype(BF16) for first in firsts]
-            points = []
-            counts = []
-            for p, n, half in zip(pairs, near, half2):
-                point, slope2 = silu_pair(half)
-                count = [
-                    jnp.full((slots, width), point_count_ref[b].astype(F32)).astype(BF16)
-                    for b in (p, p + half_blocks)
-                ]
-                mask = [
-                    jnp.clip(jnp.tile(c, (block_len // slots, 1)) - spot_ref[...], 0, 1) for c in count
-                ]
-                slope2_ref[n, :] = slope2 * jnp.concatenate(mask, axis=1)
-                points.append(point)
-                counts.append(count)
-            for p, n, f, point, count in zip(pairs, near, far, points, counts):
-                masks = [jnp.clip(jnp.concatenate([c, c], axis=1) - lane_ref[...], 0, 1) for c in count]
-                edges = [span(b * slots, slots) for b in (p, p + half_blocks)]
-                send = jnp.concatenate([send_ref[e, :] * m for e, m in zip(edges, masks)], axis=0)
-                ret = jnp.concatenate([ret_ref[e, :] * m for e, m in zip(edges, masks)], axis=0)
-                cot = jnp.concatenate([cot_ref[n, :], cot_ref[f, :]], axis=1)
-                message = dot(send, point)
-                back = dot(ret, cot)
-                messages[0].append(message[:slots, :width])
-                messages[1].append(message[slots:, width:])
-                backs[0].append(back[:slots, :width])
-                backs[1].append(back[slots:, width:])
+            mask = [jnp.clip(jnp.tile(c, (block_len // slots, 1)) - spot_ref[...], 0, 1) for c in count]
+            slope2_ref[near, :] = slope2 * jnp.concatenate(mask, axis=1)
+            masks = [jnp.clip(jnp.concatenate([c, c], axis=1) - lane_ref[...], 0, 1) for c in count]
+            edges = [span(b * slots, slots) for b in (p, p + half_blocks)]
+            send = jnp.concatenate([send_ref[e, :] * m for e, m in zip(edges, masks)], axis=0)
+            ret = jnp.concatenate([ret_ref[e, :] * m for e, m in zip(edges, masks)], axis=0)
+            cot = jnp.concatenate([cot_ref[near, :], cot_ref[far, :]], axis=1)
+            sent = dot(send, point)
+            returned = dot(ret, cot)
+            mine = pl.ds(j * slots, slots)
+            for side in range(2):
+                lanes = slice(side * width, (side + 1) * width)
+                both_ref[side, mine, :width] = sent[side * slots : (side + 1) * slots, lanes].astype(BF16)
+                both_ref[side, mine, width:] = returned[side * slots : (side + 1) * slots, lanes].astype(BF16)
+
+    def collect(step):
         for side in range(2):
-            both = jnp.concatenate(
-                [jnp.concatenate(messages[side], axis=0), jnp.concatenate(backs[side], axis=0)], axis=1
-            ).astype(BF16)
             block = step * OUT_PAIRS + side * half_blocks
             select = []
             for i in range(OUT_PAIRS):
@@ -194,10 +210,46 @@
                 select.append(jnp.where(column == mine, 1.0, 0.0).astype(BF16))
             select = jnp.concatenate(select, axis=0)
             select_ref[span(block * slots, OUT_PAIRS * slots), :] = select
-            part_ref[...] += dot_rows(select, both)
+            part_ref[...] += dot_rows(select, both_ref[side])
+
+    def stages(fourth, third, second, first):
+        if fourth is not None:
+            collect(fourth)
+        for i in range(0, OUT_PAIRS, OUT_MERGE):
+            if third is not None:
+                messages(third, i)
+            if second is not None:
+                second_layer(second, i)
+            if first is not None:
+                start_layer(first, i)
+
+    def work(step, carry):
+        arrive(step, points_in)
+        ask(step + AHEAD, points_in)
+        ask(step + 1, others_in)
+        arrive(step - 2, others_in)
+        stages(step - 3, step - 2, step - 1, step)
         return carry
 
-    lax.fori_loop(0, steps, work, 0)
+    arrive(0, points_in)
+    ask(AHEAD, points_in)
+    ask(1, others_in)
+    stages(None, None, None, 0)
+    arrive(1, points_in)
+    ask(1 + AHEAD, points_in)
+    ask(2, others_in)
+    stages(None, None, 0, 1)
+    arrive(2, points_in)
+    ask(2 + AHEAD, points_in)
+    ask(3, others_in)
+    arrive(0, others_in)
+    stages(None, 0, 1, 2)
+    lax.fori_loop(3, steps, work, 0)
+    arrive(steps - 2, others_in)
+    stages(steps - 3, steps - 2, steps - 1, None)
+    arrive(steps - 1, others_in)
+    stages(steps - 2, steps - 1, None, None)
+    stages(steps - 1, None, None, None)
     part_out_ref[...] = jnp.zeros_like(part_out_ref)
     for place in range(3):
         part_out_ref[pl.ds(place * A_PAD, A_DEV), :] = part_ref[
@@ -250,8 +302,11 @@
             pltpu.VMEM((slots, block_len), BF16),
             pltpu.VMEM((width, 2 * width), F32),
             pltpu.VMEM((steps, 2, slots, OUT_PAIRS), jnp.int32),
+            pltpu.VMEM((OUT_PAIRS * block_len, 2 * width), BF16),
+            pltpu.VMEM((OUT_PAIRS * block_len, 2 * width), BF16),
+            pltpu.VMEM((2, OUT_PAIRS * slots, 2 * width), BF16),
             pltpu.SemaphoreType.DMA((5,)),
-            pltpu.SemaphoreType.DMA((8, steps)),
+            pltpu.SemaphoreType.DMA((8, blocks // 2 // OUT_PAIRS)),
         ],
         compiler_params=pltpu.CompilerParams(vmem_limit_bytes=12 * 2**20),
         name="outgoing",
@@ -278,8 +333,10 @@
     w1_ref,
     w2_ref,
     total_ref,
-    dcoarse_ref,
-    dpre1_ref,
+    send_t_ref,
+    owner_ref,
+    spread_in_ref,
+    held1_ref,
     dpre2_ref,
     acc1_ref,
     acc2_ref,
@@ -291,7 +348,6 @@
     slots = send_ref.shape[0] // blocks
     half_blocks = blocks // 2
     steps = half_blocks // IN_PAIRS
-    rows = IN_PAIRS * block_len
 
     w1_ref[...] = diag_pair(w_first_ref[...].T * 0.5)
     w2_ref[...] = diag_pair(w_second_ref[...].T * 0.5)
@@ -305,100 +361,112 @@
     sig = jax.nn.sigmoid(pre)
     slope = sig * (1.0 + pre * (1.0 - sig))
     dpre = (total_ref[:, width:] * slope).astype(BF16)
+    edge_rows = IN_PAIRS * slots
+    for chunk in range(2 * steps):
+        send_t_ref[chunk] = send_ref[pl.ds(chunk * edge_rows, edge_rows), :].T
+    owner = lax.broadcasted_iota(jnp.int32, (edge_rows, width), 0) // slots
+    for place in range(IN_PAIRS):
+        owner_ref[place] = jnp.where(owner == place, 1.0, 0.0).astype(BF16)
     dcoarse = dot(dpre, w_coarse_ref[...].T)
     dcoarse = [dcoarse[place * A_PAD : place * A_PAD + A_DEV] for place in range(3)]
-    dcoarse.append(jnp.zeros((dcoarse_ref.shape[0] - 3 * A_DEV, width), F32))
-    dcoarse_ref[...] = jnp.concatenate(dcoarse, axis=0).astype(BF16)
+    dcoarse.append(jnp.zeros((select_ref.shape[1] - 3 * A_DEV, width), F32))
+    dcoarse = jnp.concatenate(dcoarse, axis=0).astype(BF16)
+    spread_in_ref[...] = dot(select_ref[...], dcoarse).astype(BF16)
     grads_ref[2 * width :, :] = dot_rows(coarse[A_PAD : 2 * A_PAD], dpre[A_PAD : 2 * A_PAD]).astype(
         BF16
     )
 
+    def rows(step, i, merge=IN_MERGE):
+        near, far = [
+            pl.ds(pl.multiple_of((step * IN_PAIRS + i + b) * block_len, block_len), merge * block_len)
+            for b in (0, half_blocks)
+        ]
+        return near, far, pl.ds(i * block_len, merge * block_len)
+
+    def second_grad(step, i):
+        edges = [
+            span((step * IN_PAIRS + half * half_blocks) * slots, IN_PAIRS * slots) for half in range(2)
+        ]
+        send_t = jnp.concatenate(
+            [send_t_ref[step], send_t_ref[step + half_blocks // IN_PAIRS]], axis=1
+        )
+        for p in range(i, i + IN_MERGE):
+            near, far, held = rows(step, p, 1)
+            mine = [spread_in_ref[e, :] * owner_ref[p] for e in edges]
+            zero = jnp.zeros_like(mine[0])
+            share = jnp.concatenate(
+                [jnp.concatenate([mine[0], zero], axis=1), jnp.concatenate([zero, mine[1]], axis=1)], axis=0
+            )
+            spread = dot(send_t, share).astype(BF16)
+            cot = jnp.concatenate([cot_ref[near, :], cot_ref[far, :]], axis=1)
+            dpre2_ref[held, :] = (cot + spread) * slope2_ref[near, :]
+
+    def first_grad(step, i):
+        near, _, held = rows(step, i)
+        dpre2 = dpre2_ref[held, :]
+        dpre1 = dot(dpre2, w2_ref[...]).astype(BF16) * slope1_ref[near, :]
+        held1_ref[held, :] = dpre1
+        acc2_ref[...] += dot_rows(first_ref[near, :], dpre2)
+
     def send_out(step):
         slot = lax.rem(step, 2)
+        size = IN_PAIRS * block_len
         return [
             pltpu.make_async_copy(
                 stage_ref.at[slot, half],
-                grad_feats_hbm.at[span(step * rows + half * half_blocks * block_len, rows), :],
+                grad_feats_hbm.at[span(step * size + half * half_blocks * block_len, size), :],
                 sems.at[slot, half],
             )
             for half in range(2)
         ]
 
-    def places(step):
-        pairs = [step * IN_PAIRS + i for i in range(IN_PAIRS)]
-        near = [span(p * block_len, block_len) for p in pairs]
-        far = [span((p + half_blocks) * block_len, block_len) for p in pairs]
-        held = [pl.ds(i * block_len, block_len) for i in range(IN_PAIRS)]
-        return near, far, held
-
-    def second_grad(step):
-        near, far, held = places(step)
-        edges = [
-            span((step * IN_PAIRS + half * half_blocks) * slots, IN_PAIRS * slots) for half in range(2)
-        ]
-        send_t = jnp.concatenate([send_ref[e, :] for e in edges], axis=0).T
-        spread_in = jnp.concatenate([dot(select_ref[e, :], dcoarse_ref[...]) for e in edges], axis=0)
-        owner = lax.broadcasted_iota(jnp.int32, spread_in.shape, 0) // slots
-        for p, (n, f, h) in enumerate(zip(near, far, held)):
-            share = jnp.concatenate(
-                [jnp.where(owner == b, spread_in, 0.0).astype(BF16) for b in (p, p + IN_PAIRS)], axis=1
-            )
-            spread = dot(send_t, share).astype(BF16)
-            cot = jnp.concatenate([cot_ref[n, :], cot_ref[f, :]], axis=1)
-            dpre2_ref[h, :] = (cot + spread) * slope2_ref[n, :]
-
-    def first_grad(step):
-        near, _, held = places(step)
-        for n, h in zip(near, held):
-            dfirst = dot(dpre2_ref[h, :], w2_ref[...]).astype(BF16)
-            dpre1_ref[h, :] = dfirst * slope1_ref[n, :]
-        packed = span(step * IN_PAIRS * block_len, IN_PAIRS * block_len)
-        acc2_ref[...] += dot_rows(first_ref[packed, :], dpre2_ref[...])
-
-    def feats_grad(step):
-        near, far, held = places(step)
+    def feats_grad(step, i):
+        near, far, held = rows(step, i)
+        grad = dot(held1_ref[held, :], w1_ref[...]).astype(BF16)
         slot = lax.rem(step, 2)
-        for p, h in enumerate(held):
-            grad = dot(dpre1_ref[h, :], w1_ref[...]).astype(BF16)
-            stage_ref[slot, 0, h, :] = grad[:, :width]
-            stage_ref[slot, 1, h, :] = grad[:, width:]
-        feats = [jnp.concatenate([feats_ref[n, :], feats_ref[f, :]], axis=1) for n, f in zip(near, far)]
-        acc1_ref[...] += dot_rows(jnp.concatenate(feats, axis=0), dpre1_ref[...])
+        stage_ref[slot, 0, held, :] = grad[:, :width]
+        stage_ref[slot, 1, held, :] = grad[:, width:]
+        feats = jnp.concatenate([feats_ref[near, :], feats_ref[far, :]], axis=1)
+        acc1_ref[...] += dot_rows(feats, held1_ref[held, :])
+
+    def stages(third, second, first):
+        for i in range(0, IN_PAIRS, IN_MERGE):
+            if third is not None:
+                feats_grad(third, i)
+            if second is not None:
+                first_grad(second, i)
+            if first is not None:
+                second_grad(first, i)
+
+    def await_slot(step):
+        for copy in send_out(step):
+            copy.wait()
 
     def depart(step):
         for copy in send_out(step):
             copy.start()
 
     def work(step, carry):
-        @pl.when(step >= 4)
-        def _():
-            for copy in send_out(step - 4):
-                copy.wait()
-
-        feats_grad(step - 2)
-        first_grad(step - 1)
-        second_grad(step)
+        pl.when(step >= 4)(lambda: await_slot(step - 4))
+        stages(step - 2, step - 1, step)
         depart(step - 2)
         return carry
 
-    second_grad(0)
-    first_grad(0)
-    second_grad(1)
+    stages(None, None, 0)
+    stages(None, 0, 1)
     lax.fori_loop(2, steps, work, 0)
-    for step in (steps - 2, steps - 1):
-        for copy in send_out(step - 2):
-            copy.wait()
-        feats_grad(step)
-        if step < steps - 1:
-            first_grad(step + 1)
-        depart(step)
+    await_slot(steps - 4)
+    stages(steps - 2, steps - 1, None)
+    depart(steps - 2)
+    await_slot(steps - 3)
+    stages(steps - 1, None, None)
+    depart(steps - 1)
     for place, ref in enumerate((acc1_ref, acc2_ref)):
         grads_ref[pl.ds(place * width, width), :] = (ref[:width, :width] + ref[width:, width:]).astype(
             BF16
         )
-    for step in range(steps - 2, steps):
-        for copy in send_out(step):
-            copy.wait()
+    await_slot(steps - 2)
+    await_slot(steps - 1)
 
 
 def incoming(side, w_first, w_second, w_coarse, kept, last, resident):
@@ -410,6 +478,7 @@
     weights = pltpu.VMEM((2 * width, 2 * width), BF16)
     sums = pltpu.VMEM((2 * width, 2 * width), F32)
     held = pltpu.VMEM((IN_PAIRS * block_len, 2 * width), BF16)
+    edge_rows = IN_PAIRS * (resident[2].shape[0] * block_len // points)
 
     def kernel(*refs):
         incoming_kernel(side(), *refs)
@@ -418,13 +487,15 @@
         kernel,
         in_specs=[vmem] * len(inputs),
         out_specs=[pl.BlockSpec(memory_space=pltpu.HBM), vmem],
-        out_shape=[pltpu.HBM((points, width), BF16), jax.ShapeDtypeStruct((3 * width, width), BF16)],
+        out_shape=[pltpu.HBM((points, width), BF16), pltpu.VMEM((3 * width, width), BF16)],
         scratch_shapes=[
             pltpu.VMEM((2, 2, IN_PAIRS * block_len, width), BF16),
             weights,
             weights,
             pltpu.VMEM((3 * A_PAD, 2 * width), F32),
-            pltpu.VMEM((width, width), BF16),
+            pltpu.VMEM((resident[2].shape[0] // edge_rows, block_len, edge_rows), BF16),
+            pltpu.VMEM((IN_PAIRS, edge_rows, width), BF16),
+            pltpu.VMEM((resident[2].shape[0], width), BF16),
             held,
             held,
             sums,

time: 69.5 us -> 65.9 us (0.948)
  Pallas kernels: 28.3 us -> 24.7 us
    pallas_call x1, Pallas kernels: 14.5 us -> 11.6 us  [outgoing(): pl.pallas_call(kernel, in_specs=[hbm] * len(inputs), out_specs=[vmem] * 8...]
    pallas_call x1, Pallas kernels: 13.8 us -> 13.1 us  [incoming(): pl.pallas_call(kernel, in_specs=[vmem] * len(inputs), out_specs=[pl.Block...]
where the time goes in v3:
time: 65.9 us; the launch traced here: 65.8 us
  Pallas kernels  24.7 us (37%)
  starting transfers between devices  23.8 us (36%)
  waiting for transfers between devices  15.5 us (24%)
  other arithmetic  1.03 us (2%)
  between operations  0.77 us (1%)
    ppermute x13, starting transfers between devices, flipped(): return lax.ppermute(value, 'pts', [(i, i ^ flip) for i in range(count)])  20.3 us
    ppermute x13, waiting for transfers between devices, flipped(): return lax.ppermute(value, 'pts', [(i, i ^ flip) for i in range(count)])  13.6 us
    pallas_call x1, Pallas kernels, incoming(): pl.pallas_call(kernel, in_specs=[vmem] * len(inputs), out_specs=[pl.Block...  13.1 us
    pallas_call x1, Pallas kernels, outgoing(): pl.pallas_call(kernel, in_specs=[hbm] * len(inputs), out_specs=[vmem] * 8...  11.6 us
    ppermute x1, starting transfers between devices, near_sums(): lax.ppermute(kept, 'pts', steps + [(j, i) for i, j in steps])  3.42 us
    ppermute x1, waiting for transfers between devices, near_sums(): lax.ppermute(kept, 'pts', steps + [(j, i) for i, j in steps])  1.98 us
  transfers between devices with their start and end apart: 14, of which 11 were waited for; matrix products, arithmetic and copies ran while one was open for 0% of the time, Pallas kernels for 0%

profile of v3, /device:TPU:1, one launch (start us, length us, event | category | flops | bytes accessed | tf_op | source)
XLA Modules:
  0.0 65.8 jit_solution(968432879174370976)
XLA Ops:
  0.7 11.6 %outgoing.1 = (bf16[28672,128]{1,0:T(8,128)(2,1)S(1)}, bf16[28672,128]{1,0:T(8,128)(2,1)S(1)}, bf16[1792,256]{1,0:T(8,128)(2,1)S(1)}, bf16[1792,128]{1,0:T(8,128...) custom-call(s32[112]{0:T(128)} %refs_0_.2, ...), custom_call_target="tpu_custom_call" | custom-call | tf_op jit(solution)/shard_map/outgoing/pallas_call | solution.py:278
  12.3 1.5 %collective-permute-start = (bf16[48,256]{1,0:T(8,128)(2,1)S(1)}, bf16[48,256]{1,0:T(8,128)(2,1)S(1)}, u32[]{:S(2)}, u32[]{:S(2)}) collective-permute-start(bf16[48,256]{1,0:T(8,128)(2,1)S(1)} %slice_select_fusion.2), channel_id=1, source_target_pairs={{0,1},{1,0},{2,3},{3,2},{4,5},{5,4},{6,7},{7,6},{8,9},{9,8},{10,11... | collective-permute-start | bytes 73736 | tf_op jit(solution)/shard_map/ppermute | solution.py:512
  13.8 0.8 %collective-permute-done = bf16[48,256]{1,0:T(8,128)(2,1)S(1)} collective-permute-done((bf16[48,256]{1,0:T(8,128)(2,1)S(1)}, bf16[48,256]{1,0:T(8,128)(2,1)S(1)}, u32[]{:S(2)}, u32[]{:S(2)}) %collective-permute-start) | collective-permute-done | bytes 24608 | tf_op jit(solution)/shard_map/ppermute | solution.py:512
  14.6 0.1 fusion
  14.7 3.4 %collective-permute-start.1 = (bf16[2,48,256]{2,1,0:T(8,128)(2,1)S(1)}, bf16[2,48,256]{2,1,0:T(8,128)(2,1)S(1)}, u32[]{:S(2)}, u32[]{:S(2)}) collective-permute-start(bf16[2,48,256]{2,1,0:T(8,128)(2,1)S(1)} %fusion), channel_id=1, source_target_pairs={{1,2},{3,4},{5,6},{7,8},{9,10},{11,12},{13,14},{15,16},{17,18},{19... | collective-permute-start | bytes 147464 | tf_op jit(solution)/shard_map/ppermute | solution.py:531
  18.2 2.0 %collective-permute-done.1 = bf16[2,48,256]{2,1,0:T(8,128)(2,1)S(1)} collective-permute-done((bf16[2,48,256]{2,1,0:T(8,128)(2,1)S(1)}, bf16[2,48,256]{2,1,0:T(8,128)(2,1)S(1)}, u32[]{:S(2)}, u32[]{:S(2)}) %collective-permute-start.1) | collective-permute-done | bytes 49184 | tf_op jit(solution)/shard_map/ppermute | solution.py:531
  20.1 0.1 add_convert_fusion.4
  20.2 0.1 collective-permute-start.2
  20.3 1.2 %collective-permute-done.2.refs_4_ = bf16[48,256]{1,0:T(8,128)(2,1)S(1)} collective-permute-done((bf16[48,256]{1,0:T(8,128)(2,1)S(1)}, bf16[48,256]{1,0:T(8,128)(2,1)S(1)}, u32[]{:S(2)}, u32[]{:S(2)}) %collective-permute-start.2) | collective-permute-done | bytes 24608 | tf_op jit(solution)/shard_map/ppermute | solution.py:512
  21.5 13.1 %incoming.1 = (bf16[28672,128]{1,0:T(8,128)(2,1)}, bf16[384,128]{1,0:T(8,128)(2,1)S(1)}) custom-call(bf16[128,128]{1,0:T(8,128)(2,1)S(1)} %copy-done, bf16[128,128]{1,0:T(8,128)(2,1)S(1)} %copy-done.1, bf16[128,128]{1,0:T(8,128)(2,1)S(1)} %copy-done.2, bf16[96,256]{1,0:T(8,128)(2,1)S(1)} %bitcast.8, bf16[48,256]{1,0:T(8,128)(2,1)S(1)} %collective-permute-done.2.refs_4_, ...), custom_call_target="tpu_custom_call" | custom-call | tf_op jit(solution)/shard_map/incoming/pallas_call | solution.py:486
  34.6 0.2 collective-permute-start.3
  34.9 1.1 %collective-permute-done.3 = bf16[192,128]{1,0:T(8,128)(2,1)S(1)} collective-permute-done((bf16[192,128]{1,0:T(8,128)(2,1)S(1)}, bf16[192,128]{1,0:T(8,128)(2,1)S(1)}, u32[]{:S(2)}, u32[]{:S(2)}) %collective-permute-start.3) | collective-permute-done | bytes 49184 | tf_op jit(solution)/shard_map/ppermute | solution.py:512
  36.0 2.9 %collective-permute-start.6 = (bf16[192,128]{1,0:T(8,128)(2,1)S(1)}, bf16[192,128]{1,0:T(8,128)(2,1)S(1)}, u32[]{:S(2)}, u32[]{:S(2)}) collective-permute-start(bf16[192,128]{1,0:T(8,128)(2,1)S(1)} %add_convert_fusion.3), channel_id=1, source_target_pairs={{0,4},{1,5},{2,6},{3,7},{4,0},{5,1},{6,2},{7,3},{8,12},{9,13},{10,... | collective-permute-start | bytes 147464 | tf_op jit(solution)/shard_map/ppermute | solution.py:512
  38.9 1.9 %collective-permute-start.5 = (bf16[192,128]{1,0:T(8,128)(2,1)S(1)}, bf16[192,128]{1,0:T(8,128)(2,1)S(1)}, u32[]{:S(2)}, u32[]{:S(2)}) collective-permute-start(bf16[192,128]{1,0:T(8,128)(2,1)S(1)} %add_convert_fusion.3), channel_id=1, source_target_pairs={{0,6},{1,7},{2,4},{3,5},{4,2},{5,3},{6,0},{7,1},{8,14},{9,15},{10,... | collective-permute-start | bytes 147464 | tf_op jit(solution)/shard_map/ppermute | solution.py:512
  40.8 0.5 collective-permute-start.4
  41.3 0.0 collective-permute-done.6
  41.3 1.7 %collective-permute-done.5 = bf16[192,128]{1,0:T(8,128)(2,1)S(1)} collective-permute-done((bf16[192,128]{1,0:T(8,128)(2,1)S(1)}, bf16[192,128]{1,0:T(8,128)(2,1)S(1)}, u32[]{:S(2)}, u32[]{:S(2)}) %collective-permute-start.5) | collective-permute-done | bytes 49184 | tf_op jit(solution)/shard_map/ppermute | solution.py:512
  43.0 1.2 %collective-permute-done.4 = bf16[192,128]{1,0:T(8,128)(2,1)S(1)} collective-permute-done((bf16[192,128]{1,0:T(8,128)(2,1)S(1)}, bf16[192,128]{1,0:T(8,128)(2,1)S(1)}, u32[]{:S(2)}, u32[]{:S(2)}) %collective-permute-start.4) | collective-permute-done | bytes 49184 | tf_op jit(solution)/shard_map/ppermute | solution.py:512
  44.2 3.0 %collective-permute-start.9 = (bf16[192,128]{1,0:T(8,128)(2,1)S(1)}, bf16[192,128]{1,0:T(8,128)(2,1)S(1)}, u32[]{:S(2)}, u32[]{:S(2)}) collective-permute-start(bf16[192,128]{1,0:T(8,128)(2,1)S(1)} %add_convert_fusion.2), channel_id=1, source_target_pairs={{0,16},{1,17},{2,18},{3,19},{4,20},{5,21},{6,22},{7,23},{8,24},{9,... | collective-permute-start | bytes 147464 | tf_op jit(solution)/shard_map/ppermute | solution.py:512
  47.2 1.7 %collective-permute-start.8 = (bf16[192,128]{1,0:T(8,128)(2,1)S(1)}, bf16[192,128]{1,0:T(8,128)(2,1)S(1)}, u32[]{:S(2)}, u32[]{:S(2)}) collective-permute-start(bf16[192,128]{1,0:T(8,128)(2,1)S(1)} %add_convert_fusion.2), channel_id=1, source_target_pairs={{0,24},{1,25},{2,26},{3,27},{4,28},{5,29},{6,30},{7,31},{8,16},{9,... | collective-permute-start | bytes 147464 | tf_op jit(solution)/shard_map/ppermute | solution.py:512
  49.0 0.5 collective-permute-start.7
  49.5 1.9 %collective-permute-done.8 = bf16[192,128]{1,0:T(8,128)(2,1)S(1)} collective-permute-done((bf16[192,128]{1,0:T(8,128)(2,1)S(1)}, bf16[192,128]{1,0:T(8,128)(2,1)S(1)}, u32[]{:S(2)}, u32[]{:S(2)}) %collective-permute-start.8) | collective-permute-done | bytes 49184 | tf_op jit(solution)/shard_map/ppermute | solution.py:512
  51.4 0.5 collective-permute-done.7
  51.9 3.9 %collective-permute-start.12 = (bf16[192,128]{1,0:T(8,128)(2,1)S(1)}, bf16[192,128]{1,0:T(8,128)(2,1)S(1)}, u32[]{:S(2)}, u32[]{:S(2)}) collective-permute-start(bf16[192,128]{1,0:T(8,128)(2,1)S(1)} %add_convert_fusion.1), channel_id=1, source_target_pairs={{0,64},{1,65},{2,66},{3,67},{4,68},{5,69},{6,70},{7,71},{8,72},{9,... | collective-permute-start | bytes 147464 | tf_op jit(solution)/shard_map/ppermute | solution.py:512
  55.9 0.4 collective-permute-start.11
  56.3 0.0 collective-permute-start.10
  56.3 1.0 %collective-permute-done.12 = bf16[192,128]{1,0:T(8,128)(2,1)S(1)} collective-permute-done((bf16[192,128]{1,0:T(8,128)(2,1)S(1)}, bf16[192,128]{1,0:T(8,128)(2,1)S(1)}, u32[]{:S(2)}, u32[]{:S(2)}) %collective-permute-start.12) | collective-permute-done | bytes 49184 | tf_op jit(solution)/shard_map/ppermute | solution.py:512
  57.4 3.2 %collective-permute-done.11 = bf16[192,128]{1,0:T(8,128)(2,1)S(1)} collective-permute-done((bf16[192,128]{1,0:T(8,128)(2,1)S(1)}, bf16[192,128]{1,0:T(8,128)(2,1)S(1)}, u32[]{:S(2)}, u32[]{:S(2)}) %collective-permute-start.11) | collective-permute-done | bytes 49184 | tf_op jit(solution)/shard_map/ppermute | solution.py:512
  60.6 0.0 collective-permute-done.10
  60.6 3.6 %collective-permute-start.13 = (bf16[192,128]{1,0:T(8,128)(2,1)S(1)}, bf16[192,128]{1,0:T(8,128)(2,1)S(1)}, u32[]{:S(2)}, u32[]{:S(2)}) collective-permute-start(bf16[192,128]{1,0:T(8,128)(2,1)S(1)} %add_convert_fusion), channel_id=1, source_target_pairs={{0,1},{1,0},{2,3},{3,2},{4,5},{5,4},{6,7},{7,6},{8,9},{9,8},{10,11... | collective-permute-start | bytes 147464 | tf_op jit(solution)/shard_map/ppermute | solution.py:512
  64.2 0.9 %collective-permute-done.13 = bf16[192,128]{1,0:T(8,128)(2,1)S(1)} collective-permute-done((bf16[192,128]{1,0:T(8,128)(2,1)S(1)}, bf16[192,128]{1,0:T(8,128)(2,1)S(1)}, u32[]{:S(2)}, u32[]{:S(2)}) %collective-permute-start.13) | collective-permute-done | bytes 49184 | tf_op jit(solution)/shard_map/ppermute | solution.py:512
  65.1 0.7 %slice_multiply_fusion = (f32[128,128]{1,0:T(8,128)}, f32[128,128]{1,0:T(8,128)}, f32[128,128]{1,0:T(8,128)}) fusion(f32[384,128]{1,0:T(8,128)S(1)} %maximum_convert_fusion), kind=kLoop, calls=%fused_computation.8 | loop fusion | flops 49152 | bytes 393216 | tf_op jit(solution)/shard_map/mul | solution.py:590
  (18 shorter events, 0.2 us)
Async XLA Ops:
  0.6 20.9 %copy-start = (bf16[128,128]{1,0:T(8,128)(2,1)S(1)}, bf16[128,128]{1,0:T(8,128)(2,1)}, u32[]{:S(2)}) copy-start(bf16[128,128]{1,0:T(8,128)(2,1)} %refs_0_.3) | copy-start | bytes 98308
  0.6 20.9 %copy-start.1 = (bf16[128,128]{1,0:T(8,128)(2,1)S(1)}, bf16[128,128]{1,0:T(8,128)(2,1)}, u32[]{:S(2)}) copy-start(bf16[128,128]{1,0:T(8,128)(2,1)} %refs_1_.3) | copy-start | bytes 98308
  0.7 20.9 %copy-start.2 = (bf16[128,128]{1,0:T(8,128)(2,1)S(1)}, bf16[128,128]{1,0:T(8,128)(2,1)}, u32[]{:S(2)}) copy-start(bf16[128,128]{1,0:T(8,128)(2,1)} %refs_2_.1) | copy-start | bytes 98308
  12.3 2.4 %collective-permute-start = (bf16[48,256]{1,0:T(8,128)(2,1)S(1)}, bf16[48,256]{1,0:T(8,128)(2,1)S(1)}, u32[]{:S(2)}, u32[]{:S(2)}) collective-permute-start(bf16[48,256]{1,0:T(8,128)(2,1)S(1)} %slice_select_fusion.2), channel_id=1, source_target_pairs={{0,1},{1,0},{2,3},{3,2},{4,5},{5,4},{6,7},{7,6},{8,9},{9,8},{10,11... | collective-permute-start | bytes 73736 | tf_op jit(solution)/shard_map/ppermute | solution.py:512
  14.7 5.4 %collective-permute-start.1 = (bf16[2,48,256]{2,1,0:T(8,128)(2,1)S(1)}, bf16[2,48,256]{2,1,0:T(8,128)(2,1)S(1)}, u32[]{:S(2)}, u32[]{:S(2)}) collective-permute-start(bf16[2,48,256]{2,1,0:T(8,128)(2,1)S(1)} %fusion), channel_id=1, source_target_pairs={{1,2},{3,4},{5,6},{7,8},{9,10},{11,12},{13,14},{15,16},{17,18},{19... | collective-permute-start | bytes 147464 | tf_op jit(solution)/shard_map/ppermute | solution.py:531
  20.2 1.3 %collective-permute-start.2 = (bf16[48,256]{1,0:T(8,128)(2,1)S(1)}, bf16[48,256]{1,0:T(8,128)(2,1)S(1)}, u32[]{:S(2)}, u32[]{:S(2)}) collective-permute-start(bf16[48,256]{1,0:T(8,128)(2,1)S(1)} %fusion.1), channel_id=1, source_target_pairs={{0,1},{1,0},{2,3},{3,2},{4,5},{5,4},{6,7},{7,6},{8,9},{9,8},{10,11... | collective-permute-start | bytes 73736 | tf_op jit(solution)/shard_map/ppermute | solution.py:512
  34.6 1.3 %collective-permute-start.3 = (bf16[192,128]{1,0:T(8,128)(2,1)S(1)}, bf16[192,128]{1,0:T(8,128)(2,1)S(1)}, u32[]{:S(2)}, u32[]{:S(2)}) collective-permute-start(bf16[192,128]{1,0:T(8,128)(2,1)S(1)} %broadcast_select_fusion.2), channel_id=1, source_target_pairs={{0,1},{1,0},{2,3},{3,2},{4,5},{5,4},{6,7},{7,6},{8,9},{9,8},{10,11... | collective-permute-start | bytes 147464 | tf_op jit(solution)/shard_map/ppermute | solution.py:512
  36.0 5.3 %collective-permute-start.6 = (bf16[192,128]{1,0:T(8,128)(2,1)S(1)}, bf16[192,128]{1,0:T(8,128)(2,1)S(1)}, u32[]{:S(2)}, u32[]{:S(2)}) collective-permute-start(bf16[192,128]{1,0:T(8,128)(2,1)S(1)} %add_convert_fusion.3), channel_id=1, source_target_pairs={{0,4},{1,5},{2,6},{3,7},{4,0},{5,1},{6,2},{7,3},{8,12},{9,13},{10,... | collective-permute-start | bytes 147464 | tf_op jit(solution)/shard_map/ppermute | solution.py:512
  38.9 4.2 %collective-permute-start.5 = (bf16[192,128]{1,0:T(8,128)(2,1)S(1)}, bf16[192,128]{1,0:T(8,128)(2,1)S(1)}, u32[]{:S(2)}, u32[]{:S(2)}) collective-permute-start(bf16[192,128]{1,0:T(8,128)(2,1)S(1)} %add_convert_fusion.3), channel_id=1, source_target_pairs={{0,6},{1,7},{2,4},{3,5},{4,2},{5,3},{6,0},{7,1},{8,14},{9,15},{10,... | collective-permute-start | bytes 147464 | tf_op jit(solution)/shard_map/ppermute | solution.py:512
  40.8 3.4 %collective-permute-start.4 = (bf16[192,128]{1,0:T(8,128)(2,1)S(1)}, bf16[192,128]{1,0:T(8,128)(2,1)S(1)}, u32[]{:S(2)}, u32[]{:S(2)}) collective-permute-start(bf16[192,128]{1,0:T(8,128)(2,1)S(1)} %add_convert_fusion.3), channel_id=1, source_target_pairs={{0,2},{1,3},{2,0},{3,1},{4,6},{5,7},{6,4},{7,5},{8,10},{9,11},{10,... | collective-permute-start | bytes 147464 | tf_op jit(solution)/shard_map/ppermute | solution.py:512
  44.2 5.2 %collective-permute-start.9 = (bf16[192,128]{1,0:T(8,128)(2,1)S(1)}, bf16[192,128]{1,0:T(8,128)(2,1)S(1)}, u32[]{:S(2)}, u32[]{:S(2)}) collective-permute-start(bf16[192,128]{1,0:T(8,128)(2,1)S(1)} %add_convert_fusion.2), channel_id=1, source_target_pairs={{0,16},{1,17},{2,18},{3,19},{4,20},{5,21},{6,22},{7,23},{8,24},{9,... | collective-permute-start | bytes 147464 | tf_op jit(solution)/shard_map/ppermute | solution.py:512
  47.2 4.2 %collective-permute-start.8 = (bf16[192,128]{1,0:T(8,128)(2,1)S(1)}, bf16[192,128]{1,0:T(8,128)(2,1)S(1)}, u32[]{:S(2)}, u32[]{:S(2)}) collective-permute-start(bf16[192,128]{1,0:T(8,128)(2,1)S(1)} %add_convert_fusion.2), channel_id=1, source_target_pairs={{0,24},{1,25},{2,26},{3,27},{4,28},{5,29},{6,30},{7,31},{8,16},{9,... | collective-permute-start | bytes 147464 | tf_op jit(solution)/shard_map/ppermute | solution.py:512
  49.0 2.9 %collective-permute-start.7 = (bf16[192,128]{1,0:T(8,128)(2,1)S(1)}, bf16[192,128]{1,0:T(8,128)(2,1)S(1)}, u32[]{:S(2)}, u32[]{:S(2)}) collective-permute-start(bf16[192,128]{1,0:T(8,128)(2,1)S(1)} %add_convert_fusion.2), channel_id=1, source_target_pairs={{0,8},{1,9},{2,10},{3,11},{4,12},{5,13},{6,14},{7,15},{8,0},{9,1},... | collective-permute-start | bytes 147464 | tf_op jit(solution)/shard_map/ppermute | solution.py:512
  51.9 5.4 %collective-permute-start.12 = (bf16[192,128]{1,0:T(8,128)(2,1)S(1)}, bf16[192,128]{1,0:T(8,128)(2,1)S(1)}, u32[]{:S(2)}, u32[]{:S(2)}) collective-permute-start(bf16[192,128]{1,0:T(8,128)(2,1)S(1)} %add_convert_fusion.1), channel_id=1, source_target_pairs={{0,64},{1,65},{2,66},{3,67},{4,68},{5,69},{6,70},{7,71},{8,72},{9,... | collective-permute-start | bytes 147464 | tf_op jit(solution)/shard_map/ppermute | solution.py:512
  55.9 4.7 %collective-permute-start.11 = (bf16[192,128]{1,0:T(8,128)(2,1)S(1)}, bf16[192,128]{1,0:T(8,128)(2,1)S(1)}, u32[]{:S(2)}, u32[]{:S(2)}) collective-permute-start(bf16[192,128]{1,0:T(8,128)(2,1)S(1)} %add_convert_fusion.1), channel_id=1, source_target_pairs={{0,96},{1,97},{2,98},{3,99},{4,100},{5,101},{6,102},{7,103},{8,104... | collective-permute-start | bytes 147464 | tf_op jit(solution)/shard_map/ppermute | solution.py:512
  56.3 4.2 %collective-permute-start.10 = (bf16[192,128]{1,0:T(8,128)(2,1)S(1)}, bf16[192,128]{1,0:T(8,128)(2,1)S(1)}, u32[]{:S(2)}, u32[]{:S(2)}) collective-permute-start(bf16[192,128]{1,0:T(8,128)(2,1)S(1)} %add_convert_fusion.1), channel_id=1, source_target_pairs={{0,32},{1,33},{2,34},{3,35},{4,36},{5,37},{6,38},{7,39},{8,40},{9,... | collective-permute-start | bytes 147464 | tf_op jit(solution)/shard_map/ppermute | solution.py:512
  60.6 4.5 %collective-permute-start.13 = (bf16[192,128]{1,0:T(8,128)(2,1)S(1)}, bf16[192,128]{1,0:T(8,128)(2,1)S(1)}, u32[]{:S(2)}, u32[]{:S(2)}) collective-permute-start(bf16[192,128]{1,0:T(8,128)(2,1)S(1)} %add_convert_fusion), channel_id=1, source_target_pairs={{0,1},{1,0},{2,3},{3,2},{4,5},{5,4},{6,7},{7,6},{8,9},{9,8},{10,11... | collective-permute-start | bytes 147464 | tf_op jit(solution)/shard_map/ppermute | solution.py:512

commit v4 on v3

--- a/solution.py
+++ b/solution.py
@@ -1,3 +1,4 @@
+import functools
 import math
 
 import jax
@@ -12,6 +13,8 @@
 AHEAD = 2
 OUT_PAIRS, OUT_MERGE = 8, 2
 IN_PAIRS, IN_MERGE = 8, 2
+FEATS_PARTS = (20, 18, 18)
+FEATS_GROUP = 4
 
 BF16 = jnp.bfloat16
 F32 = jnp.float32
@@ -315,7 +318,6 @@
 
 def incoming_kernel(
     side,
-    w_first_ref,
     w_second_ref,
     w_coarse_ref,
     kept_ref,
@@ -327,10 +329,8 @@
     first_ref,
     slope1_ref,
     slope2_ref,
-    grad_feats_hbm,
+    dpre1_ref,
     grads_ref,
-    stage_ref,
-    w1_ref,
     w2_ref,
     total_ref,
     send_t_ref,
@@ -340,7 +340,6 @@
     dpre2_ref,
     acc1_ref,
     acc2_ref,
-    sems,
 ):
     width = feats_ref.shape[1]
     block_len = send_ref.shape[1]
@@ -349,7 +348,6 @@
     half_blocks = blocks // 2
     steps = half_blocks // IN_PAIRS
 
-    w1_ref[...] = diag_pair(w_first_ref[...].T * 0.5)
     w2_ref[...] = diag_pair(w_second_ref[...].T * 0.5)
     acc1_ref[...] = jnp.zeros_like(acc1_ref)
     acc2_ref[...] = jnp.zeros_like(acc2_ref)
@@ -405,76 +403,45 @@
         near, _, held = rows(step, i)
         dpre2 = dpre2_ref[held, :]
         dpre1 = dot(dpre2, w2_ref[...]).astype(BF16) * slope1_ref[near, :]
+        dpre1_ref[near, :] = dpre1
         held1_ref[held, :] = dpre1
         acc2_ref[...] += dot_rows(first_ref[near, :], dpre2)
 
-    def send_out(step):
-        slot = lax.rem(step, 2)
-        size = IN_PAIRS * block_len
-        return [
-            pltpu.make_async_copy(
-                stage_ref.at[slot, half],
-                grad_feats_hbm.at[span(step * size + half * half_blocks * block_len, size), :],
-                sems.at[slot, half],
-            )
-            for half in range(2)
-        ]
-
-    def feats_grad(step, i):
+    def feats_sum(step, i):
         near, far, held = rows(step, i)
-        grad = dot(held1_ref[held, :], w1_ref[...]).astype(BF16)
-        slot = lax.rem(step, 2)
-        stage_ref[slot, 0, held, :] = grad[:, :width]
-        stage_ref[slot, 1, held, :] = grad[:, width:]
         feats = jnp.concatenate([feats_ref[near, :], feats_ref[far, :]], axis=1)
         acc1_ref[...] += dot_rows(feats, held1_ref[held, :])
 
     def stages(third, second, first):
         for i in range(0, IN_PAIRS, IN_MERGE):
             if third is not None:
-                feats_grad(third, i)
+                feats_sum(third, i)
             if second is not None:
                 first_grad(second, i)
             if first is not None:
                 second_grad(first, i)
 
-    def await_slot(step):
-        for copy in send_out(step):
-            copy.wait()
-
-    def depart(step):
-        for copy in send_out(step):
-            copy.start()
-
     def work(step, carry):
-        pl.when(step >= 4)(lambda: await_slot(step - 4))
         stages(step - 2, step - 1, step)
-        depart(step - 2)
         return carry
 
     stages(None, None, 0)
     stages(None, 0, 1)
     lax.fori_loop(2, steps, work, 0)
-    await_slot(steps - 4)
     stages(steps - 2, steps - 1, None)
-    depart(steps - 2)
-    await_slot(steps - 3)
     stages(steps - 1, None, None)
-    depart(steps - 1)
     for place, ref in enumerate((acc1_ref, acc2_ref)):
         grads_ref[pl.ds(place * width, width), :] = (ref[:width, :width] + ref[width:, width:]).astype(
             BF16
         )
-    await_slot(steps - 2)
-    await_slot(steps - 1)
-
-
-def incoming(side, w_first, w_second, w_coarse, kept, last, resident):
+
+
+def incoming(side, w_second, w_coarse, kept, last, resident):
     points, width = resident[0].shape
     block_len = resident[2].shape[1]
     vmem = pl.BlockSpec(memory_space=pltpu.VMEM)
     resident = [pltpu.with_memory_space_constraint(value, pltpu.VMEM) for value in resident]
-    inputs = (w_first, w_second, w_coarse, kept, last, *resident)
+    inputs = (w_second, w_coarse, kept, last, *resident)
     weights = pltpu.VMEM((2 * width, 2 * width), BF16)
     sums = pltpu.VMEM((2 * width, 2 * width), F32)
     held = pltpu.VMEM((IN_PAIRS * block_len, 2 * width), BF16)
@@ -486,11 +453,10 @@
     return pl.pallas_call(
         kernel,
         in_specs=[vmem] * len(inputs),
-        out_specs=[pl.BlockSpec(memory_space=pltpu.HBM), vmem],
-        out_shape=[pltpu.HBM((points, width), BF16), pltpu.VMEM((3 * width, width), BF16)],
+        out_specs=[vmem, vmem],
+        out_shape=[pltpu.VMEM((points // 2, 2 * width), BF16), pltpu.VMEM((3 * width, width), BF16)],
+        input_output_aliases={9: 0},
         scratch_shapes=[
-            pltpu.VMEM((2, 2, IN_PAIRS * block_len, width), BF16),
-            weights,
             weights,
             pltpu.VMEM((3 * A_PAD, 2 * width), F32),
             pltpu.VMEM((resident[2].shape[0] // edge_rows, block_len, edge_rows), BF16),
@@ -500,16 +466,74 @@
             held,
             sums,
             sums,
-            pltpu.SemaphoreType.DMA((2, 2)),
         ],
         compiler_params=pltpu.CompilerParams(vmem_limit_bytes=12 * 2**20),
         name="incoming",
     )(*inputs)
 
 
+def feats_grad_kernel(first, block_len, dpre1_ref, w_first_ref, *refs):
+    grad_feats_hbm, stage_ref, w1_ref, sems = refs[-4:]
+    width = w_first_ref.shape[0]
+    half_rows = dpre1_ref.shape[0]
+    rows = stage_ref.shape[1]
+    w1_ref[...] = diag_pair(w_first_ref[...].T * 0.5)
+    group = FEATS_GROUP * block_len
+    copies = []
+    for place, start in enumerate(range(0, rows, group)):
+        size = min(group, rows - start)
+        grad = dot(dpre1_ref[pl.ds(first + start, size), :], w1_ref[...]).astype(BF16)
+        for half in range(2):
+            stage_ref[half, pl.ds(start, size), :] = grad[:, half * width : (half + 1) * width]
+            copies.append(
+                pltpu.make_async_copy(
+                    stage_ref.at[half, pl.ds(start, size), :],
+                    grad_feats_hbm.at[pl.ds(half * half_rows + first + start, size), :],
+                    sems.at[half, place],
+                )
+            )
+            copies[-1].start()
+    for copy in copies:
+        copy.wait()
+
+
+def feats_grad(first, pairs, block_len, dpre1, w_first, grad_feats):
+    width = w_first.shape[0]
+    half_rows = dpre1.shape[0]
+    rows = pairs * block_len
+    vmem = pl.BlockSpec(memory_space=pltpu.VMEM)
+    hbm = pl.BlockSpec(memory_space=pltpu.HBM)
+    inputs = [pltpu.with_memory_space_constraint(dpre1, pltpu.VMEM), w_first]
+    if grad_feats is not None:
+        inputs.append(pltpu.with_memory_space_constraint(grad_feats, pltpu.HBM))
+    return pl.pallas_call(
+        functools.partial(feats_grad_kernel, first * block_len, block_len),
+        in_specs=[vmem, vmem, hbm][: len(inputs)],
+        out_specs=hbm,
+        out_shape=pltpu.HBM((2 * half_rows, width), BF16),
+        input_output_aliases={} if grad_feats is None else {2: 0},
+        scratch_shapes=[
+            pltpu.VMEM((2, rows, width), BF16),
+            pltpu.VMEM((2 * width, 2 * width), BF16),
+            pltpu.SemaphoreType.DMA((2, pl.cdiv(pairs, FEATS_GROUP))),
+        ],
+        compiler_params=pltpu.CompilerParams(vmem_limit_bytes=12 * 2**20),
+        cost_estimate=pl.CostEstimate(
+            flops=4 * rows * width * width, bytes_accessed=4 * rows * width * 2, transcendentals=0
+        ),
+        name="feats_grad",
+    )(*inputs)
+
+
 def flipped(value, flip):
     count = lax.axis_size("pts")
     return lax.ppermute(value, "pts", [(i, i ^ flip) for i in range(count)])
+
+
+def turned(value, place, by):
+    count = lax.axis_size("pts")
+    targets = [(i & ~(3 << place)) | (((i >> place) + by & 3) << place) for i in range(count)]
+    return lax.ppermute(value, "pts", list(enumerate(targets)))
 
 
 def added(*values):
@@ -533,17 +557,21 @@
     return kept.reshape(2 * A_PAD, -1), last
 
 
-def device_sum(value):
+def device_sum(value, beside):
     count = lax.axis_size("pts")
     odd = lax.rem(lax.axis_index("pts"), 2) == 1
     low, high = jnp.split(value, 2, axis=0)
     part = added(jnp.where(odd, high, low), flipped(jnp.where(odd, low, high), 1))
     place = 1
     while 2 << place <= count:
-        part = added(part, *(flipped(part, k << place) for k in (1, 3, 2)))
+        part, result = beside(part)
+        one, three, two = [turned(part, place, k) for k in (1, 3, 2)]
+        total = (part.astype(F32) + two.astype(F32)) + (one.astype(F32) + three.astype(F32))
+        part = total.astype(BF16)
+        part, result = lax.optimization_barrier((part, result))
         place += 2
     other = flipped(part, 1)
-    return jnp.concatenate([jnp.where(odd, other, part), jnp.where(odd, part, other)], axis=0)
+    return jnp.concatenate([jnp.where(odd, other, part), jnp.where(odd, part, other)], axis=0), result
 
 
 def body(
@@ -576,10 +604,23 @@
         w_second,
     )
     kept, last = near_sums(part)
-    grad_feats, grads = incoming(
-        lambda: lax.rem(lax.axis_index("pts"), 2), w_first, w_second, w_coarse, kept, last, resident
+    dpre1, grads = incoming(
+        lambda: lax.rem(lax.axis_index("pts"), 2), w_second, w_coarse, kept, last, resident
     )
-    grads = device_sum(grads).astype(F32)
+    grad_feats = None
+    done = 0
+    left = list(FEATS_PARTS)
+
+    def beside(part):
+        nonlocal grad_feats, done
+        held, part = lax.optimization_barrier((dpre1, part))
+        size = left.pop(0)
+        grad_feats = feats_grad(done, size, block_len, held, w_first, grad_feats)
+        done += size
+        return part, grad_feats
+
+    grads, grad_feats = device_sum(grads, beside)
+    grads = grads.astype(F32)
     total_points = devices * num_blocks * block_len
     total_atoms = devices * A_DEV
     factor = 0.5 / math.sqrt(total_points)

time: 65.9 us -> 66.6 us (1.011)
  waiting for transfers between devices: 15.5 us -> 9.43 us
  Pallas kernels: 24.7 us -> 28.5 us
  starting transfers between devices: 23.8 us -> 26.6 us
    ppermute x0 -> x9, starting transfers between devices: none -> 17.3 us  [turned(): return lax.ppermute(value, 'pts', list(enumerate(targets)))]
    ppermute x13 -> x4, starting transfers between devices: 20.3 us -> 5.84 us  [flipped(): return lax.ppermute(value, 'pts', [(i, i ^ flip) for i in range(count)])]
    ppermute x13 -> x4, waiting for transfers between devices: 13.6 us -> 3.94 us  [flipped(): return lax.ppermute(value, 'pts', [(i, i ^ flip) for i in range(count)])]
    pallas_call x1 -> x4, Pallas kernels: 13.1 us -> 17 us  [the longest x1 11.1 us: incoming(): pl.pallas_call(kernel, in_specs=[vmem] * len(inputs), out_specs=[vmem, vm...]
    ppermute x0 -> x9, waiting for transfers between devices: none -> 3.53 us  [turned(): return lax.ppermute(value, 'pts', list(enumerate(targets)))]
  transfers between devices with their start and end apart: 14 -> 14, of which waited for: 11 -> 8; matrix products, arithmetic and copies ran while one was open for 0% -> 0% of each run, Pallas kernels for 0% -> 9%
where the time goes in v4:
time: 66.6 us; the launch traced here: 66.4 us
  Pallas kernels  28.5 us (43%)
  starting transfers between devices  26.6 us (40%)
  waiting for transfers between devices  9.43 us (14%)
  other arithmetic  1.03 us (2%)
  between operations  0.82 us (1%)
    ppermute x9, starting transfers between devices, turned(): return lax.ppermute(value, 'pts', list(enumerate(targets)))  17.3 us
    pallas_call x1, Pallas kernels, outgoing(): pl.pallas_call(kernel, in_specs=[hbm] * len(inputs), out_specs=[vmem] * 8...  11.5 us
    pallas_call x1, Pallas kernels, incoming(): pl.pallas_call(kernel, in_specs=[vmem] * len(inputs), out_specs=[vmem, vm...  11.1 us
    pallas_call x3, Pallas kernels, feats_grad(): pl.pallas_call(functools.partial(feats_grad_kernel, first * block_len, bl...  5.91 us
    ppermute x4, starting transfers between devices, flipped(): return lax.ppermute(value, 'pts', [(i, i ^ flip) for i in range(count)])  5.84 us
    ppermute x4, waiting for transfers between devices, flipped(): return lax.ppermute(value, 'pts', [(i, i ^ flip) for i in range(count)])  3.94 us
    ppermute x9, waiting for transfers between devices, turned(): return lax.ppermute(value, 'pts', list(enumerate(targets)))  3.53 us
    ppermute x1, starting transfers between devices, near_sums(): lax.ppermute(kept, 'pts', steps + [(j, i) for i, j in steps])  3.44 us
  transfers between devices with their start and end apart: 14, of which 8 were waited for; matrix products, arithmetic and copies ran while one was open for 0% of the time, Pallas kernels for 9%

profile of v4, /device:TPU:1, one launch (start us, length us, event | category | flops | bytes accessed | tf_op | source)
XLA Modules:
  0.0 66.4 jit_solution(3784045371272694503)
XLA Ops:
  0.7 11.5 %outgoing.1 = (bf16[28672,128]{1,0:T(8,128)(2,1)S(1)}, bf16[28672,128]{1,0:T(8,128)(2,1)S(1)}, bf16[1792,256]{1,0:T(8,128)(2,1)S(1)}, bf16[1792,128]{1,0:T(8,128...) custom-call(s32[112]{0:T(128)} %refs_0_.2, ...), custom_call_target="tpu_custom_call" | custom-call | tf_op jit(solution)/shard_map/outgoing/pallas_call | solution.py:281
  12.2 1.5 %collective-permute-start = (bf16[48,256]{1,0:T(8,128)(2,1)S(1)}, bf16[48,256]{1,0:T(8,128)(2,1)S(1)}, u32[]{:S(2)}, u32[]{:S(2)}) collective-permute-start(bf16[48,256]{1,0:T(8,128)(2,1)S(1)} %slice_select_fusion.2), channel_id=1, source_target_pairs={{0,1},{1,0},{2,3},{3,2},{4,5},{5,4},{6,7},{7,6},{8,9},{9,8},{10,11... | collective-permute-start | bytes 73736 | tf_op jit(solution)/shard_map/ppermute | solution.py:530
  13.7 0.8 %collective-permute-done = bf16[48,256]{1,0:T(8,128)(2,1)S(1)} collective-permute-done((bf16[48,256]{1,0:T(8,128)(2,1)S(1)}, bf16[48,256]{1,0:T(8,128)(2,1)S(1)}, u32[]{:S(2)}, u32[]{:S(2)}) %collective-permute-start) | collective-permute-done | bytes 24608 | tf_op jit(solution)/shard_map/ppermute | solution.py:530
  14.5 0.1 fusion
  14.6 3.4 %collective-permute-start.1 = (bf16[2,48,256]{2,1,0:T(8,128)(2,1)S(1)}, bf16[2,48,256]{2,1,0:T(8,128)(2,1)S(1)}, u32[]{:S(2)}, u32[]{:S(2)}) collective-permute-start(bf16[2,48,256]{2,1,0:T(8,128)(2,1)S(1)} %fusion), channel_id=1, source_target_pairs={{1,2},{3,4},{5,6},{7,8},{9,10},{11,12},{13,14},{15,16},{17,18},{19... | collective-permute-start | bytes 147464 | tf_op jit(solution)/shard_map/ppermute | solution.py:555
  18.1 2.0 %collective-permute-done.1 = bf16[2,48,256]{2,1,0:T(8,128)(2,1)S(1)} collective-permute-done((bf16[2,48,256]{2,1,0:T(8,128)(2,1)S(1)}, bf16[2,48,256]{2,1,0:T(8,128)(2,1)S(1)}, u32[]{:S(2)}, u32[]{:S(2)}) %collective-permute-start.1) | collective-permute-done | bytes 49184 | tf_op jit(solution)/shard_map/ppermute | solution.py:555
  20.0 0.1 add_convert_fusion.4
  20.1 0.1 collective-permute-start.2
  20.2 1.2 %collective-permute-done.2.refs_3_ = bf16[48,256]{1,0:T(8,128)(2,1)S(1)} collective-permute-done((bf16[48,256]{1,0:T(8,128)(2,1)S(1)}, bf16[48,256]{1,0:T(8,128)(2,1)S(1)}, u32[]{:S(2)}, u32[]{:S(2)}) %collective-permute-start.2) | collective-permute-done | bytes 24608 | tf_op jit(solution)/shard_map/ppermute | solution.py:530
  21.4 11.1 %incoming.1 = (bf16[14336,256]{1,0:T(8,128)(2,1)S(1)}, bf16[384,128]{1,0:T(8,128)(2,1)S(1)}) custom-call(bf16[128,128]{1,0:T(8,128)(2,1)S(1)} %copy-done.1, bf16[128,128]{1,0:T(8,128)(2,1)S(1)} %copy-done.2, bf16[96,256]{1,0:T(8,128)(2,1)S(1)} %bitcast.8, bf16[48,256]{1,0:T(8,128)(2,1)S(1)} %collective-permute-done.2.refs_3_, ...), custom_call_target="tpu_custom_call", output_to_operand_aliasing={{0}: (9, {})} | custom-call | tf_op jit(solution)/shard_map/incoming/pallas_call | solution.py:453
  32.5 0.3 collective-permute-start.3
  32.8 1.1 %collective-permute-done.3 = bf16[192,128]{1,0:T(8,128)(2,1)S(1)} collective-permute-done((bf16[192,128]{1,0:T(8,128)(2,1)S(1)}, bf16[192,128]{1,0:T(8,128)(2,1)S(1)}, u32[]{:S(2)}, u32[]{:S(2)}) %collective-permute-start.3) | collective-permute-done | bytes 49184 | tf_op jit(solution)/shard_map/ppermute | solution.py:530
  33.9 4.8 %collective-permute-start.6 = (bf16[192,128]{1,0:T(8,128)(2,1)S(1)}, bf16[192,128]{1,0:T(8,128)(2,1)S(1)}, u32[]{:S(2)}, u32[]{:S(2)}) collective-permute-start(bf16[192,128]{1,0:T(8,128)(2,1)S(1)} %add_convert_fusion.3), channel_id=1, source_target_pairs={{0,6},{1,7},{2,0},{3,1},{4,2},{5,3},{6,4},{7,5},{8,14},{9,15},{10,... | collective-permute-start | bytes 147464 | tf_op jit(solution)/shard_map/ppermute | solution.py:536
  38.6 0.0 collective-permute-start.5
  38.6 1.3 %collective-permute-start.4 = (bf16[192,128]{1,0:T(8,128)(2,1)S(1)}, bf16[192,128]{1,0:T(8,128)(2,1)S(1)}, u32[]{:S(2)}, u32[]{:S(2)}) collective-permute-start(bf16[192,128]{1,0:T(8,128)(2,1)S(1)} %add_convert_fusion.3), channel_id=1, source_target_pairs={{0,4},{1,5},{2,6},{3,7},{4,0},{5,1},{6,2},{7,3},{8,12},{9,13},{10,... | collective-permute-start | bytes 147464 | tf_op jit(solution)/shard_map/ppermute | solution.py:536
  39.9 2.1 %feats_grad.3.refs_0_ = bf16[28672,128]{1,0:T(8,128)(2,1)} custom-call(bf16[14336,256]{1,0:T(8,128)(2,1)S(1)} %get-tuple-element.41.dpre1_ref, bf16[128,128]{1,0:T(8,128)(2,1)S(1)} %copy-done), custom_call_target="tpu_custom_call" | custom-call | flops 335544320 | bytes 5242880 | tf_op jit(solution)/shard_map/feats_grad/pallas_call | solution.py:509
  42.0 1.8 %collective-permute-done.5 = bf16[192,128]{1,0:T(8,128)(2,1)S(1)} collective-permute-done((bf16[192,128]{1,0:T(8,128)(2,1)S(1)}, bf16[192,128]{1,0:T(8,128)(2,1)S(1)}, u32[]{:S(2)}, u32[]{:S(2)}) %collective-permute-start.5) | collective-permute-done | bytes 49184 | tf_op jit(solution)/shard_map/ppermute | solution.py:536
  43.8 4.9 %collective-permute-start.9 = (bf16[192,128]{1,0:T(8,128)(2,1)S(1)}, bf16[192,128]{1,0:T(8,128)(2,1)S(1)}, u32[]{:S(2)}, u32[]{:S(2)}) collective-permute-start(bf16[192,128]{1,0:T(8,128)(2,1)S(1)} %add_convert_fusion.2), channel_id=1, source_target_pairs={{0,24},{1,25},{2,26},{3,27},{4,28},{5,29},{6,30},{7,31},{8,0},{9,1... | collective-permute-start | bytes 147464 | tf_op jit(solution)/shard_map/ppermute | solution.py:536
  48.7 0.0 collective-permute-start.8
  48.7 1.3 %collective-permute-start.7 = (bf16[192,128]{1,0:T(8,128)(2,1)S(1)}, bf16[192,128]{1,0:T(8,128)(2,1)S(1)}, u32[]{:S(2)}, u32[]{:S(2)}) collective-permute-start(bf16[192,128]{1,0:T(8,128)(2,1)S(1)} %add_convert_fusion.2), channel_id=1, source_target_pairs={{0,16},{1,17},{2,18},{3,19},{4,20},{5,21},{6,22},{7,23},{8,24},{9,... | collective-permute-start | bytes 147464 | tf_op jit(solution)/shard_map/ppermute | solution.py:536
  49.9 1.9 %feats_grad.4.refs_0_ = bf16[28672,128]{1,0:T(8,128)(2,1)} custom-call(bf16[14336,256]{1,0:T(8,128)(2,1)S(1)} %get-tuple-element.41.dpre1_ref, bf16[128,128]{1,0:T(8,128)(2,1)S(1)} %copy-done, bf16[28672,128]{1,0:T(8,128)(2,1)} %feats_grad.3.refs_0_), custom_call_target="tpu_custom_call", output_to_operand_aliasing={{}: (2, {})} | custom-call | flops 301989888 | bytes 4718592 | tf_op jit(solution)/shard_map/feats_grad/pallas_call | solution.py:509
  51.9 0.0 collective-permute-done.9
  51.9 1.2 %collective-permute-done.8 = bf16[192,128]{1,0:T(8,128)(2,1)S(1)} collective-permute-done((bf16[192,128]{1,0:T(8,128)(2,1)S(1)}, bf16[192,128]{1,0:T(8,128)(2,1)S(1)}, u32[]{:S(2)}, u32[]{:S(2)}) %collective-permute-start.8) | collective-permute-done | bytes 49184 | tf_op jit(solution)/shard_map/ppermute | solution.py:536
  53.1 0.5 collective-permute-done.7
  53.6 0.5 collective-permute-start.12
  54.1 1.3 %collective-permute-start.11 = (bf16[192,128]{1,0:T(8,128)(2,1)S(1)}, bf16[192,128]{1,0:T(8,128)(2,1)S(1)}, u32[]{:S(2)}, u32[]{:S(2)}) collective-permute-start(bf16[192,128]{1,0:T(8,128)(2,1)S(1)} %add_convert_fusion.1), channel_id=1, source_target_pairs={{0,32},{1,33},{2,34},{3,35},{4,36},{5,37},{6,38},{7,39},{8,40},{9,... | collective-permute-start | bytes 147464 | tf_op jit(solution)/shard_map/ppermute | solution.py:536
  55.4 3.4 %collective-permute-start.10 = (bf16[192,128]{1,0:T(8,128)(2,1)S(1)}, bf16[192,128]{1,0:T(8,128)(2,1)S(1)}, u32[]{:S(2)}, u32[]{:S(2)}) collective-permute-start(bf16[192,128]{1,0:T(8,128)(2,1)S(1)} %add_convert_fusion.1), channel_id=1, source_target_pairs={{0,64},{1,65},{2,66},{3,67},{4,68},{5,69},{6,70},{7,71},{8,72},{9,... | collective-permute-start | bytes 147464 | tf_op jit(solution)/shard_map/ppermute | solution.py:536
  58.8 1.9 %feats_grad.5 = bf16[28672,128]{1,0:T(8,128)(2,1)} custom-call(bf16[14336,256]{1,0:T(8,128)(2,1)S(1)} %get-tuple-element.41.dpre1_ref, bf16[128,128]{1,0:T(8,128)(2,1)S(1)} %copy-done, bf16[28672,128]{1,0:T(8,128)(2,1)} %feats_grad.4.refs_0_), custom_call_target="tpu_custom_call", output_to_operand_aliasing={{}: (2, {})} | custom-call | flops 301989888 | bytes 4718592 | tf_op jit(solution)/shard_map/feats_grad/pallas_call | solution.py:509
  60.7 0.0 collective-permute-done.10
  60.8 4.0 %collective-permute-start.13 = (bf16[192,128]{1,0:T(8,128)(2,1)S(1)}, bf16[192,128]{1,0:T(8,128)(2,1)S(1)}, u32[]{:S(2)}, u32[]{:S(2)}) collective-permute-start(bf16[192,128]{1,0:T(8,128)(2,1)S(1)} %add_convert_fusion), channel_id=1, source_target_pairs={{0,1},{1,0},{2,3},{3,2},{4,5},{5,4},{6,7},{7,6},{8,9},{9,8},{10,11... | collective-permute-start | bytes 147464 | tf_op jit(solution)/shard_map/ppermute | solution.py:530
  64.8 0.9 %collective-permute-done.13 = bf16[192,128]{1,0:T(8,128)(2,1)S(1)} collective-permute-done((bf16[192,128]{1,0:T(8,128)(2,1)S(1)}, bf16[192,128]{1,0:T(8,128)(2,1)S(1)}, u32[]{:S(2)}, u32[]{:S(2)}) %collective-permute-start.13) | collective-permute-done | bytes 49184 | tf_op jit(solution)/shard_map/ppermute | solution.py:530
  65.7 0.7 %slice_multiply_fusion = (f32[128,128]{1,0:T(8,128)}, f32[128,128]{1,0:T(8,128)}, f32[128,128]{1,0:T(8,128)}) fusion(f32[384,128]{1,0:T(8,128)S(1)} %maximum_convert_fusion), kind=kLoop, calls=%fused_computation.8 | loop fusion | flops 49152 | bytes 393216 | tf_op jit(solution)/shard_map/mul | solution.py:631
  (21 shorter events, 0.2 us)
Async XLA Ops:
  0.6 20.8 %copy-start.1 = (bf16[128,128]{1,0:T(8,128)(2,1)S(1)}, bf16[128,128]{1,0:T(8,128)(2,1)}, u32[]{:S(2)}) copy-start(bf16[128,128]{1,0:T(8,128)(2,1)} %refs_0_.3) | copy-start | bytes 98308
  0.6 20.8 %copy-start.2 = (bf16[128,128]{1,0:T(8,128)(2,1)S(1)}, bf16[128,128]{1,0:T(8,128)(2,1)}, u32[]{:S(2)}) copy-start(bf16[128,128]{1,0:T(8,128)(2,1)} %refs_1_.3) | copy-start | bytes 98308
  12.2 2.3 %collective-permute-start = (bf16[48,256]{1,0:T(8,128)(2,1)S(1)}, bf16[48,256]{1,0:T(8,128)(2,1)S(1)}, u32[]{:S(2)}, u32[]{:S(2)}) collective-permute-start(bf16[48,256]{1,0:T(8,128)(2,1)S(1)} %slice_select_fusion.2), channel_id=1, source_target_pairs={{0,1},{1,0},{2,3},{3,2},{4,5},{5,4},{6,7},{7,6},{8,9},{9,8},{10,11... | collective-permute-start | bytes 73736 | tf_op jit(solution)/shard_map/ppermute | solution.py:530
  14.6 5.4 %collective-permute-start.1 = (bf16[2,48,256]{2,1,0:T(8,128)(2,1)S(1)}, bf16[2,48,256]{2,1,0:T(8,128)(2,1)S(1)}, u32[]{:S(2)}, u32[]{:S(2)}) collective-permute-start(bf16[2,48,256]{2,1,0:T(8,128)(2,1)S(1)} %fusion), channel_id=1, source_target_pairs={{1,2},{3,4},{5,6},{7,8},{9,10},{11,12},{13,14},{15,16},{17,18},{19... | collective-permute-start | bytes 147464 | tf_op jit(solution)/shard_map/ppermute | solution.py:555
  20.1 1.3 %collective-permute-start.2 = (bf16[48,256]{1,0:T(8,128)(2,1)S(1)}, bf16[48,256]{1,0:T(8,128)(2,1)S(1)}, u32[]{:S(2)}, u32[]{:S(2)}) collective-permute-start(bf16[48,256]{1,0:T(8,128)(2,1)S(1)} %fusion.1), channel_id=1, source_target_pairs={{0,1},{1,0},{2,3},{3,2},{4,5},{5,4},{6,7},{7,6},{8,9},{9,8},{10,11... | collective-permute-start | bytes 73736 | tf_op jit(solution)/shard_map/ppermute | solution.py:530
  21.4 18.5 %copy-start = (bf16[128,128]{1,0:T(8,128)(2,1)S(1)}, bf16[128,128]{1,0:T(8,128)(2,1)}, u32[]{:S(2)}) copy-start(bf16[128,128]{1,0:T(8,128)(2,1)} %w_first_ref.5) | copy-start | bytes 98308
  32.5 1.3 %collective-permute-start.3 = (bf16[192,128]{1,0:T(8,128)(2,1)S(1)}, bf16[192,128]{1,0:T(8,128)(2,1)S(1)}, u32[]{:S(2)}, u32[]{:S(2)}) collective-permute-start(bf16[192,128]{1,0:T(8,128)(2,1)S(1)} %broadcast_select_fusion.2), channel_id=1, source_target_pairs={{0,1},{1,0},{2,3},{3,2},{4,5},{5,4},{6,7},{7,6},{8,9},{9,8},{10,11... | collective-permute-start | bytes 147464 | tf_op jit(solution)/shard_map/ppermute | solution.py:530
  33.9 8.1 %collective-permute-start.6 = (bf16[192,128]{1,0:T(8,128)(2,1)S(1)}, bf16[192,128]{1,0:T(8,128)(2,1)S(1)}, u32[]{:S(2)}, u32[]{:S(2)}) collective-permute-start(bf16[192,128]{1,0:T(8,128)(2,1)S(1)} %add_convert_fusion.3), channel_id=1, source_target_pairs={{0,6},{1,7},{2,0},{3,1},{4,2},{5,3},{6,4},{7,5},{8,14},{9,15},{10,... | collective-permute-start | bytes 147464 | tf_op jit(solution)/shard_map/ppermute | solution.py:536
  38.6 5.1 %collective-permute-start.5 = (bf16[192,128]{1,0:T(8,128)(2,1)S(1)}, bf16[192,128]{1,0:T(8,128)(2,1)S(1)}, u32[]{:S(2)}, u32[]{:S(2)}) collective-permute-start(bf16[192,128]{1,0:T(8,128)(2,1)S(1)} %add_convert_fusion.3), channel_id=1, source_target_pairs={{0,2},{1,3},{2,4},{3,5},{4,6},{5,7},{6,0},{7,1},{8,10},{9,11},{10,... | collective-permute-start | bytes 147464 | tf_op jit(solution)/shard_map/ppermute | solution.py:536
  38.6 5.1 %collective-permute-start.4 = (bf16[192,128]{1,0:T(8,128)(2,1)S(1)}, bf16[192,128]{1,0:T(8,128)(2,1)S(1)}, u32[]{:S(2)}, u32[]{:S(2)}) collective-permute-start(bf16[192,128]{1,0:T(8,128)(2,1)S(1)} %add_convert_fusion.3), channel_id=1, source_target_pairs={{0,4},{1,5},{2,6},{3,7},{4,0},{5,1},{6,2},{7,3},{8,12},{9,13},{10,... | collective-permute-start | bytes 147464 | tf_op jit(solution)/shard_map/ppermute | solution.py:536
  43.8 8.1 %collective-permute-start.9 = (bf16[192,128]{1,0:T(8,128)(2,1)S(1)}, bf16[192,128]{1,0:T(8,128)(2,1)S(1)}, u32[]{:S(2)}, u32[]{:S(2)}) collective-permute-start(bf16[192,128]{1,0:T(8,128)(2,1)S(1)} %add_convert_fusion.2), channel_id=1, source_target_pairs={{0,24},{1,25},{2,26},{3,27},{4,28},{5,29},{6,30},{7,31},{8,0},{9,1... | collective-permute-start | bytes 147464 | tf_op jit(solution)/shard_map/ppermute | solution.py:536
  48.7 4.4 %collective-permute-start.8 = (bf16[192,128]{1,0:T(8,128)(2,1)S(1)}, bf16[192,128]{1,0:T(8,128)(2,1)S(1)}, u32[]{:S(2)}, u32[]{:S(2)}) collective-permute-start(bf16[192,128]{1,0:T(8,128)(2,1)S(1)} %add_convert_fusion.2), channel_id=1, source_target_pairs={{0,8},{1,9},{2,10},{3,11},{4,12},{5,13},{6,14},{7,15},{8,16},{9,17... | collective-permute-start | bytes 147464 | tf_op jit(solution)/shard_map/ppermute | solution.py:536
  48.7 4.9 %collective-permute-start.7 = (bf16[192,128]{1,0:T(8,128)(2,1)S(1)}, bf16[192,128]{1,0:T(8,128)(2,1)S(1)}, u32[]{:S(2)}, u32[]{:S(2)}) collective-permute-start(bf16[192,128]{1,0:T(8,128)(2,1)S(1)} %add_convert_fusion.2), channel_id=1, source_target_pairs={{0,16},{1,17},{2,18},{3,19},{4,20},{5,21},{6,22},{7,23},{8,24},{9,... | collective-permute-start | bytes 147464 | tf_op jit(solution)/shard_map/ppermute | solution.py:536
  53.6 7.1 %collective-permute-start.12 = (bf16[192,128]{1,0:T(8,128)(2,1)S(1)}, bf16[192,128]{1,0:T(8,128)(2,1)S(1)}, u32[]{:S(2)}, u32[]{:S(2)}) collective-permute-start(bf16[192,128]{1,0:T(8,128)(2,1)S(1)} %add_convert_fusion.1), channel_id=1, source_target_pairs={{0,96},{1,97},{2,98},{3,99},{4,100},{5,101},{6,102},{7,103},{8,104... | collective-permute-start | bytes 147464 | tf_op jit(solution)/shard_map/ppermute | solution.py:536
  54.1 6.6 %collective-permute-start.11 = (bf16[192,128]{1,0:T(8,128)(2,1)S(1)}, bf16[192,128]{1,0:T(8,128)(2,1)S(1)}, u32[]{:S(2)}, u32[]{:S(2)}) collective-permute-start(bf16[192,128]{1,0:T(8,128)(2,1)S(1)} %add_convert_fusion.1), channel_id=1, source_target_pairs={{0,32},{1,33},{2,34},{3,35},{4,36},{5,37},{6,38},{7,39},{8,40},{9,... | collective-permute-start | bytes 147464 | tf_op jit(solution)/shard_map/ppermute | solution.py:536
  55.4 5.4 %collective-permute-start.10 = (bf16[192,128]{1,0:T(8,128)(2,1)S(1)}, bf16[192,128]{1,0:T(8,128)(2,1)S(1)}, u32[]{:S(2)}, u32[]{:S(2)}) collective-permute-start(bf16[192,128]{1,0:T(8,128)(2,1)S(1)} %add_convert_fusion.1), channel_id=1, source_target_pairs={{0,64},{1,65},{2,66},{3,67},{4,68},{5,69},{6,70},{7,71},{8,72},{9,... | collective-permute-start | bytes 147464 | tf_op jit(solution)/shard_map/ppermute | solution.py:536
  60.8 4.9 %collective-permute-start.13 = (bf16[192,128]{1,0:T(8,128)(2,1)S(1)}, bf16[192,128]{1,0:T(8,128)(2,1)S(1)}, u32[]{:S(2)}, u32[]{:S(2)}) collective-permute-start(bf16[192,128]{1,0:T(8,128)(2,1)S(1)} %add_convert_fusion), channel_id=1, source_target_pairs={{0,1},{1,0},{2,3},{3,2},{4,5},{5,4},{6,7},{7,6},{8,9},{9,8},{10,11... | collective-permute-start | bytes 147464 | tf_op jit(solution)/shard_map/ppermute | solution.py:530

commit v5 on v4

--- a/solution.py
+++ b/solution.py
@@ -530,12 +530,6 @@
     return lax.ppermute(value, "pts", [(i, i ^ flip) for i in range(count)])
 
 
-def turned(value, place, by):
-    count = lax.axis_size("pts")
-    targets = [(i & ~(3 << place)) | (((i >> place) + by & 3) << place) for i in range(count)]
-    return lax.ppermute(value, "pts", list(enumerate(targets)))
-
-
 def added(*values):
     total = values[0].astype(F32)
     for value in values[1:]:
@@ -565,8 +559,8 @@
     place = 1
     while 2 << place <= count:
         part, result = beside(part)
-        one, three, two = [turned(part, place, k) for k in (1, 3, 2)]
-        total = (part.astype(F32) + two.astype(F32)) + (one.astype(F32) + three.astype(F32))
+        one, three, two = [flipped(part, k << place) for k in (1, 3, 2)]
+        total = (part.astype(F32) + one.astype(F32)) + (two.astype(F32) + three.astype(F32))
         part = total.astype(BF16)
         part, result = lax.optimization_barrier((part, result))
         place += 2

time: 66.6 us -> 65.7 us (0.986)
  starting transfers between devices: 26.6 us -> 24.8 us
  waiting for transfers between devices: 9.43 us -> 10.4 us
    ppermute x9 -> x0, starting transfers between devices: 17.3 us -> none  [turned(): return lax.ppermute(value, 'pts', list(enumerate(targets)))]
    ppermute x4 -> x13, starting transfers between devices: 5.84 us -> 21.3 us  [flipped(): return lax.ppermute(value, 'pts', [(i, i ^ flip) for i in range(count)])]
    ppermute x4 -> x13, waiting for transfers between devices: 3.94 us -> 8.46 us  [flipped(): return lax.ppermute(value, 'pts', [(i, i ^ flip) for i in range(count)])]
    ppermute x9 -> x0, waiting for transfers between devices: 3.53 us -> none  [turned(): return lax.ppermute(value, 'pts', list(enumerate(targets)))]
where the time goes in v5:
time: 65.7 us; the launch traced here: 65.6 us
  Pallas kernels  28.5 us (43%)
  starting transfers between devices  24.8 us (38%)
  waiting for transfers between devices  10.4 us (16%)
  other arithmetic  1.03 us (2%)
  between operations  0.82 us (1%)
    ppermute x13, starting transfers between devices, flipped(): return lax.ppermute(value, 'pts', [(i, i ^ flip) for i in range(count)])  21.3 us
    pallas_call x1, Pallas kernels, outgoing(): pl.pallas_call(kernel, in_specs=[hbm] * len(inputs), out_specs=[vmem] * 8...  11.5 us
    pallas_call x1, Pallas kernels, incoming(): pl.pallas_call(kernel, in_specs=[vmem] * len(inputs), out_specs=[vmem, vm...  11.1 us
    ppermute x13, waiting for transfers between devices, flipped(): return lax.ppermute(value, 'pts', [(i, i ^ flip) for i in range(count)])  8.46 us
    pallas_call x3, Pallas kernels, feats_grad(): pl.pallas_call(functools.partial(feats_grad_kernel, first * block_len, bl...  5.91 us
    ppermute x1, starting transfers between devices, near_sums(): lax.ppermute(kept, 'pts', steps + [(j, i) for i, j in steps])  3.44 us
    ppermute x1, waiting for transfers between devices, near_sums(): lax.ppermute(kept, 'pts', steps + [(j, i) for i, j in steps])  1.96 us
  transfers between devices with their start and end apart: 14, of which 8 were waited for; matrix products, arithmetic and copies ran while one was open for 0% of the time, Pallas kernels for 9%

profile of v5, /device:TPU:1, one launch (start us, length us, event | category | flops | bytes accessed | tf_op | source)
XLA Modules:
  0.0 65.6 jit_solution(7360286699043659418)
XLA Ops:
  0.7 11.5 %outgoing.1 = (bf16[28672,128]{1,0:T(8,128)(2,1)S(1)}, bf16[28672,128]{1,0:T(8,128)(2,1)S(1)}, bf16[1792,256]{1,0:T(8,128)(2,1)S(1)}, bf16[1792,128]{1,0:T(8,128...) custom-call(s32[112]{0:T(128)} %refs_0_.2, ...), custom_call_target="tpu_custom_call" | custom-call | tf_op jit(solution)/shard_map/outgoing/pallas_call | solution.py:281
  12.2 1.5 %collective-permute-start = (bf16[48,256]{1,0:T(8,128)(2,1)S(1)}, bf16[48,256]{1,0:T(8,128)(2,1)S(1)}, u32[]{:S(2)}, u32[]{:S(2)}) collective-permute-start(bf16[48,256]{1,0:T(8,128)(2,1)S(1)} %slice_select_fusion.2), channel_id=1, source_target_pairs={{0,1},{1,0},{2,3},{3,2},{4,5},{5,4},{6,7},{7,6},{8,9},{9,8},{10,11... | collective-permute-start | bytes 73736 | tf_op jit(solution)/shard_map/ppermute | solution.py:530
  13.7 0.8 %collective-permute-done = bf16[48,256]{1,0:T(8,128)(2,1)S(1)} collective-permute-done((bf16[48,256]{1,0:T(8,128)(2,1)S(1)}, bf16[48,256]{1,0:T(8,128)(2,1)S(1)}, u32[]{:S(2)}, u32[]{:S(2)}) %collective-permute-start) | collective-permute-done | bytes 24608 | tf_op jit(solution)/shard_map/ppermute | solution.py:530
  14.5 0.1 fusion
  14.6 3.4 %collective-permute-start.1 = (bf16[2,48,256]{2,1,0:T(8,128)(2,1)S(1)}, bf16[2,48,256]{2,1,0:T(8,128)(2,1)S(1)}, u32[]{:S(2)}, u32[]{:S(2)}) collective-permute-start(bf16[2,48,256]{2,1,0:T(8,128)(2,1)S(1)} %fusion), channel_id=1, source_target_pairs={{1,2},{3,4},{5,6},{7,8},{9,10},{11,12},{13,14},{15,16},{17,18},{19... | collective-permute-start | bytes 147464 | tf_op jit(solution)/shard_map/ppermute | solution.py:549
  18.1 2.0 %collective-permute-done.1 = bf16[2,48,256]{2,1,0:T(8,128)(2,1)S(1)} collective-permute-done((bf16[2,48,256]{2,1,0:T(8,128)(2,1)S(1)}, bf16[2,48,256]{2,1,0:T(8,128)(2,1)S(1)}, u32[]{:S(2)}, u32[]{:S(2)}) %collective-permute-start.1) | collective-permute-done | bytes 49184 | tf_op jit(solution)/shard_map/ppermute | solution.py:549
  20.0 0.1 add_convert_fusion.4
  20.1 0.1 collective-permute-start.2
  20.2 1.2 %collective-permute-done.2.refs_3_ = bf16[48,256]{1,0:T(8,128)(2,1)S(1)} collective-permute-done((bf16[48,256]{1,0:T(8,128)(2,1)S(1)}, bf16[48,256]{1,0:T(8,128)(2,1)S(1)}, u32[]{:S(2)}, u32[]{:S(2)}) %collective-permute-start.2) | collective-permute-done | bytes 24608 | tf_op jit(solution)/shard_map/ppermute | solution.py:530
  21.4 11.1 %incoming.1 = (bf16[14336,256]{1,0:T(8,128)(2,1)S(1)}, bf16[384,128]{1,0:T(8,128)(2,1)S(1)}) custom-call(bf16[128,128]{1,0:T(8,128)(2,1)S(1)} %copy-done.1, bf16[128,128]{1,0:T(8,128)(2,1)S(1)} %copy-done.2, bf16[96,256]{1,0:T(8,128)(2,1)S(1)} %bitcast.8, bf16[48,256]{1,0:T(8,128)(2,1)S(1)} %collective-permute-done.2.refs_3_, ...), custom_call_target="tpu_custom_call", output_to_operand_aliasing={{0}: (9, {})} | custom-call | tf_op jit(solution)/shard_map/incoming/pallas_call | solution.py:453
  32.5 0.3 collective-permute-start.3
  32.8 1.1 %collective-permute-done.3 = bf16[192,128]{1,0:T(8,128)(2,1)S(1)} collective-permute-done((bf16[192,128]{1,0:T(8,128)(2,1)S(1)}, bf16[192,128]{1,0:T(8,128)(2,1)S(1)}, u32[]{:S(2)}, u32[]{:S(2)}) %collective-permute-start.3) | collective-permute-done | bytes 49184 | tf_op jit(solution)/shard_map/ppermute | solution.py:530
  33.9 4.8 %collective-permute-start.6 = (bf16[192,128]{1,0:T(8,128)(2,1)S(1)}, bf16[192,128]{1,0:T(8,128)(2,1)S(1)}, u32[]{:S(2)}, u32[]{:S(2)}) collective-permute-start(bf16[192,128]{1,0:T(8,128)(2,1)S(1)} %add_convert_fusion.3), channel_id=1, source_target_pairs={{0,6},{1,7},{2,4},{3,5},{4,2},{5,3},{6,0},{7,1},{8,14},{9,15},{10,... | collective-permute-start | bytes 147464 | tf_op jit(solution)/shard_map/ppermute | solution.py:530
  38.6 0.0 collective-permute-start.5
  38.6 0.7 %collective-permute-start.4 = (bf16[192,128]{1,0:T(8,128)(2,1)S(1)}, bf16[192,128]{1,0:T(8,128)(2,1)S(1)}, u32[]{:S(2)}, u32[]{:S(2)}) collective-permute-start(bf16[192,128]{1,0:T(8,128)(2,1)S(1)} %add_convert_fusion.3), channel_id=1, source_target_pairs={{0,2},{1,3},{2,0},{3,1},{4,6},{5,7},{6,4},{7,5},{8,10},{9,11},{10,... | collective-permute-start | bytes 147464 | tf_op jit(solution)/shard_map/ppermute | solution.py:530
  39.3 2.1 %feats_grad.3.refs_0_ = bf16[28672,128]{1,0:T(8,128)(2,1)} custom-call(bf16[14336,256]{1,0:T(8,128)(2,1)S(1)} %get-tuple-element.41.dpre1_ref, bf16[128,128]{1,0:T(8,128)(2,1)S(1)} %copy-done), custom_call_target="tpu_custom_call" | custom-call | flops 335544320 | bytes 5242880 | tf_op jit(solution)/shard_map/feats_grad/pallas_call | solution.py:509
  41.4 1.7 %collective-permute-done.5 = bf16[192,128]{1,0:T(8,128)(2,1)S(1)} collective-permute-done((bf16[192,128]{1,0:T(8,128)(2,1)S(1)}, bf16[192,128]{1,0:T(8,128)(2,1)S(1)}, u32[]{:S(2)}, u32[]{:S(2)}) %collective-permute-start.5) | collective-permute-done | bytes 49184 | tf_op jit(solution)/shard_map/ppermute | solution.py:530
  43.1 0.0 collective-permute-done.4
  43.1 4.9 %collective-permute-start.9 = (bf16[192,128]{1,0:T(8,128)(2,1)S(1)}, bf16[192,128]{1,0:T(8,128)(2,1)S(1)}, u32[]{:S(2)}, u32[]{:S(2)}) collective-permute-start(bf16[192,128]{1,0:T(8,128)(2,1)S(1)} %add_convert_fusion.2), channel_id=1, source_target_pairs={{0,24},{1,25},{2,26},{3,27},{4,28},{5,29},{6,30},{7,31},{8,16},{9,... | collective-permute-start | bytes 147464 | tf_op jit(solution)/shard_map/ppermute | solution.py:530
  48.0 0.0 collective-permute-start.8
  48.0 0.7 %collective-permute-start.7 = (bf16[192,128]{1,0:T(8,128)(2,1)S(1)}, bf16[192,128]{1,0:T(8,128)(2,1)S(1)}, u32[]{:S(2)}, u32[]{:S(2)}) collective-permute-start(bf16[192,128]{1,0:T(8,128)(2,1)S(1)} %add_convert_fusion.2), channel_id=1, source_target_pairs={{0,8},{1,9},{2,10},{3,11},{4,12},{5,13},{6,14},{7,15},{8,0},{9,1},... | collective-permute-start | bytes 147464 | tf_op jit(solution)/shard_map/ppermute | solution.py:530
  48.7 1.9 %feats_grad.4.refs_0_ = bf16[28672,128]{1,0:T(8,128)(2,1)} custom-call(bf16[14336,256]{1,0:T(8,128)(2,1)S(1)} %get-tuple-element.41.dpre1_ref, bf16[128,128]{1,0:T(8,128)(2,1)S(1)} %copy-done, bf16[28672,128]{1,0:T(8,128)(2,1)} %feats_grad.3.refs_0_), custom_call_target="tpu_custom_call", output_to_operand_aliasing={{}: (2, {})} | custom-call | flops 301989888 | bytes 4718592 | tf_op jit(solution)/shard_map/feats_grad/pallas_call | solution.py:509
  50.6 0.0 collective-permute-done.9
  50.6 1.8 %collective-permute-done.8 = bf16[192,128]{1,0:T(8,128)(2,1)S(1)} collective-permute-done((bf16[192,128]{1,0:T(8,128)(2,1)S(1)}, bf16[192,128]{1,0:T(8,128)(2,1)S(1)}, u32[]{:S(2)}, u32[]{:S(2)}) %collective-permute-start.8) | collective-permute-done | bytes 49184 | tf_op jit(solution)/shard_map/ppermute | solution.py:530
  52.5 0.0 collective-permute-done.7
  52.5 0.6 collective-permute-start.12
  53.1 3.2 %collective-permute-start.11 = (bf16[192,128]{1,0:T(8,128)(2,1)S(1)}, bf16[192,128]{1,0:T(8,128)(2,1)S(1)}, u32[]{:S(2)}, u32[]{:S(2)}) collective-permute-start(bf16[192,128]{1,0:T(8,128)(2,1)S(1)} %add_convert_fusion.1), channel_id=1, source_target_pairs={{0,64},{1,65},{2,66},{3,67},{4,68},{5,69},{6,70},{7,71},{8,72},{9,... | collective-permute-start | bytes 147464 | tf_op jit(solution)/shard_map/ppermute | solution.py:530
  56.3 1.9 %feats_grad.5 = bf16[28672,128]{1,0:T(8,128)(2,1)} custom-call(bf16[14336,256]{1,0:T(8,128)(2,1)S(1)} %get-tuple-element.41.dpre1_ref, bf16[128,128]{1,0:T(8,128)(2,1)S(1)} %copy-done, bf16[28672,128]{1,0:T(8,128)(2,1)} %feats_grad.4.refs_0_), custom_call_target="tpu_custom_call", output_to_operand_aliasing={{}: (2, {})} | custom-call | flops 301989888 | bytes 4718592 | tf_op jit(solution)/shard_map/feats_grad/pallas_call | solution.py:509
  58.2 1.0 %collective-permute-done.10 = bf16[192,128]{1,0:T(8,128)(2,1)S(1)} collective-permute-done((bf16[192,128]{1,0:T(8,128)(2,1)S(1)}, bf16[192,128]{1,0:T(8,128)(2,1)S(1)}, u32[]{:S(2)}, u32[]{:S(2)}) %collective-permute-start.10) | collective-permute-done | bytes 49184 | tf_op jit(solution)/shard_map/ppermute | solution.py:530
  59.3 4.7 %collective-permute-start.13 = (bf16[192,128]{1,0:T(8,128)(2,1)S(1)}, bf16[192,128]{1,0:T(8,128)(2,1)S(1)}, u32[]{:S(2)}, u32[]{:S(2)}) collective-permute-start(bf16[192,128]{1,0:T(8,128)(2,1)S(1)} %add_convert_fusion), channel_id=1, source_target_pairs={{0,1},{1,0},{2,3},{3,2},{4,5},{5,4},{6,7},{7,6},{8,9},{9,8},{10,11... | collective-permute-start | bytes 147464 | tf_op jit(solution)/shard_map/ppermute | solution.py:530
  64.0 0.9 %collective-permute-done.13 = bf16[192,128]{1,0:T(8,128)(2,1)S(1)} collective-permute-done((bf16[192,128]{1,0:T(8,128)(2,1)S(1)}, bf16[192,128]{1,0:T(8,128)(2,1)S(1)}, u32[]{:S(2)}, u32[]{:S(2)}) %collective-permute-start.13) | collective-permute-done | bytes 49184 | tf_op jit(solution)/shard_map/ppermute | solution.py:530
  64.9 0.7 %slice_multiply_fusion = (f32[128,128]{1,0:T(8,128)}, f32[128,128]{1,0:T(8,128)}, f32[128,128]{1,0:T(8,128)}) fusion(f32[384,128]{1,0:T(8,128)S(1)} %maximum_convert_fusion), kind=kLoop, calls=%fused_computation.8 | loop fusion | flops 49152 | bytes 393216 | tf_op jit(solution)/shard_map/mul | solution.py:625
  (21 shorter events, 0.2 us)
Async XLA Ops:
  0.6 20.8 %copy-start.1 = (bf16[128,128]{1,0:T(8,128)(2,1)S(1)}, bf16[128,128]{1,0:T(8,128)(2,1)}, u32[]{:S(2)}) copy-start(bf16[128,128]{1,0:T(8,128)(2,1)} %refs_0_.3) | copy-start | bytes 98308
  0.6 20.8 %copy-start.2 = (bf16[128,128]{1,0:T(8,128)(2,1)S(1)}, bf16[128,128]{1,0:T(8,128)(2,1)}, u32[]{:S(2)}) copy-start(bf16[128,128]{1,0:T(8,128)(2,1)} %refs_1_.3) | copy-start | bytes 98308
  12.2 2.3 %collective-permute-start = (bf16[48,256]{1,0:T(8,128)(2,1)S(1)}, bf16[48,256]{1,0:T(8,128)(2,1)S(1)}, u32[]{:S(2)}, u32[]{:S(2)}) collective-permute-start(bf16[48,256]{1,0:T(8,128)(2,1)S(1)} %slice_select_fusion.2), channel_id=1, source_target_pairs={{0,1},{1,0},{2,3},{3,2},{4,5},{5,4},{6,7},{7,6},{8,9},{9,8},{10,11... | collective-permute-start | bytes 73736 | tf_op jit(solution)/shard_map/ppermute | solution.py:530
  14.6 5.4 %collective-permute-start.1 = (bf16[2,48,256]{2,1,0:T(8,128)(2,1)S(1)}, bf16[2,48,256]{2,1,0:T(8,128)(2,1)S(1)}, u32[]{:S(2)}, u32[]{:S(2)}) collective-permute-start(bf16[2,48,256]{2,1,0:T(8,128)(2,1)S(1)} %fusion), channel_id=1, source_target_pairs={{1,2},{3,4},{5,6},{7,8},{9,10},{11,12},{13,14},{15,16},{17,18},{19... | collective-permute-start | bytes 147464 | tf_op jit(solution)/shard_map/ppermute | solution.py:549
  20.1 1.3 %collective-permute-start.2 = (bf16[48,256]{1,0:T(8,128)(2,1)S(1)}, bf16[48,256]{1,0:T(8,128)(2,1)S(1)}, u32[]{:S(2)}, u32[]{:S(2)}) collective-permute-start(bf16[48,256]{1,0:T(8,128)(2,1)S(1)} %fusion.1), channel_id=1, source_target_pairs={{0,1},{1,0},{2,3},{3,2},{4,5},{5,4},{6,7},{7,6},{8,9},{9,8},{10,11... | collective-permute-start | bytes 73736 | tf_op jit(solution)/shard_map/ppermute | solution.py:530
  21.4 17.9 %copy-start = (bf16[128,128]{1,0:T(8,128)(2,1)S(1)}, bf16[128,128]{1,0:T(8,128)(2,1)}, u32[]{:S(2)}) copy-start(bf16[128,128]{1,0:T(8,128)(2,1)} %w_first_ref.5) | copy-start | bytes 98308
  32.5 1.3 %collective-permute-start.3 = (bf16[192,128]{1,0:T(8,128)(2,1)S(1)}, bf16[192,128]{1,0:T(8,128)(2,1)S(1)}, u32[]{:S(2)}, u32[]{:S(2)}) collective-permute-start(bf16[192,128]{1,0:T(8,128)(2,1)S(1)} %broadcast_select_fusion.2), channel_id=1, source_target_pairs={{0,1},{1,0},{2,3},{3,2},{4,5},{5,4},{6,7},{7,6},{8,9},{9,8},{10,11... | collective-permute-start | bytes 147464 | tf_op jit(solution)/shard_map/ppermute | solution.py:530
  33.9 7.5 %collective-permute-start.6 = (bf16[192,128]{1,0:T(8,128)(2,1)S(1)}, bf16[192,128]{1,0:T(8,128)(2,1)S(1)}, u32[]{:S(2)}, u32[]{:S(2)}) collective-permute-start(bf16[192,128]{1,0:T(8,128)(2,1)S(1)} %add_convert_fusion.3), channel_id=1, source_target_pairs={{0,6},{1,7},{2,4},{3,5},{4,2},{5,3},{6,0},{7,1},{8,14},{9,15},{10,... | collective-permute-start | bytes 147464 | tf_op jit(solution)/shard_map/ppermute | solution.py:530
  38.6 4.4 %collective-permute-start.5 = (bf16[192,128]{1,0:T(8,128)(2,1)S(1)}, bf16[192,128]{1,0:T(8,128)(2,1)S(1)}, u32[]{:S(2)}, u32[]{:S(2)}) collective-permute-start(bf16[192,128]{1,0:T(8,128)(2,1)S(1)} %add_convert_fusion.3), channel_id=1, source_target_pairs={{0,4},{1,5},{2,6},{3,7},{4,0},{5,1},{6,2},{7,3},{8,12},{9,13},{10,... | collective-permute-start | bytes 147464 | tf_op jit(solution)/shard_map/ppermute | solution.py:530
  38.6 4.4 %collective-permute-start.4 = (bf16[192,128]{1,0:T(8,128)(2,1)S(1)}, bf16[192,128]{1,0:T(8,128)(2,1)S(1)}, u32[]{:S(2)}, u32[]{:S(2)}) collective-permute-start(bf16[192,128]{1,0:T(8,128)(2,1)S(1)} %add_convert_fusion.3), channel_id=1, source_target_pairs={{0,2},{1,3},{2,0},{3,1},{4,6},{5,7},{6,4},{7,5},{8,10},{9,11},{10,... | collective-permute-start | bytes 147464 | tf_op jit(solution)/shard_map/ppermute | solution.py:530
  43.1 7.5 %collective-permute-start.9 = (bf16[192,128]{1,0:T(8,128)(2,1)S(1)}, bf16[192,128]{1,0:T(8,128)(2,1)S(1)}, u32[]{:S(2)}, u32[]{:S(2)}) collective-permute-start(bf16[192,128]{1,0:T(8,128)(2,1)S(1)} %add_convert_fusion.2), channel_id=1, source_target_pairs={{0,24},{1,25},{2,26},{3,27},{4,28},{5,29},{6,30},{7,31},{8,16},{9,... | collective-permute-start | bytes 147464 | tf_op jit(solution)/shard_map/ppermute | solution.py:530
  48.0 4.4 %collective-permute-start.8 = (bf16[192,128]{1,0:T(8,128)(2,1)S(1)}, bf16[192,128]{1,0:T(8,128)(2,1)S(1)}, u32[]{:S(2)}, u32[]{:S(2)}) collective-permute-start(bf16[192,128]{1,0:T(8,128)(2,1)S(1)} %add_convert_fusion.2), channel_id=1, source_target_pairs={{0,16},{1,17},{2,18},{3,19},{4,20},{5,21},{6,22},{7,23},{8,24},{9,... | collective-permute-start | bytes 147464 | tf_op jit(solution)/shard_map/ppermute | solution.py:530
  48.0 4.4 %collective-permute-start.7 = (bf16[192,128]{1,0:T(8,128)(2,1)S(1)}, bf16[192,128]{1,0:T(8,128)(2,1)S(1)}, u32[]{:S(2)}, u32[]{:S(2)}) collective-permute-start(bf16[192,128]{1,0:T(8,128)(2,1)S(1)} %add_convert_fusion.2), channel_id=1, source_target_pairs={{0,8},{1,9},{2,10},{3,11},{4,12},{5,13},{6,14},{7,15},{8,0},{9,1},... | collective-permute-start | bytes 147464 | tf_op jit(solution)/shard_map/ppermute | solution.py:530
  52.5 5.7 %collective-permute-start.12 = (bf16[192,128]{1,0:T(8,128)(2,1)S(1)}, bf16[192,128]{1,0:T(8,128)(2,1)S(1)}, u32[]{:S(2)}, u32[]{:S(2)}) collective-permute-start(bf16[192,128]{1,0:T(8,128)(2,1)S(1)} %add_convert_fusion.1), channel_id=1, source_target_pairs={{0,96},{1,97},{2,98},{3,99},{4,100},{5,101},{6,102},{7,103},{8,104... | collective-permute-start | bytes 147464 | tf_op jit(solution)/shard_map/ppermute | solution.py:530
  53.1 5.1 %collective-permute-start.11 = (bf16[192,128]{1,0:T(8,128)(2,1)S(1)}, bf16[192,128]{1,0:T(8,128)(2,1)S(1)}, u32[]{:S(2)}, u32[]{:S(2)}) collective-permute-start(bf16[192,128]{1,0:T(8,128)(2,1)S(1)} %add_convert_fusion.1), channel_id=1, source_target_pairs={{0,64},{1,65},{2,66},{3,67},{4,68},{5,69},{6,70},{7,71},{8,72},{9,... | collective-permute-start | bytes 147464 | tf_op jit(solution)/shard_map/ppermute | solution.py:530
  56.3 2.9 %collective-permute-start.10 = (bf16[192,128]{1,0:T(8,128)(2,1)S(1)}, bf16[192,128]{1,0:T(8,128)(2,1)S(1)}, u32[]{:S(2)}, u32[]{:S(2)}) collective-permute-start(bf16[192,128]{1,0:T(8,128)(2,1)S(1)} %add_convert_fusion.1), channel_id=1, source_target_pairs={{0,32},{1,33},{2,34},{3,35},{4,36},{5,37},{6,38},{7,39},{8,40},{9,... | collective-permute-start | bytes 147464 | tf_op jit(solution)/shard_map/ppermute | solution.py:530
  59.3 5.6 %collective-permute-start.13 = (bf16[192,128]{1,0:T(8,128)(2,1)S(1)}, bf16[192,128]{1,0:T(8,128)(2,1)S(1)}, u32[]{:S(2)}, u32[]{:S(2)}) collective-permute-start(bf16[192,128]{1,0:T(8,128)(2,1)S(1)} %add_convert_fusion), channel_id=1, source_target_pairs={{0,1},{1,0},{2,3},{3,2},{4,5},{5,4},{6,7},{7,6},{8,9},{9,8},{10,11... | collective-permute-start | bytes 147464 | tf_op jit(solution)/shard_map/ppermute | solution.py:530
